TPU v7x, 256 devices: a whole 4x4x8 slice. The times are simulated.
256 devices in a mesh: tile: 64 (over x, z_lo, y), exp: 4 (over z_hi, core).
Axes of the slice: x: 4, y: 4, z: 8 (z_hi: 2, z_lo: 4; z = z_hi * 4 + z_lo), core: 2. Of those that a mesh axis runs over, the one named last changes fastest.
Arguments:
- template: bfloat16 [64, 256, 256], P('tile', 'exp'), may hold values from -8 to 8
- exposures: bfloat16 [64, 16, 256, 256], P('tile', 'exp'), may hold values from -20 to 20
- masks: int32 [64, 16, 256, 256], P('tile', 'exp'), may hold values 0 or 1
- basis_rows: float32 [27, 21], replicated, may hold values from -1.2 to 2.7
- basis_cols: float32 [27, 21], replicated, may hold values from -1.2 to 2.7
- psf_row: float32 [21], replicated, may hold values from 0 to 0.5
- psf_col: float32 [21], replicated, may hold values from 0 to 0.5
Outputs:
- coadd: float32 [64, 256, 256], P('tile', 'exp')
All inputs are finite; a program needn't handle non-finite values. No bound on the sum of `masks` on one device may be relied on, other than what follows from the above.
Results may differ from a plain program's by a relative error of at most 0.0077.
Values may be sent and summed in bfloat16 or wider, within the bound.
No kernel may reach another device: no remote copies, remote signals or barrier semaphores. Data moves between devices by JAX's collectives and lax.ppermute only.
A program may use at most 128 MiB of HBM per device.

v0:
```python
import jax
import jax.numpy as jnp
from jax import lax
from jax.sharding import PartitionSpec as P

HW = 10
KW = 21
NB = 27
GW = 8


def passed_along(block, axis, distance):
    devices = range(lax.axis_size(axis))
    route = [(i - distance, i) for i in devices if i - distance in devices]
    return lax.ppermute(block, axis, route)


def band_table(size_out, dtype):
    offsets = jnp.arange(size_out + 2 * HW)[:, None] - jnp.arange(size_out)[None, :]
    return (offsets[None, :, :] == jnp.arange(KW)[:, None, None]).astype(dtype)


def banded_low(kernel_taps, size_out):
    return jnp.einsum(
        "bk,kpq->bpq",
        kernel_taps.astype(jnp.bfloat16),
        band_table(size_out, jnp.bfloat16),
        preferred_element_type=jnp.float32,
    ).astype(jnp.bfloat16)


def banded_high(kernel_taps, size_out):
    return jnp.einsum(
        "k,kpq->pq", kernel_taps, band_table(size_out, jnp.float32), precision=lax.Precision.HIGHEST
    )


def edge_flags():
    grid_col = lax.axis_index("tile") % GW
    return (grid_col > 0, grid_col < GW - 1)


def rim_halo(values):
    has_west, has_east = edge_flags()
    from_west = passed_along(values[..., -HW:], "tile", 1)
    from_east = passed_along(values[..., :HW], "tile", -1)
    from_west = jnp.where(has_west, from_west, jnp.zeros_like(from_west))
    from_east = jnp.where(has_east, from_east, jnp.zeros_like(from_east))
    widened = jnp.concatenate([from_west, values, from_east], -1)
    from_north = passed_along(widened[..., -HW:, :], "tile", GW)
    from_south = passed_along(widened[..., :HW, :], "tile", -GW)
    return jnp.concatenate([from_north, widened, from_south], -2)


def convolve_rows(padded_rows, col_band, basis_rows, count_rows):
    column_pass = jnp.einsum(
        "iq,bqj->bij", padded_rows, col_band, preferred_element_type=jnp.float32
    ).astype(jnp.bfloat16)
    row_band = banded_low(basis_rows, count_rows)
    return jnp.einsum(
        "bpi,bpj->bij", row_band, column_pass, preferred_element_type=jnp.float32
    ).astype(jnp.bfloat16)


def shards(template, exposures, masks, basis_rows, basis_cols, psf_row, psf_col):
    tile_width = template.shape[2]
    full_tile = lax.all_gather(template, "exp", axis=1, tiled=True)
    padded = rim_halo(full_tile)[0]
    col_band = banded_low(basis_cols, tile_width)
    basis_img = convolve_rows(padded, col_band, basis_rows, tile_width)
    flat = basis_img.reshape(NB, tile_width * tile_width)
    results = []
    for slot_index in range(exposures.shape[1]):
        exposure = exposures[0, slot_index].reshape(-1)
        mask_flat = masks[0, slot_index].reshape(-1)
        masked = flat * mask_flat.astype(jnp.bfloat16)[None, :]
        normal = lax.dot_general(
            masked, flat, (((1,), (1,)), ((), ())), preferred_element_type=jnp.float32
        )
        right_side = jnp.dot(masked, exposure, preferred_element_type=jnp.float32)
        factor = jnp.linalg.cholesky(normal)
        coefficients = jax.scipy.linalg.cho_solve((factor, True), right_side).astype(jnp.bfloat16)
        model = jnp.dot(coefficients, flat, preferred_element_type=jnp.float32)
        difference = mask_flat.astype(jnp.float32) * (exposure.astype(jnp.float32) - model)
        results.append(difference.astype(jnp.bfloat16).reshape(tile_width, tile_width))
    stacked = jnp.stack(results, 0)
    coverage = jnp.sum(masks[0].astype(jnp.float32), axis=0)
    psf_cols_band = banded_high(psf_col, tile_width)
    beside_all = rim_halo(stacked)
    plane = jnp.sum(beside_all, axis=0, dtype=jnp.float32)
    column_pass = jnp.dot(plane, psf_cols_band, precision=lax.Precision.HIGHEST)
    psf_rows_band = banded_high(psf_row, tile_width)
    filtered = jnp.einsum("qi,qj->ij", psf_rows_band, column_pass, precision=lax.Precision.HIGHEST)
    summed, coverage_rows = (
        lax.psum_scatter(filtered, "exp", scatter_dimension=0, tiled=True),
        lax.psum_scatter(coverage, "exp", scatter_dimension=0, tiled=True),
    )
    return (summed / jnp.maximum(coverage_rows, 1.0))[None]


def solution(mesh):
    placed = (
        P("tile", "exp", None),
        P("tile", "exp", None, None),
        P("tile", "exp", None, None),
        P(),
        P(),
        P(),
        P(),
    )
    return jax.shard_map(
        shards, mesh=mesh, in_specs=placed, out_specs=P("tile", "exp", None), check_vma=False
    )
```

profile of v0, /device:TPU:1, one launch (start us, length us, event | category | flops | bytes accessed | tf_op | source)
XLA Modules:
  0.0 254.0 jit_solution(16707825145330876191)
XLA Ops:
  6.5 12.7 %all_gather.3 = bf16[1,256,256]{2,1,0:T(8,128)(2,1)S(1)} all-gather(bf16[1,64,256]{2,1,0:T(8,128)(2,1)} %param.10), channel_id=1, replica_groups=mesh['tile'=64,'exp'=4] {'exp'}, dimensions={1}, use_global_device_ids=true | all-gather | bytes 163840 | tf_op jit(solution)/shard_map/all_gather | solution.py:67
  20.7 4.0 %collective-permute-start = (bf16[1,256,10]{2,1,0:T(8,128)(2,1)S(1)}, bf16[1,256,10]{2,1,0:T(8,128)(2,1)S(1)}, u32[]{:S(2)}, u32[]{:S(2)}) collective-permute-start(bf16[1,256,10]{2,1,0:T(8,128)(2,1)S(1)} %get-tuple-element.33), channel_id=1, source_target_pairs={{0,4},{4,8},{8,12},{12,16},{16,20},{20,24},{24,28},{28,32},{32,36}... | collective-permute-start | bytes 15368 | tf_op jit(solution)/shard_map/ppermute | solution.py:15
  26.8 4.4 %convert_bitcast_fusion = bf16[27,276,256]{2,0,1:T(8,128)(2,1)} fusion(s32[276,256]{1,0:T(8,128)S(1)} %iota_subtract_fusion, f32[27,21]{0,1:T(8,128)} %param.14), kind=kOutput, calls=%fused_computation.5 | convolution fusion | flops 83515960 | bytes 4100316 | tf_op jit(solution)/shard_map/bk,kpq->bpq/dot_general | solution.py:24
  31.2 3.6 %convert_bitcast_fusion.1 = bf16[27,276,256]{2,0,1:T(8,128)(2,1)} fusion(s32[276,256]{1,0:T(8,128)S(1)} %iota_subtract_fusion, f32[27,21]{0,1:T(8,128)S(1)} %copy-done.32), kind=kOutput, calls=%fused_computation.6 | convolution fusion | flops 83515960 | bytes 4100316 | tf_op jit(solution)/shard_map/bk,kpq->bpq/dot_general | solution.py:24
  35.1 4.5 %collective-permute-start.2 = (bf16[1,10,276]{2,1,0:T(8,128)(2,1)S(1)}, bf16[1,10,276]{2,1,0:T(8,128)(2,1)S(1)}, u32[]{:S(2)}, u32[]{:S(2)}) collective-permute-start(bf16[1,10,276]{2,1,0:T(8,128)(2,1)S(1)} %get-tuple-element.31), channel_id=1, source_target_pairs={{0,32},{4,36},{8,40},{12,44},{16,48},{20,52},{24,56},{28,60},{32,6... | collective-permute-start | bytes 16568 | tf_op jit(solution)/shard_map/ppermute | solution.py:15
  52.8 18.9 %broadcast_multiply_fusion = (bf16[27,256,256]{2,1,0:T(8,128)(2,1)}, bf16[27,256,256]{2,1,0:T(8,128)(2,1)}, bf16[27,256,256]{2,1,0:T(8,128)(2,1)}, bf16[27,256,256]{2,1,0:T(8,128)(2,1)S(1)}, bf16[27,256,256]{2,1,0:T(8,128)(2,1)}) fusion(bf16[256,256]{1,0:T(8,128)(2,1)} %get-tuple-element.13, bf16[256,256]{1,0:T(8,128)(2,1)} %get-tuple-element.16, ...), kind=kOutput, calls=%fused_computation.29 | convolution fusion | flops 2057247616 | bytes 26002208 | tf_op jit(solution)/shard_map/bpi,bpj->bij/dot_general | solution.py:60
  71.7 8.0 %fusion.51 = f32[27,27]{1,0:T(8,128)} fusion(bf16[27,256,256]{2,1,0:T(8,128)(2,1)} %get-tuple-element.35, bf16[27,256,256]{2,1,0:T(8,128)(2,1)} %get-tuple-element.6), kind=kOutput, calls=%fused_computation.37 | convolution fusion | flops 95551488 | bytes 7080804 | tf_op jit(solution)/shard_map/dot_general | solution.py:77
  79.7 2.5 %pad.32 = bf16[32,256,256]{2,1,0:T(8,128)(2,1)} pad(bf16[27,256,256]{2,1,0:T(8,128)(2,1)S(1)} %copy-done.10, bf16[]{:T(256)} %constant.62.clone.1), padding=0_5x0_0x0_0 | pad | bytes 7733250
  82.8 2.6 %pad.29 = bf16[32,256,256]{2,1,0:T(8,128)(2,1)} pad(bf16[27,256,256]{2,1,0:T(8,128)(2,1)S(1)} %copy-done.7, bf16[]{:T(256)} %constant.62.clone.1), padding=0_5x0_0x0_0 | pad | bytes 7733250
  85.9 4.8 %fusion.46 = f32[27,27]{1,0:T(8,128)} fusion(bf16[27,256,256]{2,1,0:T(8,128)(2,1)S(1)} %copy-done.7, bf16[27,256,256]{2,1,0:T(8,128)(2,1)S(1)} %copy-done.9), kind=kOutput, calls=%fused_computation.36 | convolution fusion | flops 95551488 | bytes 7080804 | tf_op jit(solution)/shard_map/dot_general | solution.py:77
  90.8 2.5 %pad.31 = bf16[32,256,256]{2,1,0:T(8,128)(2,1)} pad(bf16[27,256,256]{2,1,0:T(8,128)(2,1)S(1)} %copy-done.9, bf16[]{:T(256)} %constant.62.clone.1), padding=0_5x0_0x0_0 | pad | bytes 7733250
  93.9 5.0 %fusion.41 = f32[27,27]{1,0:T(8,128)} fusion(bf16[27,256,256]{2,1,0:T(8,128)(2,1)S(1)} %copy-done.7, bf16[27,256,256]{2,1,0:T(8,128)(2,1)S(1)} %copy-done.8), kind=kOutput, calls=%fused_computation.35 | convolution fusion | flops 95551488 | bytes 7080804 | tf_op jit(solution)/shard_map/dot_general | solution.py:77
  98.8 2.6 %pad.30 = bf16[32,256,256]{2,1,0:T(8,128)(2,1)} pad(bf16[27,256,256]{2,1,0:T(8,128)(2,1)S(1)} %copy-done.8, bf16[]{:T(256)} %constant.62.clone.1), padding=0_5x0_0x0_0 | pad | bytes 7733250
  101.4 4.8 %fusion.36 = f32[27,27]{1,0:T(8,128)} fusion(bf16[27,256,256]{2,1,0:T(8,128)(2,1)S(1)} %copy-done.7, bf16[27,256,256]{2,1,0:T(8,128)(2,1)S(1)} %get-tuple-element.10), kind=kOutput, calls=%fused_computation.34 | convolution fusion | flops 95551488 | bytes 7080804 | tf_op jit(solution)/shard_map/dot_general | solution.py:77
  115.9 4.7 %copy.65 = bf16[4,8,256,256]{3,1,2,0:T(8,128)(2,1)S(1)} copy(bf16[4,8,256,256]{3,2,1,0:T(8,128)(2,1)} %bitcast.244) | data formatting | bytes 8388608
  134.0 4.7 %copy.61 = bf16[4,8,256,256]{3,1,2,0:T(8,128)(2,1)S(1)} copy(bf16[4,8,256,256]{3,2,1,0:T(8,128)(2,1)} %bitcast.242) | data formatting | bytes 8388608
  147.6 4.7 %copy.57 = bf16[4,8,256,256]{3,1,2,0:T(8,128)(2,1)S(1)} copy(bf16[4,8,256,256]{3,2,1,0:T(8,128)(2,1)} %bitcast.241) | data formatting | bytes 8388608
  161.2 4.9 %copy.52 = bf16[4,8,256,256]{3,1,2,0:T(8,128)(2,1)S(1)} copy(bf16[4,8,256,256]{3,2,1,0:T(8,128)(2,1)} %bitcast.240) | data formatting | bytes 8388608
  169.4 2.7 %collective-permute-start.4 = (bf16[4,256,10]{2,1,0:T(8,128)(2,1)S(1)}, bf16[4,256,10]{2,1,0:T(8,128)(2,1)S(1)}, u32[]{:S(2)}, u32[]{:S(2)}) collective-permute-start(bf16[4,256,10]{2,1,0:T(8,128)(2,1)S(1)} %get-tuple-element.21), channel_id=1, source_target_pairs={{0,4},{4,8},{8,12},{12,16},{16,20},{20,24},{24,28},{28,32},{32,36}... | collective-permute-start | bytes 61448 | tf_op jit(solution)/shard_map/ppermute | solution.py:15
  172.1 2.5 fusion
  176.6 6.4 %collective-permute-done.5 = bf16[4,256,10]{2,1,0:T(8,128)(2,1)S(1)} collective-permute-done((bf16[4,256,10]{2,1,0:T(8,128)(2,1)S(1)}, bf16[4,256,10]{2,1,0:T(8,128)(2,1)S(1)}, u32[]{:S(2)}, u32[]{:S(2)}) %collective-permute-start.5) | collective-permute-done | bytes 20512 | tf_op jit(solution)/shard_map/ppermute | solution.py:15
  183.2 8.0 %collective-permute-start.6 = (bf16[4,10,276]{2,1,0:T(8,128)(2,1)S(1)}, bf16[4,10,276]{2,1,0:T(8,128)(2,1)S(1)}, u32[]{:S(2)}, u32[]{:S(2)}) collective-permute-start(bf16[4,10,276]{2,1,0:T(8,128)(2,1)S(1)} %get-tuple-element.11), channel_id=1, source_target_pairs={{0,32},{4,36},{8,40},{12,44},{16,48},{20,52},{24,56},{28,60},{32,6... | collective-permute-start | bytes 66248 | tf_op jit(solution)/shard_map/ppermute | solution.py:15
  195.1 4.9 %collective-permute-done.7 = bf16[4,10,276]{2,1,0:T(8,128)(2,1)S(1)} collective-permute-done((bf16[4,10,276]{2,1,0:T(8,128)(2,1)S(1)}, bf16[4,10,276]{2,1,0:T(8,128)(2,1)S(1)}, u32[]{:S(2)}, u32[]{:S(2)}) %collective-permute-start.7) | collective-permute-done | bytes 22112 | tf_op jit(solution)/shard_map/ppermute | solution.py:15
  202.8 42.4 %reduce-scatter.3.cloned.1.call-done = f32[64,256]{1,0:T(8,128)} async-done(((f32[256,256]{1,0:T(8,128)}), f32[64,256]{1,0:T(8,128)}) %reduce-scatter.3.cloned.1.call-update) | async-done | bytes 65552 | tf_op jit(solution)/shard_map/reduce_scatter | solution.py:95
  (172 shorter events, 72.7 us)
Async XLA Ops:
  6.5 165.5 %copy-start = (f32[21]{0:T(128)S(1)}, f32[21]{0:T(128)}, u32[]{:S(2)}) copy-start(f32[21]{0:T(128)} %param.16) | copy-start | bytes 256
  6.5 24.7 %copy-start.32 = (f32[27,21]{0,1:T(8,128)S(1)}, f32[27,21]{0,1:T(8,128)}, u32[]{:S(2)}) copy-start(f32[27,21]{0,1:T(8,128)} %param.13) | copy-start | bytes 6808
  6.5 196.3 %reduce-scatter.5.cloned.1.call-start = ((), (), s32[]{:S(2)}) async-start(), calls=%async_computation.3 | async-start | bytes 327680 | tf_op jit(solution)/shard_map/reduce_scatter | solution.py:96
  19.3 15.7 %copy-start.13 = (bf16[1,256,256]{2,1,0:T(8,128)(2,1)}, bf16[1,256,256]{2,1,0:T(8,128)(2,1)S(1)}, u32[]{:S(2)}) copy-start(bf16[1,256,256]{2,1,0:T(8,128)(2,1)S(1)} %all_gather.3) | copy-start | bytes 393220
  19.4 15.6 %collective-permute-start.1 = (bf16[1,256,10]{2,1,0:T(8,128)(2,1)S(1)}, bf16[1,256,10]{2,1,0:T(8,128)(2,1)S(1)}, u32[]{:S(2)}, u32[]{:S(2)}) collective-permute-start(bf16[1,256,10]{2,1,0:T(8,128)(2,1)S(1)} %get-tuple-element.34), channel_id=1, source_target_pairs={{4,0},{8,4},{12,8},{16,12},{20,16},{24,20},{28,24},{32,28},{36,32}... | collective-permute-start | bytes 15368 | tf_op jit(solution)/shard_map/ppermute | solution.py:15
  20.7 14.3 %collective-permute-start = (bf16[1,256,10]{2,1,0:T(8,128)(2,1)S(1)}, bf16[1,256,10]{2,1,0:T(8,128)(2,1)S(1)}, u32[]{:S(2)}, u32[]{:S(2)}) collective-permute-start(bf16[1,256,10]{2,1,0:T(8,128)(2,1)S(1)} %get-tuple-element.33), channel_id=1, source_target_pairs={{0,4},{4,8},{8,12},{12,16},{16,20},{20,24},{24,28},{28,32},{32,36}... | collective-permute-start | bytes 15368 | tf_op jit(solution)/shard_map/ppermute | solution.py:15
  26.7 218.5 %reduce-scatter.3.cloned.1.call-start = ((), (), s32[]{:S(2)}) async-start(), calls=%async_computation.2 | async-start | bytes 327680 | tf_op jit(solution)/shard_map/reduce_scatter | solution.py:95
  26.8 8.0 %copy-start.11 = (s32[276,256]{1,0:T(8,128)}, s32[276,256]{1,0:T(8,128)S(1)}, u32[]{:S(2)}) copy-start(s32[276,256]{1,0:T(8,128)S(1)} %iota_subtract_fusion) | copy-start | bytes 847876
  26.8 7.9 %copy-start.18 = (bf16[1,4,256,256]{3,2,1,0:T(8,128)(2,1)S(1)}, bf16[1,4,256,256]{3,2,1,0:T(8,128)(2,1)}, u32[]{:S(2)}) copy-start(bf16[1,4,256,256]{3,2,1,0:T(8,128)(2,1)} %param.11) | copy-start | bytes 1572868
  31.2 9.9 %copy-start.6 = (s32[1,4,256,256]{3,2,1,0:T(8,128)S(1)}, s32[1,4,256,256]{3,2,1,0:T(8,128)}, u32[]{:S(2)}) copy-start(s32[1,4,256,256]{3,2,1,0:T(8,128)} %param.12) | copy-start | bytes 3145732
  35.0 4.7 %copy-start.27 = (bf16[1,256,10]{2,1,0:T(8,128)(2,1)}, bf16[1,256,10]{2,1,0:T(8,128)(2,1)S(1)}, u32[]{:S(2)}) copy-start(bf16[1,256,10]{2,1,0:T(8,128)(2,1)S(1)} %broadcast_select_fusion.2) | copy-start | bytes 15364
  35.1 17.1 %collective-permute-start.2 = (bf16[1,10,276]{2,1,0:T(8,128)(2,1)S(1)}, bf16[1,10,276]{2,1,0:T(8,128)(2,1)S(1)}, u32[]{:S(2)}, u32[]{:S(2)}) collective-permute-start(bf16[1,10,276]{2,1,0:T(8,128)(2,1)S(1)} %get-tuple-element.31), channel_id=1, source_target_pairs={{0,32},{4,36},{8,40},{12,44},{16,48},{20,52},{24,56},{28,60},{32,6... | collective-permute-start | bytes 16568 | tf_op jit(solution)/shard_map/ppermute | solution.py:15
  39.6 12.5 %collective-permute-start.3 = (bf16[1,10,276]{2,1,0:T(8,128)(2,1)S(1)}, bf16[1,10,276]{2,1,0:T(8,128)(2,1)S(1)}, u32[]{:S(2)}, u32[]{:S(2)}) collective-permute-start(bf16[1,10,276]{2,1,0:T(8,128)(2,1)S(1)} %get-tuple-element.32), channel_id=1, source_target_pairs={{32,0},{36,4},{40,8},{44,12},{48,16},{52,20},{56,24},{60,28},{64,3... | collective-permute-start | bytes 16568 | tf_op jit(solution)/shard_map/ppermute | solution.py:15
  71.7 8.0 %copy-start.10 = (bf16[27,256,256]{2,1,0:T(8,128)(2,1)S(1)}, bf16[27,256,256]{2,1,0:T(8,128)(2,1)}, u32[]{:S(2)}) copy-start(bf16[27,256,256]{2,1,0:T(8,128)(2,1)} %get-tuple-element.6) | copy-start | bytes 10616836
  115.9 4.7 %copy-start.26 = (bf16[1,1,256,256]{3,1,2,0:T(2,128)(2,1)S(1)}, bf16[1,1,256,256]{3,1,2,0:T(2,128)(2,1)}, u32[]{:S(2)}) copy-start(bf16[1,1,256,256]{3,1,2,0:T(2,128)(2,1)} %copy.66) | copy-start | bytes 393220
  134.0 4.7 %copy-start.25 = (bf16[1,1,256,256]{3,1,2,0:T(2,128)(2,1)S(1)}, bf16[1,1,256,256]{3,1,2,0:T(2,128)(2,1)}, u32[]{:S(2)}) copy-start(bf16[1,1,256,256]{3,1,2,0:T(2,128)(2,1)} %copy.62) | copy-start | bytes 393220
  147.6 4.7 %copy-start.24 = (bf16[1,1,256,256]{3,1,2,0:T(2,128)(2,1)S(1)}, bf16[1,1,256,256]{3,1,2,0:T(2,128)(2,1)}, u32[]{:S(2)}) copy-start(bf16[1,1,256,256]{3,1,2,0:T(2,128)(2,1)} %copy.58) | copy-start | bytes 393220
  161.2 4.9 %copy-start.23 = (bf16[1,1,256,256]{3,1,2,0:T(2,128)(2,1)S(1)}, bf16[1,1,256,256]{3,1,2,0:T(2,128)(2,1)}, u32[]{:S(2)}) copy-start(bf16[1,1,256,256]{3,1,2,0:T(2,128)(2,1)} %copy.53) | copy-start | bytes 393220
  167.4 4.7 %copy-start.12 = (s32[276,256]{1,0:T(8,128)S(1)}, s32[276,256]{1,0:T(8,128)}, u32[]{:S(2)}) copy-start(s32[276,256]{1,0:T(8,128)} %copy-done.11) | copy-start | bytes 847876
  169.0 23.5 %copy-start.34 = (f32[21]{0:T(128)S(1)}, f32[21]{0:T(128)}, u32[]{:S(2)}) copy-start(f32[21]{0:T(128)} %param.15) | copy-start | bytes 256
  169.4 7.3 %collective-permute-start.4 = (bf16[4,256,10]{2,1,0:T(8,128)(2,1)S(1)}, bf16[4,256,10]{2,1,0:T(8,128)(2,1)S(1)}, u32[]{:S(2)}, u32[]{:S(2)}) collective-permute-start(bf16[4,256,10]{2,1,0:T(8,128)(2,1)S(1)} %get-tuple-element.21), channel_id=1, source_target_pairs={{0,4},{4,8},{8,12},{12,16},{16,20},{20,24},{24,28},{28,32},{32,36}... | collective-permute-start | bytes 61448 | tf_op jit(solution)/shard_map/ppermute | solution.py:15
  174.6 8.4 %collective-permute-start.5 = (bf16[4,256,10]{2,1,0:T(8,128)(2,1)S(1)}, bf16[4,256,10]{2,1,0:T(8,128)(2,1)S(1)}, u32[]{:S(2)}, u32[]{:S(2)}) collective-permute-start(bf16[4,256,10]{2,1,0:T(8,128)(2,1)S(1)} %get-tuple-element.22), channel_id=1, source_target_pairs={{4,0},{8,4},{12,8},{16,12},{20,16},{24,20},{28,24},{32,28},{36,32}... | collective-permute-start | bytes 61448 | tf_op jit(solution)/shard_map/ppermute | solution.py:15
  183.2 11.9 %collective-permute-start.6 = (bf16[4,10,276]{2,1,0:T(8,128)(2,1)S(1)}, bf16[4,10,276]{2,1,0:T(8,128)(2,1)S(1)}, u32[]{:S(2)}, u32[]{:S(2)}) collective-permute-start(bf16[4,10,276]{2,1,0:T(8,128)(2,1)S(1)} %get-tuple-element.11), channel_id=1, source_target_pairs={{0,32},{4,36},{8,40},{12,44},{16,48},{20,52},{24,56},{28,60},{32,6... | collective-permute-start | bytes 66248 | tf_op jit(solution)/shard_map/ppermute | solution.py:15
  191.2 8.8 %collective-permute-start.7 = (bf16[4,10,276]{2,1,0:T(8,128)(2,1)S(1)}, bf16[4,10,276]{2,1,0:T(8,128)(2,1)S(1)}, u32[]{:S(2)}, u32[]{:S(2)}) collective-permute-start(bf16[4,10,276]{2,1,0:T(8,128)(2,1)S(1)} %get-tuple-element.12), channel_id=1, source_target_pairs={{32,0},{36,4},{40,8},{44,12},{48,16},{52,20},{56,24},{60,28},{64,3... | collective-permute-start | bytes 66248 | tf_op jit(solution)/shard_map/ppermute | solution.py:15
  (21 other events, 56.7 us)
Sparse Core Ops, SparseCore 0:
  26.9 40.9 reduce-scatter.4
  202.9 42.2 reduce-scatter.2
where the time goes:
time: 258 us; the launch traced here: 254 us
  matrix products  65.4 us (25%)
  waiting for transfers between devices  54.4 us (21%)
  local copies, waits for them, and re-layouts  52.8 us (20%)
  other arithmetic  29.5 us (11%)
  starting transfers between devices  24.6 us (10%)
  between operations  14.6 us (6%)
  blocking collectives  12.7 us (5%)
    unnamed x96, local copies, waits for them, and re-layouts  51.3 us
    reduce_scatter x1, waiting for transfers between devices, shards(): lax.psum_scatter(filtered, 'exp', scatter_dimension=0, tiled=True)  42.4 us
    ppermute x8, starting transfers between devices, passed_along(): return lax.ppermute(block, axis, route)  24.6 us
    dot_general x4, matrix products, shards(): lax.dot_general(masked, flat, (((1,), (1,)), ((), ())), preferred_element...  22.6 us
    dot_general x1, matrix products, convolve_rows(): jnp.einsum('bpi,bpj->bij', row_band, column_pass, preferred_element_type=...  18.9 us
    all_gather x1, blocking collectives, shards(): full_tile = lax.all_gather(template, 'exp', axis=1, tiled=True)  12.7 us
    another operation x12, other arithmetic, shards(): factor = jnp.linalg.cholesky(normal)  12.5 us
    ppermute x8, waiting for transfers between devices, passed_along(): return lax.ppermute(block, axis, route)  12 us
  transfers between devices with their start and end apart: 10, of which 4 were waited for; matrix products, arithmetic and copies ran while one was open for 55% of the time, Pallas kernels for 0%

commit v1 on v0

v1 whole, which is shorter than its diff:
```python
import jax
import jax.numpy as jnp
from jax import lax
from jax.experimental import pallas as pl
from jax.experimental.pallas import tpu as pltpu
from jax.sharding import PartitionSpec as P

HW = 10
KW = 21
NB = 27
GW = 8
PIX = 256
ROWS = 64
SLAB = 32
F32 = jnp.float32
BF16 = jnp.bfloat16


def toeplitz_rows(taps, rows):
    return pltpu.roll(jnp.broadcast_to(taps, (rows, taps.shape[1])), 0, 1, stride=1, stride_axis=0)


def fit_kernel(
    sky_ref, images_ref, masks_ref, row_taps_ref, col_taps_ref, out_ref,
    window, col_band, row_band, first, slab_wide, slab, plane,
):
    pieces = [sky_ref[k].astype(F32) for k in range(4)]
    window[...] = jnp.concatenate(
        [pieces[0][ROWS:ROWS + HW]] + [piece[:ROWS] for piece in pieces]
        + [pieces[3][ROWS:ROWS + HW], jnp.zeros((12, 384), F32)], 0
    ).astype(BF16)

    def build(b, carry):
        col = toeplitz_rows(col_taps_ref[pl.ds(b, 1), :], 256)
        col_band[b // 2, :, pl.ds(pl.multiple_of((b % 2) * 128, 128), 128)] = col[:, :128].astype(BF16)
        row_band[b] = toeplitz_rows(row_taps_ref[pl.ds(b, 1), :], 128).astype(BF16)
        return carry

    lax.fori_loop(0, NB + 1, build, 0)

    def columns(pair, carry):
        for half in range(2):
            out = jnp.dot(
                window[:, half * 128:half * 128 + 256], col_band[pair], preferred_element_type=F32
            ).astype(BF16)
            first[2 * pair, :, half * 128:half * 128 + 128] = out[:, :128]
            first[2 * pair + 1, :, half * 128:half * 128 + 128] = out[:, 128:]
        return carry

    lax.fori_loop(0, (NB + 1) // 2, columns, 0)

    for k in range(4):
        for half in range(2):
            slab_wide[half, pl.ds(NB + k, PIX, stride=SLAB), :] = images_ref[
                k, :, half * 128:half * 128 + 128
            ].astype(F32)
    for half in range(2):
        slab_wide[half, pl.ds(SLAB - 1, PIX, stride=SLAB), :] = jnp.zeros((PIX, 128), F32)

    def rows_pass(b, carry):
        for block in range(2):
            out = jnp.dot(
                row_band[b, :, :160], first[b, block * 128:block * 128 + 160, :],
                preferred_element_type=F32,
            )
            for half in range(2):
                slab_wide[half, pl.ds(block * 128 * SLAB + b, 128, stride=SLAB), :] = out[
                    :, half * 128:half * 128 + 128
                ]
        return carry

    lax.fori_loop(0, NB, rows_pass, 0)

    def gram(group, total):
        base = pl.multiple_of(group * 8 * SLAB, 8 * SLAB)
        at = pl.multiple_of(group * 8, 8)
        valid = [masks_ref[k, pl.ds(at, 8), :].astype(F32) for k in range(4)]
        for i in range(8):
            here = pl.ds(base + i * SLAB, SLAB)
            rows = jnp.concatenate([slab_wide[0, here, :], slab_wide[1, here, :]], 1)
            low = rows.astype(BF16)
            slab[here, :] = low
            masked = jnp.concatenate(
                [low * jnp.broadcast_to(v[i:i + 1].astype(BF16), low.shape) for v in valid], 0
            )
            total = total + lax.dot_general(
                low, masked, (((1,), (1,)), ((), ())), preferred_element_type=F32
            )
        return total

    matrix = lax.fori_loop(0, PIX // 8, gram, jnp.zeros((SLAB, 4 * SLAB), F32))

    lane = lax.broadcasted_iota(jnp.int32, (SLAB, 4 * SLAB), 1)
    row = lax.broadcasted_iota(jnp.int32, (SLAB, 4 * SLAB), 0)
    of_exposure = lane // SLAB
    of_basis = lane % SLAB
    for k in range(NB):
        column = jnp.take_along_axis(matrix, of_exposure * SLAB + k, axis=1)
        pivot_row = matrix[k:k + 1, :]
        pivot = column[k:k + 1, :]
        scaled = jnp.where(of_basis[:1] == k, 0.0, pivot_row / pivot)
        matrix = matrix - column * scaled
    top = jnp.sum(jnp.where(row == NB + of_exposure, matrix, 0.0), axis=0, keepdims=True)
    bottom = jnp.sum(jnp.where(row == of_basis, matrix, 0.0), axis=0, keepdims=True)
    solved = jnp.broadcast_to(top / bottom, (8, 4 * SLAB))
    lane8 = lax.broadcasted_iota(jnp.int32, (8, 4 * SLAB), 1)
    row8 = lax.broadcasted_iota(jnp.int32, (8, 4 * SLAB), 0)
    weights = []
    for k in range(4):
        own = -jnp.take_along_axis(solved, lane8 % SLAB + k * SLAB, axis=1)
        own = jnp.where(lane8 % SLAB == NB + k, 1.0, jnp.where(lane8 % SLAB >= NB, 0.0, own))
        weights.append(
            jnp.concatenate([jnp.where(row8 == lane8 // SLAB + 4 * half, own, 0.0) for half in range(2)], 1)
        )
    weights = jnp.concatenate(weights, 0).astype(BF16)

    plane[...] = jnp.zeros_like(plane)

    def residual(group, carry):
        base = pl.multiple_of(group * 8 * SLAB, 8 * SLAB)
        at = pl.multiple_of(group * 8, 8)
        left = jnp.dot(weights, slab[pl.ds(base, 8 * SLAB), :], preferred_element_type=F32)
        total = jnp.zeros((8, PIX), F32)
        for k in range(4):
            valid = masks_ref[k, pl.ds(at, 8), :].astype(F32)
            total = total + (valid * left[8 * k:8 * k + 8]).astype(BF16).astype(F32)
        plane[pl.ds(pl.multiple_of(group * 8 + 16, 8), 8), :] = total
        return carry

    lax.fori_loop(0, PIX // 8, residual, 0)
    for k in range(4):
        out_ref[k] = plane[64 * k + 6:64 * k + 6 + 96, :].astype(BF16)


def fit(sky, images, masks, row_taps, col_taps):
    vmem = pl.BlockSpec(memory_space=pltpu.VMEM)
    return pl.pallas_call(
        fit_kernel,
        out_shape=jax.ShapeDtypeStruct((4, 96, PIX), BF16),
        in_specs=[vmem] * 5,
        out_specs=vmem,
        scratch_shapes=[
            pltpu.VMEM((288, 384), BF16),
            pltpu.VMEM((14, 256, 256), BF16),
            pltpu.VMEM((28, 128, 256), BF16),
            pltpu.VMEM((28, 288, 256), BF16),
            pltpu.VMEM((2, PIX * SLAB, 128), F32),
            pltpu.VMEM((PIX * SLAB, 256), BF16),
            pltpu.VMEM((320, PIX), F32),
        ],
        compiler_params=pltpu.CompilerParams(vmem_limit_bytes=48 * 1024 * 1024),
        name="fit",
    )(sky, images, masks, row_taps, col_taps)


def filter_kernel(sky_ref, coverage_ref, row_taps_ref, col_taps_ref, out_ref):
    col_band = toeplitz_rows(col_taps_ref[...], 256)[:, :128]
    row_band = toeplitz_rows(row_taps_ref[...], ROWS)[:, :88]
    halves = [
        jnp.dot(sky_ref[:, half * 128:half * 128 + 256], col_band, precision=lax.Precision.HIGHEST,
                preferred_element_type=F32)
        for half in range(2)
    ]
    column_pass = jnp.concatenate(halves, 1)
    summed = jnp.dot(row_band, column_pass, precision=lax.Precision.HIGHEST, preferred_element_type=F32)
    out_ref[...] = summed / jnp.maximum(coverage_ref[...], 1.0)


def filter_rows(sky, coverage, row_taps, col_taps):
    vmem = pl.BlockSpec(memory_space=pltpu.VMEM)
    return pl.pallas_call(
        filter_kernel,
        out_shape=jax.ShapeDtypeStruct((ROWS, PIX), F32),
        in_specs=[vmem] * 4,
        out_specs=vmem,
        compiler_params=pltpu.CompilerParams(vmem_limit_bytes=32 * 1024 * 1024),
        name="filter",
    )(sky, coverage, row_taps, col_taps)


def routes(tiles, exps):
    east, west, border = [], [], []
    for t in range(tiles):
        for e in range(exps):
            if t % GW < GW - 1:
                east.append((t * exps + e, (t + 1) * exps + e))
            if t % GW > 0:
                west.append((t * exps + e, (t - 1) * exps + e))
        if t >= GW:
            border.append((t * exps, (t - GW) * exps + exps - 1))
        if t < tiles - GW:
            border.append((t * exps + exps - 1, (t + GW) * exps))
    return east, west, border


def send(values, route):
    return lax.ppermute(values, ("tile", "exp"), route)


def rising(taps):
    return jnp.pad(taps, ((0, (-taps.shape[0]) % 4), (0, 256 - KW)))


def falling(taps):
    return jnp.roll(jnp.pad(taps[:, ::-1], ((0, (-taps.shape[0]) % 4), (0, 256 - KW))), 1 - KW, 1)


def shards(template, exposures, masks, basis_rows, basis_cols, psf_row, psf_col):
    east, west, border = routes(lax.axis_size("tile"), lax.axis_size("exp"))
    place = lax.axis_index("exp")
    first_place, last_place = place == 0, place == lax.axis_size("exp") - 1

    coverage = lax.psum_scatter(
        jnp.sum(masks[0], axis=0).astype(F32), "exp", scatter_dimension=0, tiled=True
    )

    own = template[0]
    from_west = send(own[:, -HW:], east)
    from_east = send(own[:, :HW], west)
    wide = jnp.concatenate([from_west, own, from_east], 1)
    from_border = send(jnp.where(first_place, wide[:HW], wide[-HW:]), border)
    block = jnp.pad(jnp.concatenate([wide, from_border], 0), ((0, 6), (0, 108)))
    sky = lax.all_gather(block, "exp", axis=0)

    rounded = lambda taps: taps.astype(BF16).astype(F32)
    parts = fit(
        sky, exposures[0], masks[0], rising(rounded(basis_rows)), falling(rounded(basis_cols))
    )
    swapped = lax.all_to_all(parts, "exp", 0, 0)
    summed = jnp.sum(swapped[:, :84].astype(F32), axis=0)
    from_west = send(summed[:, -HW:], east)
    from_east = send(summed[:, :HW], west)
    wide = jnp.concatenate([from_west, summed, from_east], 1)
    from_border = send(jnp.where(first_place, wide[HW:2 * HW], wide[ROWS:ROWS + HW]), border)
    zeros = jnp.zeros_like(from_border)
    wide = jnp.concatenate(
        [
            jnp.where(first_place, from_border, wide[:HW]),
            wide[HW:HW + ROWS],
            jnp.where(last_place, from_border, wide[HW + ROWS:]),
        ],
        0,
    )
    wide = jnp.pad(wide, ((0, 4), (0, 108)))
    return filter_rows(wide, coverage, rising(psf_row[None])[:1], falling(psf_col[None])[:1])[None]


def solution(mesh):
    placed = (
        P("tile", "exp", None),
        P("tile", "exp", None, None),
        P("tile", "exp", None, None),
        P(),
        P(),
        P(),
        P(),
    )
    return jax.shard_map(
        shards, mesh=mesh, in_specs=placed, out_specs=P("tile", "exp", None), check_vma=False
    )
```

time: 258 us -> 132 us (0.51)
  the two profiles are of different devices: /device:TPU:1 before, /device:TPU:31 now
where the time goes in v1:
time: 132 us; the launch traced here: 130 us
  Pallas kernels  37.3 us (28%)
  waiting for transfers between devices  28.6 us (22%)
  starting transfers between devices  23 us (17%)
  blocking collectives  19 us (14%)
  between operations  13.5 us (10%)
  other arithmetic  4.36 us (3%)
  local copies, waits for them, and re-layouts  4.22 us (3%)
    pallas_call x1, Pallas kernels, fit(): pl.pallas_call(fit_kernel, out_shape=jax.ShapeDtypeStruct((4, 96, PIX), B...  36 us
    reduce_scatter x1, waiting for transfers between devices, shards(): lax.psum_scatter(jnp.sum(masks[0], axis=0).astype(F32), 'exp', scatter_di...  20.8 us
    all_gather x1, blocking collectives, shards(): sky = lax.all_gather(block, 'exp', axis=0)  19 us
    ppermute x6, starting transfers between devices, send(): return lax.ppermute(values, ('tile', 'exp'), route)  18.3 us
    all_to_all x1, waiting for transfers between devices, shards(): swapped = lax.all_to_all(parts, 'exp', 0, 0)  6.73 us
    all_to_all x1, starting transfers between devices, shards(): swapped = lax.all_to_all(parts, 'exp', 0, 0)  4.68 us
    unnamed x12, local copies, waits for them, and re-layouts  2.71 us
  transfers between devices with their start and end apart: 8, of which 3 were waited for; matrix products, arithmetic and copies ran while one was open for 3% of the time, Pallas kernels for 0%

profile of v1, /device:TPU:31, one launch (start us, length us, event | category | flops | bytes accessed | tf_op | source)
XLA Modules:
  0.0 130.1 jit_solution(5604548934026576815)
XLA Ops:
  6.5 0.9 fusion.14
  7.4 2.4 %collective-permute-start.1 = (bf16[64,10]{1,0:T(8,128)(2,1)S(1)}, bf16[64,10]{1,0:T(8,128)(2,1)S(1)}, u32[]{:S(2)}, u32[]{:S(2)}) collective-permute-start(bf16[64,10]{1,0:T(8,128)(2,1)S(1)} %get-tuple-element.10), channel_id=1, source_target_pairs={{4,0},{5,1},{6,2},{7,3},{8,4},{9,5},{10,6},{11,7},{12,8},{13,9},{1... | collective-permute-start | bytes 3848 | tf_op jit(solution)/shard_map/ppermute | solution.py:197
  9.8 5.0 %collective-permute-start = (bf16[64,10]{1,0:T(8,128)(2,1)S(1)}, bf16[64,10]{1,0:T(8,128)(2,1)S(1)}, u32[]{:S(2)}, u32[]{:S(2)}) collective-permute-start(bf16[64,10]{1,0:T(8,128)(2,1)S(1)} %get-tuple-element.9), channel_id=1, source_target_pairs={{0,4},{1,5},{2,6},{3,7},{4,8},{5,9},{6,10},{7,11},{8,12},{9,13},{1... | collective-permute-start | bytes 3848 | tf_op jit(solution)/shard_map/ppermute | solution.py:197
  14.8 0.7 convert_element_type.26
  15.5 0.1 copy.10
  15.6 0.7 convert_element_type.27
  16.6 0.8 fusion.12
  17.4 0.7 collective-permute-start.2
  18.2 0.8 fusion.8
  19.0 19.0 %all-gather = bf16[320,384]{1,0:T(8,128)(2,1)S(1)} all-gather(bf16[80,384]{1,0:T(8,128)(2,1)S(1)} %fusion.8), channel_id=2, replica_groups=mesh['tile'=64,'exp'=4] {'exp'}, dimensions={0}, use_global_device_ids=true | all-gather | bytes 307200 | tf_op jit(solution)/shard_map/all_gather | solution.py:223
  38.1 1.2 copy-done
  39.3 36.0 %fit.1 = bf16[4,96,256]{2,1,0:T(8,128)(2,1)} custom-call(bf16[4,80,384]{2,1,0:T(8,128)(2,1)S(1)} %bitcast.8, bf16[4,256,256]{2,1,0:T(8,128)(2,1)S(1)} %bitcast.9, s32[4,256,256]{2,1,0:T(8,128)S(1)} %bitcast.7, f32[28,256]{1,0:T(8,128)S(1)} %pad_convert_fusion.row_taps_ref, f32[28,256]{1,0:T(8,128)S(1)} %pad_maximum_fusion.1.col_taps_ref), custom_call_target="tpu_custom_call" | custom-call | tf_op jit(solution)/shard_map/fit/pallas_call | solution.py:137
  75.3 4.7 %all-to-all-start = ((bf16[4,96,256]{2,1,0:T(8,128)(2,1)}), bf16[4,96,256]{2,1,0:T(8,128)(2,1)S(1)}, u32[]{:S(2)}, u32[]{:S(2)}) async-start(bf16[4,96,256]{2,1,0:T(8,128)(2,1)} %fit.1), calls=%async_computation | async-start | bytes 393216 | tf_op jit(solution)/shard_map/all_to_all | solution.py:229
  80.1 0.7 convert_element_type.30
  80.9 0.6 copy-done.5
  81.7 6.7 %all-to-all-done = bf16[4,96,256]{2,1,0:T(8,128)(2,1)S(1)} async-done(((bf16[4,96,256]{2,1,0:T(8,128)(2,1)}), bf16[4,96,256]{2,1,0:T(8,128)(2,1)S(1)}, u32[]{:S(2)}, u32[]{:S(2)}) %all-to-all-start) | async-done | bytes 196640 | tf_op jit(solution)/shard_map/all_to_all | solution.py:229
  88.5 1.9 %collective-permute-start.4 = (f32[84,10]{1,0:T(8,128)S(1)}, f32[84,10]{1,0:T(8,128)S(1)}, u32[]{:S(2)}, u32[]{:S(2)}) collective-permute-start(f32[84,10]{1,0:T(8,128)S(1)} %get-tuple-element.8), channel_id=1, source_target_pairs={{4,0},{5,1},{6,2},{7,3},{8,4},{9,5},{10,6},{11,7},{12,8},{13,9},{1... | collective-permute-start | bytes 10088 | tf_op jit(solution)/shard_map/ppermute | solution.py:197
  90.4 7.7 %collective-permute-start.3 = (f32[84,10]{1,0:T(8,128)S(1)}, f32[84,10]{1,0:T(8,128)S(1)}, u32[]{:S(2)}, u32[]{:S(2)}) collective-permute-start(f32[84,10]{1,0:T(8,128)S(1)} %get-tuple-element.7), channel_id=1, source_target_pairs={{0,4},{1,5},{2,6},{3,7},{4,8},{5,9},{6,10},{7,11},{8,12},{9,13},{1... | collective-permute-start | bytes 10088 | tf_op jit(solution)/shard_map/ppermute | solution.py:197
  98.2 1.0 collective-permute-done.3
  99.3 0.7 collective-permute-start.5
  100.0 0.1 pad_maximum_fusion
  100.3 20.8 %reduce-scatter.2.cloned.1.call-done.coverage_ref = f32[64,256]{1,0:T(8,128)} async-done(((f32[256,256]{1,0:T(8,128)}), f32[64,256]{1,0:T(8,128)}) %reduce-scatter.2.cloned.1.call-update) | async-done | bytes 65552 | tf_op jit(solution)/shard_map/reduce_scatter | solution.py:213
  121.1 0.8 copy-done.3
  122.0 1.3 filter.1
  (33 shorter events, 1.0 us)
Async XLA Ops:
  6.5 31.5 %copy-start.2 = (bf16[1,4,256,256]{3,2,1,0:T(8,128)(2,1)S(1)}, bf16[1,4,256,256]{3,2,1,0:T(8,128)(2,1)}, u32[]{:S(2)}) copy-start(bf16[1,4,256,256]{3,2,1,0:T(8,128)(2,1)} %param.8) | copy-start | bytes 1572868
  7.4 9.2 %collective-permute-start.1 = (bf16[64,10]{1,0:T(8,128)(2,1)S(1)}, bf16[64,10]{1,0:T(8,128)(2,1)S(1)}, u32[]{:S(2)}, u32[]{:S(2)}) collective-permute-start(bf16[64,10]{1,0:T(8,128)(2,1)S(1)} %get-tuple-element.10), channel_id=1, source_target_pairs={{4,0},{5,1},{6,2},{7,3},{8,4},{9,5},{10,6},{11,7},{12,8},{13,9},{1... | collective-permute-start | bytes 3848 | tf_op jit(solution)/shard_map/ppermute | solution.py:197
  9.8 6.9 %collective-permute-start = (bf16[64,10]{1,0:T(8,128)(2,1)S(1)}, bf16[64,10]{1,0:T(8,128)(2,1)S(1)}, u32[]{:S(2)}, u32[]{:S(2)}) collective-permute-start(bf16[64,10]{1,0:T(8,128)(2,1)S(1)} %get-tuple-element.9), channel_id=1, source_target_pairs={{0,4},{1,5},{2,6},{3,7},{4,8},{5,9},{6,10},{7,11},{8,12},{9,13},{1... | collective-permute-start | bytes 3848 | tf_op jit(solution)/shard_map/ppermute | solution.py:197
  17.4 0.8 collective-permute-start.2
  38.1 1.2 copy-start
  39.3 40.7 %copy-start.1 = (s32[1,4,256,256]{3,2,1,0:T(8,128)S(1)}, s32[1,4,256,256]{3,2,1,0:T(8,128)}, u32[]{:S(2)}) copy-start(s32[1,4,256,256]{3,2,1,0:T(8,128)} %param.9) | copy-start | bytes 3145732
  75.3 13.1 %all-to-all-start = ((bf16[4,96,256]{2,1,0:T(8,128)(2,1)}), bf16[4,96,256]{2,1,0:T(8,128)(2,1)S(1)}, u32[]{:S(2)}, u32[]{:S(2)}) async-start(bf16[4,96,256]{2,1,0:T(8,128)(2,1)} %fit.1), calls=%async_computation | async-start | bytes 393216 | tf_op jit(solution)/shard_map/all_to_all | solution.py:229
  80.0 41.1 %reduce-scatter.2.cloned.1.call-start = ((), (), s32[]{:S(2)}) async-start(), calls=%async_computation.2 | async-start | bytes 327680 | tf_op jit(solution)/shard_map/reduce_scatter | solution.py:213
  80.8 0.7 copy-start.5
  88.5 9.7 %collective-permute-start.4 = (f32[84,10]{1,0:T(8,128)S(1)}, f32[84,10]{1,0:T(8,128)S(1)}, u32[]{:S(2)}, u32[]{:S(2)}) collective-permute-start(f32[84,10]{1,0:T(8,128)S(1)} %get-tuple-element.8), channel_id=1, source_target_pairs={{4,0},{5,1},{6,2},{7,3},{8,4},{9,5},{10,6},{11,7},{12,8},{13,9},{1... | collective-permute-start | bytes 10088 | tf_op jit(solution)/shard_map/ppermute | solution.py:197
  90.4 7.7 %copy-start.4 = (f32[21]{0:T(128)S(1)}, f32[21]{0:T(128)}, u32[]{:S(2)}) copy-start(f32[21]{0:T(128)} %param.12) | copy-start | bytes 256
  90.4 8.8 %collective-permute-start.3 = (f32[84,10]{1,0:T(8,128)S(1)}, f32[84,10]{1,0:T(8,128)S(1)}, u32[]{:S(2)}, u32[]{:S(2)}) collective-permute-start(f32[84,10]{1,0:T(8,128)S(1)} %get-tuple-element.7), channel_id=1, source_target_pairs={{0,4},{1,5},{2,6},{3,7},{4,8},{5,9},{6,10},{7,11},{8,12},{9,13},{1... | collective-permute-start | bytes 10088 | tf_op jit(solution)/shard_map/ppermute | solution.py:197
  99.3 0.8 collective-permute-start.5
  121.1 0.8 copy-start.3
Sparse Core Ops, SparseCore 0:
  83.5 37.5 reduce-scatter.1

commit v2 on v1

--- a/solution.py
+++ b/solution.py
@@ -12,6 +12,7 @@
 PIX = 256
 ROWS = 64
 SLAB = 32
+PITCH = PIX + 8
 F32 = jnp.float32
 BF16 = jnp.bfloat16
 
@@ -22,7 +23,7 @@
 
 def fit_kernel(
     sky_ref, images_ref, masks_ref, row_taps_ref, col_taps_ref, out_ref,
-    window, col_band, row_band, first, slab_wide, slab, plane,
+    window, col_band, row_band, first, slab_wide, slab, plane, counts,
 ):
     pieces = [sky_ref[k].astype(F32) for k in range(4)]
     window[...] = jnp.concatenate(
@@ -36,7 +37,7 @@
         row_band[b] = toeplitz_rows(row_taps_ref[pl.ds(b, 1), :], 128).astype(BF16)
         return carry
 
-    lax.fori_loop(0, NB + 1, build, 0)
+    lax.fori_loop(0, NB + 1, build, 0, unroll=4)
 
     def columns(pair, carry):
         for half in range(2):
@@ -47,15 +48,15 @@
             first[2 * pair + 1, :, half * 128:half * 128 + 128] = out[:, 128:]
         return carry
 
-    lax.fori_loop(0, (NB + 1) // 2, columns, 0)
+    lax.fori_loop(0, (NB + 1) // 2, columns, 0, unroll=7)
 
     for k in range(4):
         for half in range(2):
-            slab_wide[half, pl.ds(NB + k, PIX, stride=SLAB), :] = images_ref[
+            slab_wide[half, pl.ds((NB + k) * PITCH, PIX), :] = images_ref[
                 k, :, half * 128:half * 128 + 128
             ].astype(F32)
     for half in range(2):
-        slab_wide[half, pl.ds(SLAB - 1, PIX, stride=SLAB), :] = jnp.zeros((PIX, 128), F32)
+        slab_wide[half, pl.ds((SLAB - 1) * PITCH, PIX), :] = jnp.zeros((PIX, 128), F32)
 
     def rows_pass(b, carry):
         for block in range(2):
@@ -64,12 +65,12 @@
                 preferred_element_type=F32,
             )
             for half in range(2):
-                slab_wide[half, pl.ds(block * 128 * SLAB + b, 128, stride=SLAB), :] = out[
+                slab_wide[half, pl.ds(pl.multiple_of(b * PITCH + block * 128, 8), 128), :] = out[
                     :, half * 128:half * 128 + 128
                 ]
         return carry
 
-    lax.fori_loop(0, NB, rows_pass, 0)
+    lax.fori_loop(0, NB, rows_pass, 0, unroll=9)
 
     def gram(group, total):
         base = pl.multiple_of(group * 8 * SLAB, 8 * SLAB)
@@ -77,7 +78,8 @@
         valid = [masks_ref[k, pl.ds(at, 8), :].astype(F32) for k in range(4)]
         for i in range(8):
             here = pl.ds(base + i * SLAB, SLAB)
-            rows = jnp.concatenate([slab_wide[0, here, :], slab_wide[1, here, :]], 1)
+            there = pl.ds(group * 8 + i, SLAB, stride=PITCH)
+            rows = jnp.concatenate([slab_wide[0, there, :], slab_wide[1, there, :]], 1)
             low = rows.astype(BF16)
             slab[here, :] = low
             masked = jnp.concatenate(
@@ -88,7 +90,7 @@
             )
         return total
 
-    matrix = lax.fori_loop(0, PIX // 8, gram, jnp.zeros((SLAB, 4 * SLAB), F32))
+    matrix = lax.fori_loop(0, PIX // 8, gram, jnp.zeros((SLAB, 4 * SLAB), F32), unroll=2)
 
     lane = lax.broadcasted_iota(jnp.int32, (SLAB, 4 * SLAB), 1)
     row = lax.broadcasted_iota(jnp.int32, (SLAB, 4 * SLAB), 0)
@@ -121,22 +123,27 @@
         at = pl.multiple_of(group * 8, 8)
         left = jnp.dot(weights, slab[pl.ds(base, 8 * SLAB), :], preferred_element_type=F32)
         total = jnp.zeros((8, PIX), F32)
+        seen = jnp.zeros((8, PIX), F32)
         for k in range(4):
             valid = masks_ref[k, pl.ds(at, 8), :].astype(F32)
+            seen = seen + valid
             total = total + (valid * left[8 * k:8 * k + 8]).astype(BF16).astype(F32)
         plane[pl.ds(pl.multiple_of(group * 8 + 16, 8), 8), :] = total
-        return carry
-
-    lax.fori_loop(0, PIX // 8, residual, 0)
+        counts[pl.ds(at, 8), :] = seen
+        return carry
+
+    lax.fori_loop(0, PIX // 8, residual, 0, unroll=4)
     for k in range(4):
-        out_ref[k] = plane[64 * k + 6:64 * k + 6 + 96, :].astype(BF16)
+        out_ref[k] = jnp.concatenate(
+            [counts[64 * k:64 * k + 64, :], plane[64 * k + 6:64 * k + 6 + 96, :]], 0
+        ).astype(BF16)
 
 
 def fit(sky, images, masks, row_taps, col_taps):
     vmem = pl.BlockSpec(memory_space=pltpu.VMEM)
     return pl.pallas_call(
         fit_kernel,
-        out_shape=jax.ShapeDtypeStruct((4, 96, PIX), BF16),
+        out_shape=jax.ShapeDtypeStruct((4, 160, PIX), BF16),
         in_specs=[vmem] * 5,
         out_specs=vmem,
         scratch_shapes=[
@@ -144,9 +151,10 @@
             pltpu.VMEM((14, 256, 256), BF16),
             pltpu.VMEM((28, 128, 256), BF16),
             pltpu.VMEM((28, 288, 256), BF16),
-            pltpu.VMEM((2, PIX * SLAB, 128), F32),
+            pltpu.VMEM((2, PITCH * SLAB, 128), F32),
             pltpu.VMEM((PIX * SLAB, 256), BF16),
             pltpu.VMEM((320, PIX), F32),
+            pltpu.VMEM((PIX, PIX), F32),
         ],
         compiler_params=pltpu.CompilerParams(vmem_limit_bytes=48 * 1024 * 1024),
         name="fit",
@@ -210,14 +218,10 @@
     place = lax.axis_index("exp")
     first_place, last_place = place == 0, place == lax.axis_size("exp") - 1
 
-    coverage = lax.psum_scatter(
-        jnp.sum(masks[0], axis=0).astype(F32), "exp", scatter_dimension=0, tiled=True
-    )
-
     own = template[0]
     from_west = send(own[:, -HW:], east)
     from_east = send(own[:, :HW], west)
-    wide = jnp.concatenate([from_west, own, from_east], 1)
+    wide = lax.optimization_barrier(jnp.concatenate([from_west, own, from_east], 1))
     from_border = send(jnp.where(first_place, wide[:HW], wide[-HW:]), border)
     block = jnp.pad(jnp.concatenate([wide, from_border], 0), ((0, 6), (0, 108)))
     sky = lax.all_gather(block, "exp", axis=0)
@@ -227,7 +231,8 @@
         sky, exposures[0], masks[0], rising(rounded(basis_rows)), falling(rounded(basis_cols))
     )
     swapped = lax.all_to_all(parts, "exp", 0, 0)
-    summed = jnp.sum(swapped[:, :84].astype(F32), axis=0)
+    coverage = jnp.sum(swapped[:, :ROWS].astype(F32), axis=0)
+    summed = jnp.sum(swapped[:, ROWS:ROWS + 84].astype(F32), axis=0)
     from_west = send(summed[:, -HW:], east)
     from_east = send(summed[:, :HW], west)
     wide = jnp.concatenate([from_west, summed, from_east], 1)

time: 132 us -> 87 us (0.66)
  the two profiles are of different devices: /device:TPU:31 before, /device:TPU:30 now
where the time goes in v2:
time: 87 us; the launch traced here: 86.5 us
  waiting for transfers between devices  27.2 us (31%)
  starting transfers between devices  24.4 us (28%)
  Pallas kernels  17.2 us (20%)
  blocking collectives  10.7 us (12%)
  local copies, waits for them, and re-layouts  4.04 us (5%)
  other arithmetic  2.8 us (3%)
    ppermute x6, starting transfers between devices, send(): return lax.ppermute(values, ('tile', 'exp'), route)  20.9 us
    ppermute x6, waiting for transfers between devices, send(): return lax.ppermute(values, ('tile', 'exp'), route)  18.1 us
    pallas_call x1, Pallas kernels, fit(): pl.pallas_call(fit_kernel, out_shape=jax.ShapeDtypeStruct((4, 160, PIX),...  15.9 us
    all_gather x1, blocking collectives, shards(): sky = lax.all_gather(block, 'exp', axis=0)  10.7 us
    all_to_all x1, waiting for transfers between devices, shards(): swapped = lax.all_to_all(parts, 'exp', 0, 0)  9.15 us
    all_to_all x1, starting transfers between devices, shards(): swapped = lax.all_to_all(parts, 'exp', 0, 0)  3.45 us
    unnamed x8, local copies, waits for them, and re-layouts  2.53 us
  transfers between devices with their start and end apart: 7, of which 5 were waited for; matrix products, arithmetic and copies ran while one was open for 3% of the time, Pallas kernels for 0%

profile of v2, /device:TPU:30, one launch (start us, length us, event | category | flops | bytes accessed | tf_op | source)
XLA Modules:
  0.0 86.5 jit_solution(11159324055898574140)
XLA Ops:
  0.0 0.9 %fusion.7 = (bf16[64,10]{1,0:T(8,128)(2,1)S(1)}, bf16[64,10]{1,0:T(8,128)(2,1)S(1)}) fusion(bf16[64,256]{1,0:T(8,128)(2,1)} %bitcast.10), kind=kLoop, calls=%fused_computation.29 | loop fusion | bytes 5120 | tf_op jit(solution)/shard_map/slice | solution.py:222
  0.9 3.5 %collective-permute-start = (bf16[64,10]{1,0:T(8,128)(2,1)S(1)}, bf16[64,10]{1,0:T(8,128)(2,1)S(1)}, u32[]{:S(2)}, u32[]{:S(2)}) collective-permute-start(bf16[64,10]{1,0:T(8,128)(2,1)S(1)} %get-tuple-element.9), channel_id=1, source_target_pairs={{0,4},{1,5},{2,6},{3,7},{4,8},{5,9},{6,10},{7,11},{8,12},{9,13},{1... | collective-permute-start | bytes 3848 | tf_op jit(solution)/shard_map/ppermute | solution.py:205
  4.4 2.4 %collective-permute-start.1 = (bf16[64,10]{1,0:T(8,128)(2,1)S(1)}, bf16[64,10]{1,0:T(8,128)(2,1)S(1)}, u32[]{:S(2)}, u32[]{:S(2)}) collective-permute-start(bf16[64,10]{1,0:T(8,128)(2,1)S(1)} %get-tuple-element.10), channel_id=1, source_target_pairs={{4,0},{5,1},{6,2},{7,3},{8,4},{9,5},{10,6},{11,7},{12,8},{13,9},{1... | collective-permute-start | bytes 3848 | tf_op jit(solution)/shard_map/ppermute | solution.py:205
  6.7 0.7 convert_element_type.26
  7.4 0.1 copy.10
  7.5 0.7 convert_element_type.27
  8.6 3.5 %collective-permute-done.1 = bf16[64,10]{1,0:T(8,128)(2,1)S(1)} collective-permute-done((bf16[64,10]{1,0:T(8,128)(2,1)S(1)}, bf16[64,10]{1,0:T(8,128)(2,1)S(1)}, u32[]{:S(2)}, u32[]{:S(2)}) %collective-permute-start.1) | collective-permute-done | bytes 1312 | tf_op jit(solution)/shard_map/ppermute | solution.py:205
  12.1 0.8 pad_maximum_fusion.1
  13.0 5.6 %collective-permute-start.2 = (bf16[10,276]{1,0:T(8,128)(2,1)S(1)}, bf16[10,276]{1,0:T(8,128)(2,1)S(1)}, u32[]{:S(2)}, u32[]{:S(2)}) collective-permute-start(bf16[10,276]{1,0:T(8,128)(2,1)S(1)} %slice_select_fusion), channel_id=1, source_target_pairs={{3,32},{7,36},{11,40},{15,44},{19,48},{23,52},{27,56},{31,60},{32,... | collective-permute-start | bytes 16568 | tf_op jit(solution)/shard_map/ppermute | solution.py:205
  18.6 2.4 %collective-permute-done.2 = bf16[10,276]{1,0:T(8,128)(2,1)S(1)} collective-permute-done((bf16[10,276]{1,0:T(8,128)(2,1)S(1)}, bf16[10,276]{1,0:T(8,128)(2,1)S(1)}, u32[]{:S(2)}, u32[]{:S(2)}) %collective-permute-start.2) | collective-permute-done | bytes 5552 | tf_op jit(solution)/shard_map/ppermute | solution.py:205
  21.0 10.7 %all-gather = bf16[320,384]{1,0:T(8,128)(2,1)S(1)} all-gather(bf16[80,384]{1,0:T(8,128)(2,1)S(1)} %fusion.5), channel_id=2, replica_groups=mesh['tile'=64,'exp'=4] {'exp'}, dimensions={0}, use_global_device_ids=true | all-gather | bytes 307200 | tf_op jit(solution)/shard_map/all_gather | solution.py:227
  31.7 1.2 %copy-done = s32[1,4,256,256]{3,2,1,0:T(8,128)S(1)} copy-done((s32[1,4,256,256]{3,2,1,0:T(8,128)S(1)}, s32[1,4,256,256]{3,2,1,0:T(8,128)}, u32[]{:S(2)}) %copy-start) | copy-done | bytes 1048600
  32.9 15.9 %fit.1 = bf16[4,160,256]{2,1,0:T(8,128)(2,1)} custom-call(bf16[4,80,384]{2,1,0:T(8,128)(2,1)S(1)} %bitcast.8, bf16[4,256,256]{2,1,0:T(8,128)(2,1)S(1)} %bitcast.9, s32[4,256,256]{2,1,0:T(8,128)S(1)} %bitcast.7, f32[28,256]{1,0:T(8,128)S(1)} %pad_convert_fusion.row_taps_ref, f32[28,256]{1,0:T(8,128)S(1)} %pad_maximum_fusion.2.col_taps_ref), custom_call_target="tpu_custom_call" | custom-call | tf_op jit(solution)/shard_map/fit/pallas_call | solution.py:144
  48.8 3.5 %all-to-all-start = ((bf16[4,160,256]{2,1,0:T(8,128)(2,1)}), bf16[4,160,256]{2,1,0:T(8,128)(2,1)S(1)}, u32[]{:S(2)}, u32[]{:S(2)}) async-start(bf16[4,160,256]{2,1,0:T(8,128)(2,1)} %fit.1), calls=%async_computation | async-start | bytes 655360 | tf_op jit(solution)/shard_map/all_to_all | solution.py:233
  52.3 0.6 copy-done.3
  53.1 0.7 copy-done.2
  53.9 9.2 %all-to-all-done = bf16[4,160,256]{2,1,0:T(8,128)(2,1)S(1)} async-done(((bf16[4,160,256]{2,1,0:T(8,128)(2,1)}), bf16[4,160,256]{2,1,0:T(8,128)(2,1)S(1)}, u32[]{:S(2)}, u32[]{:S(2)}) %all-to-all-start) | async-done | bytes 327712 | tf_op jit(solution)/shard_map/all_to_all | solution.py:233
  63.1 5.6 %collective-permute-start.3 = (f32[84,10]{1,0:T(8,128)S(1)}, f32[84,10]{1,0:T(8,128)S(1)}, u32[]{:S(2)}, u32[]{:S(2)}) collective-permute-start(f32[84,10]{1,0:T(8,128)S(1)} %get-tuple-element.7), channel_id=1, source_target_pairs={{0,4},{1,5},{2,6},{3,7},{4,8},{5,9},{6,10},{7,11},{8,12},{9,13},{1... | collective-permute-start | bytes 10088 | tf_op jit(solution)/shard_map/ppermute | solution.py:205
  68.8 1.9 %collective-permute-start.4 = (f32[84,10]{1,0:T(8,128)S(1)}, f32[84,10]{1,0:T(8,128)S(1)}, u32[]{:S(2)}, u32[]{:S(2)}) collective-permute-start(f32[84,10]{1,0:T(8,128)S(1)} %get-tuple-element.8), channel_id=1, source_target_pairs={{4,0},{5,1},{6,2},{7,3},{8,4},{9,5},{10,6},{11,7},{12,8},{13,9},{1... | collective-permute-start | bytes 10088 | tf_op jit(solution)/shard_map/ppermute | solution.py:205
  70.8 6.1 %collective-permute-done.4 = f32[84,10]{1,0:T(8,128)S(1)} collective-permute-done((f32[84,10]{1,0:T(8,128)S(1)}, f32[84,10]{1,0:T(8,128)S(1)}, u32[]{:S(2)}, u32[]{:S(2)}) %collective-permute-start.4) | collective-permute-done | bytes 3392 | tf_op jit(solution)/shard_map/ppermute | solution.py:205
  76.9 1.9 %collective-permute-start.5 = (f32[10,276]{1,0:T(8,128)S(1)}, f32[10,276]{1,0:T(8,128)S(1)}, u32[]{:S(2)}, u32[]{:S(2)}) collective-permute-start(f32[10,276]{1,0:T(8,128)S(1)} %maximum_select_fusion.2), channel_id=1, source_target_pairs={{3,32},{7,36},{11,40},{15,44},{19,48},{23,52},{27,56},{31,60},{32,... | collective-permute-start | bytes 33128 | tf_op jit(solution)/shard_map/ppermute | solution.py:205
  78.9 0.1 pad_maximum_fusion
  79.0 6.1 %collective-permute-done.5 = f32[10,276]{1,0:T(8,128)S(1)} collective-permute-done((f32[10,276]{1,0:T(8,128)S(1)}, f32[10,276]{1,0:T(8,128)S(1)}, u32[]{:S(2)}, u32[]{:S(2)}) %collective-permute-start.5) | collective-permute-done | bytes 11072 | tf_op jit(solution)/shard_map/ppermute | solution.py:205
  85.2 1.3 %filter.1 = f32[64,256]{1,0:T(8,128)} custom-call(f32[88,384]{1,0:T(8,128)S(1)} %select_maximum_fusion.sky_ref, f32[64,256]{1,0:T(8,128)S(1)} %convert_reduce_fusion.1.coverage_ref, f32[1,256]{1,0:T(1,128)S(1)} %get-tuple-element.11.row_taps_ref, f32[1,256]{1,0:T(1,128)S(1)} %get-tuple-element.12.col_taps_ref), custom_call_target="tpu_custom_call" | custom-call | tf_op jit(solution)/shard_map/filter/pallas_call | solution.py:179
  (26 shorter events, 1.0 us)
Async XLA Ops:
  0.0 31.7 %copy-start.1 = (bf16[1,4,256,256]{3,2,1,0:T(8,128)(2,1)S(1)}, bf16[1,4,256,256]{3,2,1,0:T(8,128)(2,1)}, u32[]{:S(2)}) copy-start(bf16[1,4,256,256]{3,2,1,0:T(8,128)(2,1)} %param.8) | copy-start | bytes 1572868
  0.9 7.7 %collective-permute-start = (bf16[64,10]{1,0:T(8,128)(2,1)S(1)}, bf16[64,10]{1,0:T(8,128)(2,1)S(1)}, u32[]{:S(2)}, u32[]{:S(2)}) collective-permute-start(bf16[64,10]{1,0:T(8,128)(2,1)S(1)} %get-tuple-element.9), channel_id=1, source_target_pairs={{0,4},{1,5},{2,6},{3,7},{4,8},{5,9},{6,10},{7,11},{8,12},{9,13},{1... | collective-permute-start | bytes 3848 | tf_op jit(solution)/shard_map/ppermute | solution.py:205
  4.4 7.7 %collective-permute-start.1 = (bf16[64,10]{1,0:T(8,128)(2,1)S(1)}, bf16[64,10]{1,0:T(8,128)(2,1)S(1)}, u32[]{:S(2)}, u32[]{:S(2)}) collective-permute-start(bf16[64,10]{1,0:T(8,128)(2,1)S(1)} %get-tuple-element.10), channel_id=1, source_target_pairs={{4,0},{5,1},{6,2},{7,3},{8,4},{9,5},{10,6},{11,7},{12,8},{13,9},{1... | collective-permute-start | bytes 3848 | tf_op jit(solution)/shard_map/ppermute | solution.py:205
  13.0 8.0 %collective-permute-start.2 = (bf16[10,276]{1,0:T(8,128)(2,1)S(1)}, bf16[10,276]{1,0:T(8,128)(2,1)S(1)}, u32[]{:S(2)}, u32[]{:S(2)}) collective-permute-start(bf16[10,276]{1,0:T(8,128)(2,1)S(1)} %slice_select_fusion), channel_id=1, source_target_pairs={{3,32},{7,36},{11,40},{15,44},{19,48},{23,52},{27,56},{31,60},{32,... | collective-permute-start | bytes 16568 | tf_op jit(solution)/shard_map/ppermute | solution.py:205
  31.7 1.2 %copy-start = (s32[1,4,256,256]{3,2,1,0:T(8,128)S(1)}, s32[1,4,256,256]{3,2,1,0:T(8,128)}, u32[]{:S(2)}) copy-start(s32[1,4,256,256]{3,2,1,0:T(8,128)} %param.9) | copy-start | bytes 3145732
  48.8 14.2 %all-to-all-start = ((bf16[4,160,256]{2,1,0:T(8,128)(2,1)}), bf16[4,160,256]{2,1,0:T(8,128)(2,1)S(1)}, u32[]{:S(2)}, u32[]{:S(2)}) async-start(bf16[4,160,256]{2,1,0:T(8,128)(2,1)} %fit.1), calls=%async_computation | async-start | bytes 655360 | tf_op jit(solution)/shard_map/all_to_all | solution.py:233
  52.3 0.7 copy-start.3
  53.1 0.7 copy-start.2
  63.1 7.6 %collective-permute-start.3 = (f32[84,10]{1,0:T(8,128)S(1)}, f32[84,10]{1,0:T(8,128)S(1)}, u32[]{:S(2)}, u32[]{:S(2)}) collective-permute-start(f32[84,10]{1,0:T(8,128)S(1)} %get-tuple-element.7), channel_id=1, source_target_pairs={{0,4},{1,5},{2,6},{3,7},{4,8},{5,9},{6,10},{7,11},{8,12},{9,13},{1... | collective-permute-start | bytes 10088 | tf_op jit(solution)/shard_map/ppermute | solution.py:205
  68.8 8.0 %collective-permute-start.4 = (f32[84,10]{1,0:T(8,128)S(1)}, f32[84,10]{1,0:T(8,128)S(1)}, u32[]{:S(2)}, u32[]{:S(2)}) collective-permute-start(f32[84,10]{1,0:T(8,128)S(1)} %get-tuple-element.8), channel_id=1, source_target_pairs={{4,0},{5,1},{6,2},{7,3},{8,4},{9,5},{10,6},{11,7},{12,8},{13,9},{1... | collective-permute-start | bytes 10088 | tf_op jit(solution)/shard_map/ppermute | solution.py:205
  76.9 8.2 %collective-permute-start.5 = (f32[10,276]{1,0:T(8,128)S(1)}, f32[10,276]{1,0:T(8,128)S(1)}, u32[]{:S(2)}, u32[]{:S(2)}) collective-permute-start(f32[10,276]{1,0:T(8,128)S(1)} %maximum_select_fusion.2), channel_id=1, source_target_pairs={{3,32},{7,36},{11,40},{15,44},{19,48},{23,52},{27,56},{31,60},{32,... | collective-permute-start | bytes 33128 | tf_op jit(solution)/shard_map/ppermute | solution.py:205

commit v3 on v2

--- a/solution.py
+++ b/solution.py
@@ -22,22 +22,26 @@
 
 
 def fit_kernel(
-    sky_ref, images_ref, masks_ref, row_taps_ref, col_taps_ref, out_ref,
-    window, col_band, row_band, first, slab_wide, slab, plane, counts,
+    place_ref, sky_any, images_ref, masks_ref, row_taps_ref, col_taps_ref, mine_ref, theirs_ref,
+    sky_ref, window, col_band, row_band, first, slab_wide, slab, plane, counts, sky_sem,
 ):
+    sky_copy = pltpu.make_async_copy(sky_any, sky_ref, sky_sem)
+    sky_copy.start()
+
+    def build(b, carry):
+        col = toeplitz_rows(col_taps_ref[pl.ds(b, 1), :], 256)
+        col_band[b // 2, :, pl.ds(pl.multiple_of((b % 2) * 128, 128), 128)] = col[:, :128].astype(BF16)
+        row_band[b] = toeplitz_rows(row_taps_ref[pl.ds(b, 1), :], 128).astype(BF16)
+        return carry
+
+    lax.fori_loop(0, NB + 1, build, 0, unroll=4)
+
+    sky_copy.wait()
     pieces = [sky_ref[k].astype(F32) for k in range(4)]
     window[...] = jnp.concatenate(
         [pieces[0][ROWS:ROWS + HW]] + [piece[:ROWS] for piece in pieces]
         + [pieces[3][ROWS:ROWS + HW], jnp.zeros((12, 384), F32)], 0
     ).astype(BF16)
-
-    def build(b, carry):
-        col = toeplitz_rows(col_taps_ref[pl.ds(b, 1), :], 256)
-        col_band[b // 2, :, pl.ds(pl.multiple_of((b % 2) * 128, 128), 128)] = col[:, :128].astype(BF16)
-        row_band[b] = toeplitz_rows(row_taps_ref[pl.ds(b, 1), :], 128).astype(BF16)
-        return carry
-
-    lax.fori_loop(0, NB + 1, build, 0, unroll=4)
 
     def columns(pair, carry):
         for half in range(2):
@@ -133,20 +137,29 @@
         return carry
 
     lax.fori_loop(0, PIX // 8, residual, 0, unroll=4)
+
+    def block(k):
+        return jnp.concatenate(
+            [counts[ROWS * k:ROWS * k + ROWS, :], plane[ROWS * k + 6:ROWS * k + 6 + 88, :]], 0
+        ).astype(BF16)
+
     for k in range(4):
-        out_ref[k] = jnp.concatenate(
-            [counts[64 * k:64 * k + 64, :], plane[64 * k + 6:64 * k + 6 + 96, :]], 0
-        ).astype(BF16)
-
-
-def fit(sky, images, masks, row_taps, col_taps):
+
+        @pl.when(place_ref[0] == k)
+        def _():
+            mine_ref[0], mine_ref[1] = block(k), block(k ^ 2)
+            theirs_ref[0], theirs_ref[1] = block(k ^ 1), block(k ^ 3)
+
+
+def fit(place, sky, images, masks, row_taps, col_taps):
     vmem = pl.BlockSpec(memory_space=pltpu.VMEM)
     return pl.pallas_call(
         fit_kernel,
-        out_shape=jax.ShapeDtypeStruct((4, 160, PIX), BF16),
-        in_specs=[vmem] * 5,
-        out_specs=vmem,
+        out_shape=[jax.ShapeDtypeStruct((2, 152, PIX), BF16)] * 2,
+        in_specs=[pl.BlockSpec(memory_space=pltpu.SMEM), pl.BlockSpec(memory_space=pl.ANY)] + [vmem] * 4,
+        out_specs=[vmem] * 2,
         scratch_shapes=[
+            pltpu.VMEM((4, 80, 384), BF16),
             pltpu.VMEM((288, 384), BF16),
             pltpu.VMEM((14, 256, 256), BF16),
             pltpu.VMEM((28, 128, 256), BF16),
@@ -155,10 +168,11 @@
             pltpu.VMEM((PIX * SLAB, 256), BF16),
             pltpu.VMEM((320, PIX), F32),
             pltpu.VMEM((PIX, PIX), F32),
+            pltpu.SemaphoreType.DMA(()),
         ],
         compiler_params=pltpu.CompilerParams(vmem_limit_bytes=48 * 1024 * 1024),
         name="fit",
-    )(sky, images, masks, row_taps, col_taps)
+    )(place, sky, images, masks, row_taps, col_taps)
 
 
 def filter_kernel(sky_ref, coverage_ref, row_taps_ref, col_taps_ref, out_ref):
@@ -187,9 +201,11 @@
 
 
 def routes(tiles, exps):
-    east, west, border = [], [], []
+    east, west, border, core, half = [], [], [], [], []
     for t in range(tiles):
         for e in range(exps):
+            core.append((t * exps + e, t * exps + (e ^ 1)))
+            half.append((t * exps + e, t * exps + (e ^ 2)))
             if t % GW < GW - 1:
                 east.append((t * exps + e, (t + 1) * exps + e))
             if t % GW > 0:
@@ -198,7 +214,7 @@
             border.append((t * exps, (t - GW) * exps + exps - 1))
         if t < tiles - GW:
             border.append((t * exps + exps - 1, (t + GW) * exps))
-    return east, west, border
+    return east, west, border, core, half
 
 
 def send(values, route):
@@ -214,25 +230,25 @@
 
 
 def shards(template, exposures, masks, basis_rows, basis_cols, psf_row, psf_col):
-    east, west, border = routes(lax.axis_size("tile"), lax.axis_size("exp"))
+    east, west, border, core, half = routes(lax.axis_size("tile"), lax.axis_size("exp"))
     place = lax.axis_index("exp")
     first_place, last_place = place == 0, place == lax.axis_size("exp") - 1
 
     own = template[0]
-    from_west = send(own[:, -HW:], east)
-    from_east = send(own[:, :HW], west)
+    from_west = send(own, east)[:, -HW:]
+    from_east = send(own, west)[:, :HW]
     wide = lax.optimization_barrier(jnp.concatenate([from_west, own, from_east], 1))
     from_border = send(jnp.where(first_place, wide[:HW], wide[-HW:]), border)
     block = jnp.pad(jnp.concatenate([wide, from_border], 0), ((0, 6), (0, 108)))
     sky = lax.all_gather(block, "exp", axis=0)
 
     rounded = lambda taps: taps.astype(BF16).astype(F32)
-    parts = fit(
-        sky, exposures[0], masks[0], rising(rounded(basis_rows)), falling(rounded(basis_cols))
-    )
-    swapped = lax.all_to_all(parts, "exp", 0, 0)
-    coverage = jnp.sum(swapped[:, :ROWS].astype(F32), axis=0)
-    summed = jnp.sum(swapped[:, ROWS:ROWS + 84].astype(F32), axis=0)
+    mine, theirs = fit(
+        place[None], sky, exposures[0], masks[0], rising(rounded(basis_rows)), falling(rounded(basis_cols))
+    )
+    pair = mine.astype(F32) + send(theirs, core).astype(F32)
+    whole = pair[0] + send(pair[1].astype(BF16), half).astype(F32)
+    coverage, summed = whole[:ROWS], whole[ROWS:ROWS + 84]
     from_west = send(summed[:, -HW:], east)
     from_east = send(summed[:, :HW], west)
     wide = jnp.concatenate([from_west, summed, from_east], 1)

time: 87 us -> 79.3 us (0.911)
  waiting for transfers between devices: 27.2 us -> 23.8 us
  starting transfers between devices: 24.4 us -> 22.4 us
  local copies, waits for them, and re-layouts: 4.04 us -> 2.2 us
    all_to_all x1 -> x0, waiting for transfers between devices: 9.15 us -> none  [shards(): swapped = lax.all_to_all(parts, 'exp', 0, 0)]
    ppermute x6 -> x8, waiting for transfers between devices: 18.1 us -> 23.8 us  [send(): return lax.ppermute(values, ('tile', 'exp'), route)]
    all_to_all x1 -> x0, starting transfers between devices: 3.45 us -> none  [shards(): swapped = lax.all_to_all(parts, 'exp', 0, 0)]
    ppermute x6 -> x8, starting transfers between devices: 20.9 us -> 22.4 us  [send(): return lax.ppermute(values, ('tile', 'exp'), route)]
    unnamed x8, local copies, waits for them, and re-layouts: 2.53 us -> 1.45 us
  transfers between devices with their start and end apart: 7 -> 8, of which waited for: 5 -> 6; matrix products, arithmetic and copies ran while one was open for 3% -> 3% of each run, Pallas kernels for 0% -> 0%
where the time goes in v3:
time: 79.3 us; the launch traced here: 78.9 us
  waiting for transfers between devices  23.8 us (30%)
  starting transfers between devices  22.4 us (28%)
  Pallas kernels  16.8 us (21%)
  blocking collectives  10.7 us (13%)
  other arithmetic  2.81 us (4%)
  local copies, waits for them, and re-layouts  2.2 us (3%)
    ppermute x8, waiting for transfers between devices, send(): return lax.ppermute(values, ('tile', 'exp'), route)  23.8 us
    ppermute x8, starting transfers between devices, send(): return lax.ppermute(values, ('tile', 'exp'), route)  22.4 us
    pallas_call x1, Pallas kernels, fit(): pl.pallas_call(fit_kernel, out_shape=[jax.ShapeDtypeStruct((2, 152, PIX),...  15.5 us
    all_gather x1, blocking collectives, shards(): sky = lax.all_gather(block, 'exp', axis=0)  10.7 us
  transfers between devices with their start and end apart: 8, of which 6 were waited for; matrix products, arithmetic and copies ran while one was open for 3% of the time, Pallas kernels for 0%

profile of v3, /device:TPU:30, one launch (start us, length us, event | category | flops | bytes accessed | tf_op | source)
XLA Modules:
  0.0 78.9 jit_solution(15345088238468051506)
XLA Ops:
  0.0 3.6 %collective-permute-start = (bf16[64,256]{1,0:T(8,128)(2,1)}, bf16[64,256]{1,0:T(8,128)(2,1)S(1)}, u32[]{:S(2)}, u32[]{:S(2)}) collective-permute-start(bf16[64,256]{1,0:T(8,128)(2,1)} %bitcast.17), channel_id=1, source_target_pairs={{0,4},{1,5},{2,6},{3,7},{4,8},{5,9},{6,10},{7,11},{8,12},{9,13},{1... | collective-permute-start | bytes 98312 | tf_op jit(solution)/shard_map/ppermute | solution.py:221
  3.6 2.4 %collective-permute-start.1 = (bf16[64,256]{1,0:T(8,128)(2,1)}, bf16[64,256]{1,0:T(8,128)(2,1)S(1)}, u32[]{:S(2)}, u32[]{:S(2)}) collective-permute-start(bf16[64,256]{1,0:T(8,128)(2,1)} %bitcast.18), channel_id=1, source_target_pairs={{4,0},{5,1},{6,2},{7,3},{8,4},{9,5},{10,6},{11,7},{12,8},{13,9},{1... | collective-permute-start | bytes 98312 | tf_op jit(solution)/shard_map/ppermute | solution.py:221
  6.0 0.7 convert_element_type.34
  7.0 0.7 convert_element_type.33
  7.7 0.1 copy.10
  7.9 3.8 %collective-permute-done.1 = bf16[64,256]{1,0:T(8,128)(2,1)S(1)} collective-permute-done((bf16[64,256]{1,0:T(8,128)(2,1)}, bf16[64,256]{1,0:T(8,128)(2,1)S(1)}, u32[]{:S(2)}, u32[]{:S(2)}) %collective-permute-start.1) | collective-permute-done | bytes 32800 | tf_op jit(solution)/shard_map/ppermute | solution.py:221
  11.8 0.8 %pad_maximum_fusion.1 = bf16[64,276]{1,0:T(8,128)(2,1)S(1)} fusion(bf16[64,10]{1,0:T(8,128)(2,1)S(1)} %slice.92, bf16[64,256]{1,0:T(8,128)(2,1)} %bitcast.19, bf16[64,10]{1,0:T(8,128)(2,1)S(1)} %slice.91), kind=kLoop, calls=%fused_computation.18 | loop fusion | flops 105984 | bytes 70656 | tf_op jit(solution)/shard_map/concatenate | solution.py:240
  12.6 5.6 %collective-permute-start.2 = (bf16[10,276]{1,0:T(8,128)(2,1)S(1)}, bf16[10,276]{1,0:T(8,128)(2,1)S(1)}, u32[]{:S(2)}, u32[]{:S(2)}) collective-permute-start(bf16[10,276]{1,0:T(8,128)(2,1)S(1)} %slice_select_fusion), channel_id=1, source_target_pairs={{3,32},{7,36},{11,40},{15,44},{19,48},{23,52},{27,56},{31,60},{32,... | collective-permute-start | bytes 16568 | tf_op jit(solution)/shard_map/ppermute | solution.py:221
  18.3 2.4 %collective-permute-done.2 = bf16[10,276]{1,0:T(8,128)(2,1)S(1)} collective-permute-done((bf16[10,276]{1,0:T(8,128)(2,1)S(1)}, bf16[10,276]{1,0:T(8,128)(2,1)S(1)}, u32[]{:S(2)}, u32[]{:S(2)}) %collective-permute-start.2) | collective-permute-done | bytes 5552 | tf_op jit(solution)/shard_map/ppermute | solution.py:221
  20.7 10.7 %all-gather = bf16[320,384]{1,0:T(8,128)(2,1)S(1)} all-gather(bf16[80,384]{1,0:T(8,128)(2,1)S(1)} %fusion.7), channel_id=2, replica_groups=mesh['tile'=64,'exp'=4] {'exp'}, dimensions={0}, use_global_device_ids=true | all-gather | bytes 307200 | tf_op jit(solution)/shard_map/all_gather | solution.py:243
  31.3 1.2 %copy-done = s32[1,4,256,256]{3,2,1,0:T(8,128)S(1)} copy-done((s32[1,4,256,256]{3,2,1,0:T(8,128)S(1)}, s32[1,4,256,256]{3,2,1,0:T(8,128)}, u32[]{:S(2)}) %copy-start) | copy-done | bytes 1048600
  32.6 15.5 %fit.1 = (bf16[2,152,256]{2,1,0:T(8,128)(2,1)S(1)}, bf16[2,152,256]{2,1,0:T(8,128)(2,1)S(1)}) custom-call(s32[1]{0:T(128)} %bitcast.place_ref, bf16[4,80,384]{2,1,0:T(8,128)(2,1)S(1)} %bitcast.15, bf16[4,256,256]{2,1,0:T(8,128)(2,1)S(1)} %bitcast.16, s32[4,256,256]{2,1,0:T(8,128)S(1)} %bitcast.14, f32[28,256]{1,0:T(8,128)S(1)} %pad_convert_fusion.row_taps_ref, ...), custom_call_target="tpu_custom_call" | custom-call | tf_op jit(solution)/shard_map/fit/pallas_call | solution.py:156
  48.1 0.4 collective-permute-start.3
  48.5 0.2 copy-done.3
  48.9 0.7 collective-permute-done.3
  49.6 1.6 %collective-permute-start.4 = (bf16[152,256]{1,0:T(8,128)(2,1)S(1)}, bf16[152,256]{1,0:T(8,128)(2,1)S(1)}, u32[]{:S(2)}, u32[]{:S(2)}) collective-permute-start(bf16[152,256]{1,0:T(8,128)(2,1)S(1)} %fusion.6), channel_id=1, source_target_pairs={{0,2},{1,3},{2,0},{3,1},{4,6},{5,7},{6,4},{7,5},{8,10},{9,11},{10,... | collective-permute-start | bytes 233480 | tf_op jit(solution)/shard_map/ppermute | solution.py:221
  51.2 8.0 %collective-permute-done.4 = bf16[152,256]{1,0:T(8,128)(2,1)S(1)} collective-permute-done((bf16[152,256]{1,0:T(8,128)(2,1)S(1)}, bf16[152,256]{1,0:T(8,128)(2,1)S(1)}, u32[]{:S(2)}, u32[]{:S(2)}) %collective-permute-start.4) | collective-permute-done | bytes 77856 | tf_op jit(solution)/shard_map/ppermute | solution.py:221
  59.2 1.9 %collective-permute-start.5 = (f32[84,10]{1,0:T(8,128)S(1)}, f32[84,10]{1,0:T(8,128)S(1)}, u32[]{:S(2)}, u32[]{:S(2)}) collective-permute-start(f32[84,10]{1,0:T(8,128)S(1)} %get-tuple-element.11), channel_id=1, source_target_pairs={{0,4},{1,5},{2,6},{3,7},{4,8},{5,9},{6,10},{7,11},{8,12},{9,13},{1... | collective-permute-start | bytes 10088 | tf_op jit(solution)/shard_map/ppermute | solution.py:221
  61.2 3.9 %collective-permute-start.6 = (f32[84,10]{1,0:T(8,128)S(1)}, f32[84,10]{1,0:T(8,128)S(1)}, u32[]{:S(2)}, u32[]{:S(2)}) collective-permute-start(f32[84,10]{1,0:T(8,128)S(1)} %get-tuple-element.12), channel_id=1, source_target_pairs={{4,0},{5,1},{6,2},{7,3},{8,4},{9,5},{10,6},{11,7},{12,8},{13,9},{1... | collective-permute-start | bytes 10088 | tf_op jit(solution)/shard_map/ppermute | solution.py:221
  65.2 4.0 %collective-permute-done.6 = f32[84,10]{1,0:T(8,128)S(1)} collective-permute-done((f32[84,10]{1,0:T(8,128)S(1)}, f32[84,10]{1,0:T(8,128)S(1)}, u32[]{:S(2)}, u32[]{:S(2)}) %collective-permute-start.6) | collective-permute-done | bytes 3392 | tf_op jit(solution)/shard_map/ppermute | solution.py:221
  69.3 3.0 %collective-permute-start.7 = (f32[10,276]{1,0:T(8,128)S(1)}, f32[10,276]{1,0:T(8,128)S(1)}, u32[]{:S(2)}, u32[]{:S(2)}) collective-permute-start(f32[10,276]{1,0:T(8,128)S(1)} %maximum_select_fusion.2), channel_id=1, source_target_pairs={{3,32},{7,36},{11,40},{15,44},{19,48},{23,52},{27,56},{31,60},{32,... | collective-permute-start | bytes 33128 | tf_op jit(solution)/shard_map/ppermute | solution.py:221
  72.4 0.1 pad_maximum_fusion
  72.5 5.0 %collective-permute-done.7 = f32[10,276]{1,0:T(8,128)S(1)} collective-permute-done((f32[10,276]{1,0:T(8,128)S(1)}, f32[10,276]{1,0:T(8,128)S(1)}, u32[]{:S(2)}, u32[]{:S(2)}) %collective-permute-start.7) | collective-permute-done | bytes 11072 | tf_op jit(solution)/shard_map/ppermute | solution.py:221
  77.6 1.3 %filter.1 = f32[64,256]{1,0:T(8,128)} custom-call(f32[88,384]{1,0:T(8,128)S(1)} %select_maximum_fusion.sky_ref, f32[64,256]{1,0:T(8,128)S(1)} %slice.101.coverage_ref, f32[1,256]{1,0:T(1,128)S(1)} %get-tuple-element.13.row_taps_ref, f32[1,256]{1,0:T(1,128)S(1)} %get-tuple-element.14.col_taps_ref), custom_call_target="tpu_custom_call" | custom-call | tf_op jit(solution)/shard_map/filter/pallas_call | solution.py:193
  (32 shorter events, 1.1 us)
Async XLA Ops:
  0.0 31.3 %copy-start.1 = (bf16[1,4,256,256]{3,2,1,0:T(8,128)(2,1)S(1)}, bf16[1,4,256,256]{3,2,1,0:T(8,128)(2,1)}, u32[]{:S(2)}) copy-start(bf16[1,4,256,256]{3,2,1,0:T(8,128)(2,1)} %param.8) | copy-start | bytes 1572868
  0.0 7.8 %collective-permute-start = (bf16[64,256]{1,0:T(8,128)(2,1)}, bf16[64,256]{1,0:T(8,128)(2,1)S(1)}, u32[]{:S(2)}, u32[]{:S(2)}) collective-permute-start(bf16[64,256]{1,0:T(8,128)(2,1)} %bitcast.17), channel_id=1, source_target_pairs={{0,4},{1,5},{2,6},{3,7},{4,8},{5,9},{6,10},{7,11},{8,12},{9,13},{1... | collective-permute-start | bytes 98312 | tf_op jit(solution)/shard_map/ppermute | solution.py:221
  3.6 8.1 %collective-permute-start.1 = (bf16[64,256]{1,0:T(8,128)(2,1)}, bf16[64,256]{1,0:T(8,128)(2,1)S(1)}, u32[]{:S(2)}, u32[]{:S(2)}) collective-permute-start(bf16[64,256]{1,0:T(8,128)(2,1)} %bitcast.18), channel_id=1, source_target_pairs={{4,0},{5,1},{6,2},{7,3},{8,4},{9,5},{10,6},{11,7},{12,8},{13,9},{1... | collective-permute-start | bytes 98312 | tf_op jit(solution)/shard_map/ppermute | solution.py:221
  12.6 8.0 %collective-permute-start.2 = (bf16[10,276]{1,0:T(8,128)(2,1)S(1)}, bf16[10,276]{1,0:T(8,128)(2,1)S(1)}, u32[]{:S(2)}, u32[]{:S(2)}) collective-permute-start(bf16[10,276]{1,0:T(8,128)(2,1)S(1)} %slice_select_fusion), channel_id=1, source_target_pairs={{3,32},{7,36},{11,40},{15,44},{19,48},{23,52},{27,56},{31,60},{32,... | collective-permute-start | bytes 16568 | tf_op jit(solution)/shard_map/ppermute | solution.py:221
  31.3 1.2 %copy-start = (s32[1,4,256,256]{3,2,1,0:T(8,128)S(1)}, s32[1,4,256,256]{3,2,1,0:T(8,128)}, u32[]{:S(2)}) copy-start(s32[1,4,256,256]{3,2,1,0:T(8,128)} %param.9) | copy-start | bytes 3145732
  48.1 0.7 copy-start.3
  48.1 1.5 %collective-permute-start.3 = (bf16[2,152,256]{2,1,0:T(8,128)(2,1)S(1)}, bf16[2,152,256]{2,1,0:T(8,128)(2,1)S(1)}, u32[]{:S(2)}, u32[]{:S(2)}) collective-permute-start(bf16[2,152,256]{2,1,0:T(8,128)(2,1)S(1)} %get-tuple-element.8), channel_id=1, source_target_pairs={{0,1},{1,0},{2,3},{3,2},{4,5},{5,4},{6,7},{7,6},{8,9},{9,8},{10,11... | collective-permute-start | bytes 466952 | tf_op jit(solution)/shard_map/ppermute | solution.py:221
  49.6 9.5 %collective-permute-start.4 = (bf16[152,256]{1,0:T(8,128)(2,1)S(1)}, bf16[152,256]{1,0:T(8,128)(2,1)S(1)}, u32[]{:S(2)}, u32[]{:S(2)}) collective-permute-start(bf16[152,256]{1,0:T(8,128)(2,1)S(1)} %fusion.6), channel_id=1, source_target_pairs={{0,2},{1,3},{2,0},{3,1},{4,6},{5,7},{6,4},{7,5},{8,10},{9,11},{10,... | collective-permute-start | bytes 233480 | tf_op jit(solution)/shard_map/ppermute | solution.py:221
  59.2 6.0 %collective-permute-start.5 = (f32[84,10]{1,0:T(8,128)S(1)}, f32[84,10]{1,0:T(8,128)S(1)}, u32[]{:S(2)}, u32[]{:S(2)}) collective-permute-start(f32[84,10]{1,0:T(8,128)S(1)} %get-tuple-element.11), channel_id=1, source_target_pairs={{0,4},{1,5},{2,6},{3,7},{4,8},{5,9},{6,10},{7,11},{8,12},{9,13},{1... | collective-permute-start | bytes 10088 | tf_op jit(solution)/shard_map/ppermute | solution.py:221
  61.2 3.9 %copy-start.2 = (f32[21]{0:T(128)S(1)}, f32[21]{0:T(128)}, u32[]{:S(2)}) copy-start(f32[21]{0:T(128)} %param.12) | copy-start | bytes 256
  61.2 8.0 %collective-permute-start.6 = (f32[84,10]{1,0:T(8,128)S(1)}, f32[84,10]{1,0:T(8,128)S(1)}, u32[]{:S(2)}, u32[]{:S(2)}) collective-permute-start(f32[84,10]{1,0:T(8,128)S(1)} %get-tuple-element.12), channel_id=1, source_target_pairs={{4,0},{5,1},{6,2},{7,3},{8,4},{9,5},{10,6},{11,7},{12,8},{13,9},{1... | collective-permute-start | bytes 10088 | tf_op jit(solution)/shard_map/ppermute | solution.py:221
  69.3 8.2 %collective-permute-start.7 = (f32[10,276]{1,0:T(8,128)S(1)}, f32[10,276]{1,0:T(8,128)S(1)}, u32[]{:S(2)}, u32[]{:S(2)}) collective-permute-start(f32[10,276]{1,0:T(8,128)S(1)} %maximum_select_fusion.2), channel_id=1, source_target_pairs={{3,32},{7,36},{11,40},{15,44},{19,48},{23,52},{27,56},{31,60},{32,... | collective-permute-start | bytes 33128 | tf_op jit(solution)/shard_map/ppermute | solution.py:221

commit v4 on v3

--- a/solution.py
+++ b/solution.py
@@ -11,6 +11,7 @@
 GW = 8
 PIX = 256
 ROWS = 64
+HALF = 128
 SLAB = 32
 PITCH = PIX + 8
 F32 = jnp.float32
@@ -22,11 +23,18 @@
 
 
 def fit_kernel(
-    place_ref, sky_any, images_ref, masks_ref, row_taps_ref, col_taps_ref, mine_ref, theirs_ref,
-    sky_ref, window, col_band, row_band, first, slab_wide, slab, plane, counts, sky_sem,
+    place_ref, own_any, far_any, far_core_any, edge_any, edge_core_any, images_ref, masks_ref, row_taps_ref, col_taps_ref, mine_ref, theirs_ref,
+    own_ref, far_ref, edge_ref, window, col_band, row_band, first, slab_wide, slab, plane, counts, sky_sem,
 ):
-    sky_copy = pltpu.make_async_copy(sky_any, sky_ref, sky_sem)
-    sky_copy.start()
+    arriving = [
+        pltpu.make_async_copy(source, target, sky_sem.at[k])
+        for k, (source, target) in enumerate((
+            (own_any, own_ref), (far_any, far_ref.at[0]), (far_core_any, far_ref.at[1]),
+            (edge_any, edge_ref.at[0]), (edge_core_any, edge_ref.at[1]),
+        ))
+    ]
+    for copy in arriving:
+        copy.start()
 
     def build(b, carry):
         col = toeplitz_rows(col_taps_ref[pl.ds(b, 1), :], 256)
@@ -34,13 +42,19 @@
         row_band[b] = toeplitz_rows(row_taps_ref[pl.ds(b, 1), :], 128).astype(BF16)
         return carry
 
-    lax.fori_loop(0, NB + 1, build, 0, unroll=4)
-
-    sky_copy.wait()
-    pieces = [sky_ref[k].astype(F32) for k in range(4)]
+    lax.fori_loop(0, NB + 1, build, 0, unroll=14)
+
+    for copy in arriving:
+        copy.wait()
+    on_left, on_top = place_ref[0] % 2 == 0, place_ref[0] < 2
+    own = own_ref[...].astype(F32)
+    quarters = [far_ref[k].astype(F32) for k in range(2)]
+    edges = [edge_ref[k].astype(F32) for k in range(2)]
+    far = jnp.concatenate([jnp.where(on_left, *quarters), jnp.where(on_left, *quarters[::-1])], 0)
+    north, south = jnp.where(on_left, *edges), jnp.where(on_left, *edges[::-1])
     window[...] = jnp.concatenate(
-        [pieces[0][ROWS:ROWS + HW]] + [piece[:ROWS] for piece in pieces]
-        + [pieces[3][ROWS:ROWS + HW], jnp.zeros((12, 384), F32)], 0
+        [north[16 - HW:], jnp.where(on_top, own, far), jnp.where(on_top, far, own), south[:HW],
+         jnp.zeros((12, 384), F32)], 0
     ).astype(BF16)
 
     def columns(pair, carry):
@@ -52,7 +66,7 @@
             first[2 * pair + 1, :, half * 128:half * 128 + 128] = out[:, 128:]
         return carry
 
-    lax.fori_loop(0, (NB + 1) // 2, columns, 0, unroll=7)
+    lax.fori_loop(0, (NB + 1) // 2, columns, 0, unroll=14)
 
     for k in range(4):
         for half in range(2):
@@ -74,7 +88,7 @@
                 ]
         return carry
 
-    lax.fori_loop(0, NB, rows_pass, 0, unroll=9)
+    lax.fori_loop(0, NB, rows_pass, 0, unroll=27)
 
     def gram(group, total):
         base = pl.multiple_of(group * 8 * SLAB, 8 * SLAB)
@@ -136,11 +150,19 @@
         counts[pl.ds(at, 8), :] = seen
         return carry
 
-    lax.fori_loop(0, PIX // 8, residual, 0, unroll=4)
+    lax.fori_loop(0, PIX // 8, residual, 0, unroll=8)
 
     def block(k):
+        side = pl.ds(HALF * (k % 2), HALF)
         return jnp.concatenate(
-            [counts[ROWS * k:ROWS * k + ROWS, :], plane[ROWS * k + 6:ROWS * k + 6 + 88, :]], 0
+            [
+                plane[16 + 118 * (k // 2):16 + 118 * (k // 2) + HALF + 16, side],
+                jnp.concatenate(
+                    [counts[ROWS * k:ROWS * k + ROWS, :HALF], counts[ROWS * k:ROWS * k + ROWS, HALF:],
+                     jnp.zeros((16, HALF), F32)], 0
+                ),
+            ],
+            1,
         ).astype(BF16)
 
     for k in range(4):
@@ -151,70 +173,91 @@
             theirs_ref[0], theirs_ref[1] = block(k ^ 1), block(k ^ 3)
 
 
-def fit(place, sky, images, masks, row_taps, col_taps):
+def fit(place, skies, images, masks, row_taps, col_taps):
     vmem = pl.BlockSpec(memory_space=pltpu.VMEM)
     return pl.pallas_call(
         fit_kernel,
-        out_shape=[jax.ShapeDtypeStruct((2, 152, PIX), BF16)] * 2,
-        in_specs=[pl.BlockSpec(memory_space=pltpu.SMEM), pl.BlockSpec(memory_space=pl.ANY)] + [vmem] * 4,
+        out_shape=[jax.ShapeDtypeStruct((2, HALF + 16, PIX), BF16)] * 2,
+        in_specs=[pl.BlockSpec(memory_space=pltpu.SMEM), *[pl.BlockSpec(memory_space=pl.ANY)] * 5] + [vmem] * 4,
         out_specs=[vmem] * 2,
         scratch_shapes=[
-            pltpu.VMEM((4, 80, 384), BF16),
+            pltpu.VMEM((HALF, 384), BF16),
+            pltpu.VMEM((2, ROWS, 384), BF16),
+            pltpu.VMEM((2, 16, 384), BF16),
             pltpu.VMEM((288, 384), BF16),
             pltpu.VMEM((14, 256, 256), BF16),
             pltpu.VMEM((28, 128, 256), BF16),
             pltpu.VMEM((28, 288, 256), BF16),
-            pltpu.VMEM((2, PITCH * SLAB, 128), F32),
+            pltpu.VMEM((2, PITCH * (SLAB + 1), 128), F32),
             pltpu.VMEM((PIX * SLAB, 256), BF16),
             pltpu.VMEM((320, PIX), F32),
             pltpu.VMEM((PIX, PIX), F32),
-            pltpu.SemaphoreType.DMA(()),
+            pltpu.SemaphoreType.DMA((5,)),
         ],
         compiler_params=pltpu.CompilerParams(vmem_limit_bytes=48 * 1024 * 1024),
         name="fit",
-    )(place, sky, images, masks, row_taps, col_taps)
-
-
-def filter_kernel(sky_ref, coverage_ref, row_taps_ref, col_taps_ref, out_ref):
-    col_band = toeplitz_rows(col_taps_ref[...], 256)[:, :128]
-    row_band = toeplitz_rows(row_taps_ref[...], ROWS)[:, :88]
-    halves = [
-        jnp.dot(sky_ref[:, half * 128:half * 128 + 256], col_band, precision=lax.Precision.HIGHEST,
-                preferred_element_type=F32)
-        for half in range(2)
-    ]
-    column_pass = jnp.concatenate(halves, 1)
-    summed = jnp.dot(row_band, column_pass, precision=lax.Precision.HIGHEST, preferred_element_type=F32)
-    out_ref[...] = summed / jnp.maximum(coverage_ref[...], 1.0)
-
-
-def filter_rows(sky, coverage, row_taps, col_taps):
+    )(place, *skies, images, masks, row_taps, col_taps)
+
+
+def filter_kernel(
+    place_ref, near_ref, far_ref, beside_ref, edge_ref, edge_too_ref, row_taps_ref, col_taps_ref,
+    keep_ref, give_ref, seen_ref,
+):
+    on_left, on_top = place_ref[0] % 2 == 0, place_ref[0] < 2
+    far = far_ref[...].astype(F32)
+    total = near_ref[...] + far[:, :PIX]
+    seen = jnp.maximum(total[:HALF, HALF:], 1.0)
+    seen_ref[...] = jnp.concatenate([seen[:ROWS], seen[ROWS:]], 1)
+    main = total[:HALF + HW, :HALF]
+    beside = beside_ref[0] + far[:HALF + HW, PIX:PIX + HW]
+    edge = edge_ref[...] + edge_too_ref[...]
+    edge = jnp.where(on_left, jnp.concatenate([edge[:, HALF:], edge[:, :HALF]], 1), edge)
+    core = jnp.where(on_left, jnp.concatenate([beside, main], 1), jnp.concatenate([main, beside], 1))
+    sky = jnp.where(on_top, jnp.concatenate([edge, core], 0), jnp.concatenate([core, edge], 0))
+    sky = jnp.concatenate([sky, jnp.zeros((4, HALF + HW), F32)], 0)
+    sky = jnp.concatenate([sky, jnp.zeros((HALF + 24, 6), F32)], 1)
+    taps = jnp.where(on_left, col_taps_ref[...], pltpu.roll(col_taps_ref[...], HALF + HW, 1))
+    col_band = toeplitz_rows(taps, HALF + 16)
+    row_band = toeplitz_rows(row_taps_ref[...], HALF)[:, :HALF + 24]
+    column_pass = jnp.dot(sky, col_band, precision=lax.Precision.HIGHEST, preferred_element_type=F32)
+    lane = lax.broadcasted_iota(jnp.int32, column_pass.shape, 1)
+    reached = jnp.logical_and(lane >= jnp.where(on_left, 0, HALF - HW), lane < jnp.where(on_left, HALF + HW, PIX))
+    column_pass = jnp.where(reached, column_pass, 0.0)
+    part = jnp.dot(row_band, column_pass, precision=lax.Precision.HIGHEST, preferred_element_type=F32)
+    keep_ref[...] = jnp.where(on_left, part[:ROWS], part[ROWS:])
+    give_ref[...] = jnp.where(on_left, part[ROWS:], part[:ROWS])
+
+
+def filter_half(place, *operands):
     vmem = pl.BlockSpec(memory_space=pltpu.VMEM)
     return pl.pallas_call(
         filter_kernel,
-        out_shape=jax.ShapeDtypeStruct((ROWS, PIX), F32),
-        in_specs=[vmem] * 4,
-        out_specs=vmem,
+        out_shape=[jax.ShapeDtypeStruct((ROWS, PIX), F32)] * 3,
+        in_specs=[pl.BlockSpec(memory_space=pltpu.SMEM)] + [vmem] * len(operands),
+        out_specs=[vmem] * 3,
         compiler_params=pltpu.CompilerParams(vmem_limit_bytes=32 * 1024 * 1024),
         name="filter",
-    )(sky, coverage, row_taps, col_taps)
+    )(place, *operands)
 
 
 def routes(tiles, exps):
-    east, west, border, core, half = [], [], [], [], []
+    core, chip, beside, border, border_too, edge = [], [], [], [], [], []
     for t in range(tiles):
+        row, col = t // GW, t % GW
         for e in range(exps):
-            core.append((t * exps + e, t * exps + (e ^ 1)))
-            half.append((t * exps + e, t * exps + (e ^ 2)))
-            if t % GW < GW - 1:
-                east.append((t * exps + e, (t + 1) * exps + e))
-            if t % GW > 0:
-                west.append((t * exps + e, (t - 1) * exps + e))
-        if t >= GW:
-            border.append((t * exps, (t - GW) * exps + exps - 1))
-        if t < tiles - GW:
-            border.append((t * exps + exps - 1, (t + GW) * exps))
-    return east, west, border, core, half
+            here = t * exps + e
+            core.append((here, t * exps + (e ^ 1)))
+            chip.append((here, t * exps + (e ^ 2)))
+            col_to = col + (1 if e % 2 else -1)
+            row_to = row + (1 if e // 2 else -1)
+            in_cols, in_rows = 0 <= col_to < GW, 0 <= row_to < tiles // GW
+            if in_cols:
+                beside.append((here, (row * GW + col_to) * exps + (e ^ 1)))
+            if in_rows:
+                border.append((here, (row_to * GW + col) * exps + (e ^ 2)))
+                border_too.append((t * exps + (e ^ 2), (row_to * GW + col) * exps + (e ^ 2)))
+                edge.append((here, (row_to * GW + col) * exps + 2 * (e % 2) + 1 - e // 2))
+    return core, chip, beside, border, border_too, edge
 
 
 def send(values, route):
@@ -230,40 +273,42 @@
 
 
 def shards(template, exposures, masks, basis_rows, basis_cols, psf_row, psf_col):
-    east, west, border, core, half = routes(lax.axis_size("tile"), lax.axis_size("exp"))
+    core, chip, beside, border, border_too, edge = routes(lax.axis_size("tile"), lax.axis_size("exp"))
     place = lax.axis_index("exp")
-    first_place, last_place = place == 0, place == lax.axis_size("exp") - 1
+    on_left, on_top = place % 2 == 0, place < 2
 
     own = template[0]
-    from_west = send(own, east)[:, -HW:]
-    from_east = send(own, west)[:, :HW]
-    wide = lax.optimization_barrier(jnp.concatenate([from_west, own, from_east], 1))
-    from_border = send(jnp.where(first_place, wide[:HW], wide[-HW:]), border)
-    block = jnp.pad(jnp.concatenate([wide, from_border], 0), ((0, 6), (0, 108)))
-    sky = lax.all_gather(block, "exp", axis=0)
+    other = send(own, core)
+    strip = jnp.concatenate(
+        [jnp.where(on_left, own[:, :HW], other[:, -HW:]), jnp.where(on_left, other[:, :HW], own[:, -HW:])], 0
+    )
+    strip = send(strip, beside)
+    half = jnp.where(on_left, jnp.concatenate([own, other], 0), jnp.concatenate([other, own], 0))
+    strip_core = send(strip, core)
+    west, east = jnp.where(on_left, strip, strip_core), jnp.where(on_left, strip_core, strip)
+    wide = lax.optimization_barrier(jnp.pad(jnp.concatenate([west, half, east], 1), ((0, 0), (0, 108))))
+    far = send(jnp.where(on_left, wide[:ROWS], wide[ROWS:]), chip)
+    rows = send(jnp.where(on_top, wide[:16], wide[-16:]), edge)
+    far_core, rows_core = send(far, core), send(rows, core)
 
     rounded = lambda taps: taps.astype(BF16).astype(F32)
     mine, theirs = fit(
-        place[None], sky, exposures[0], masks[0], rising(rounded(basis_rows)), falling(rounded(basis_cols))
+        place[None], (wide, far, far_core, rows, rows_core), exposures[0], masks[0],
+        rising(rounded(basis_rows)), falling(rounded(basis_cols)),
     )
     pair = mine.astype(F32) + send(theirs, core).astype(F32)
-    whole = pair[0] + send(pair[1].astype(BF16), half).astype(F32)
-    coverage, summed = whole[:ROWS], whole[ROWS:ROWS + 84]
-    from_west = send(summed[:, -HW:], east)
-    from_east = send(summed[:, :HW], west)
-    wide = jnp.concatenate([from_west, summed, from_east], 1)
-    from_border = send(jnp.where(first_place, wide[HW:2 * HW], wide[ROWS:ROWS + HW]), border)
-    zeros = jnp.zeros_like(from_border)
-    wide = jnp.concatenate(
-        [
-            jnp.where(first_place, from_border, wide[:HW]),
-            wide[HW:HW + ROWS],
-            jnp.where(last_place, from_border, wide[HW + ROWS:]),
-        ],
-        0,
-    )
-    wide = jnp.pad(wide, ((0, 4), (0, 108)))
-    return filter_rows(wide, coverage, rising(psf_row[None])[:1], falling(psf_col[None])[:1])[None]
+    main = pair[:, :HALF + HW, :HALF]
+    strip = send(jnp.where(on_left, main[:, :, :HW], main[:, :, -HW:]), beside)
+    far = jnp.concatenate([pair[1], jnp.pad(strip[1], ((0, 6), (0, HALF - HW)))], 1).astype(BF16)
+    ends = jnp.concatenate([main, strip], 2)
+    far, ends = lax.optimization_barrier((far, ends))
+    far = send(far, chip)
+    rows = send(jnp.where(on_top, ends[0, :HW], ends[0, -HW:]), border)
+    rows_too = send(jnp.where(on_top, ends[1, -HW:], ends[1, :HW]), border_too)
+    keep, give, seen = filter_half(
+        place[None], pair[0], far, strip, rows, rows_too, rising(psf_row[None])[:1], falling(psf_col[None])[:1]
+    )
+    return ((keep + send(give, core)) / seen)[None]
 
 
 def solution(mesh):

time: 79.3 us -> 70.1 us (0.88)
  the two profiles are of different devices: /device:TPU:30 before, /device:TPU:31 now
where the time goes in v4:
time: 70.1 us; the launch traced here: 69.7 us
  starting transfers between devices  28.2 us (40%)
  waiting for transfers between devices  21.5 us (31%)
  Pallas kernels  14.9 us (21%)
  other arithmetic  2.66 us (4%)
  local copies, waits for them, and re-layouts  2.3 us (3%)
    ppermute x13, starting transfers between devices, send(): return lax.ppermute(values, ('tile', 'exp'), route)  28.2 us
    ppermute x13, waiting for transfers between devices, send(): return lax.ppermute(values, ('tile', 'exp'), route)  21.5 us
    pallas_call x1, Pallas kernels, fit(): pl.pallas_call(fit_kernel, out_shape=[jax.ShapeDtypeStruct((2, HALF + 16,...  14 us
    unnamed x10, local copies, waits for them, and re-layouts  1.71 us
    convert_element_type x2, other arithmetic, shards(): rounded = lambda taps: taps.astype(BF16).astype(F32)  1.42 us
  transfers between devices with their start and end apart: 13, of which 9 were waited for; matrix products, arithmetic and copies ran while one was open for 3% of the time, Pallas kernels for 0%

profile of v4, /device:TPU:31, one launch (start us, length us, event | category | flops | bytes accessed | tf_op | source)
XLA Modules:
  0.0 69.7 jit_solution(71889894163179982)
XLA Ops:
  0.0 0.7 collective-permute-start
  0.7 0.7 %convert_element_type.27 = bf16[27,21]{0,1:T(8,128)(2,1)S(1)} convert(f32[27,21]{0,1:T(8,128)} %param.10) | non-fusion elementwise | flops 567 | bytes 3402 | tf_op jit(solution)/shard_map/convert_element_type | solution.py:294
  1.5 0.7 %convert_element_type.28 = bf16[27,21]{0,1:T(8,128)(2,1)S(1)} convert(f32[27,21]{0,1:T(8,128)} %param.11) | non-fusion elementwise | flops 567 | bytes 3402 | tf_op jit(solution)/shard_map/convert_element_type | solution.py:294
  2.6 3.2 %collective-permute-start.1 = (bf16[128,10]{1,0:T(8,128)(2,1)S(1)}, bf16[128,10]{1,0:T(8,128)(2,1)S(1)}, u32[]{:S(2)}, u32[]{:S(2)}) collective-permute-start(bf16[128,10]{1,0:T(8,128)(2,1)S(1)} %pad_maximum_fusion.1), channel_id=1, source_target_pairs={{1,4},{3,6},{4,1},{5,8},{6,3},{7,10},{8,5},{9,12},{10,7},{11,14},{... | collective-permute-start | bytes 7688 | tf_op jit(solution)/shard_map/ppermute | solution.py:264
  5.8 4.1 %collective-permute-done.1 = bf16[128,10]{1,0:T(8,128)(2,1)S(1)} collective-permute-done((bf16[128,10]{1,0:T(8,128)(2,1)S(1)}, bf16[128,10]{1,0:T(8,128)(2,1)S(1)}, u32[]{:S(2)}, u32[]{:S(2)}) %collective-permute-start.1) | collective-permute-done | bytes 2592 | tf_op jit(solution)/shard_map/ppermute | solution.py:264
  10.0 1.2 %collective-permute-done.2 = bf16[128,10]{1,0:T(8,128)(2,1)S(1)} collective-permute-done((bf16[128,10]{1,0:T(8,128)(2,1)S(1)}, bf16[128,10]{1,0:T(8,128)(2,1)S(1)}, u32[]{:S(2)}, u32[]{:S(2)}) %collective-permute-start.2) | collective-permute-done | bytes 2592 | tf_op jit(solution)/shard_map/ppermute | solution.py:264
  11.3 7.0 %collective-permute-start.3 = (bf16[64,384]{1,0:T(8,128)(2,1)S(1)}, bf16[64,384]{1,0:T(8,128)(2,1)S(1)}, u32[]{:S(2)}, u32[]{:S(2)}) collective-permute-start(bf16[64,384]{1,0:T(8,128)(2,1)S(1)} %slice_select_fusion.1), channel_id=1, source_target_pairs={{0,2},{1,3},{2,0},{3,1},{4,6},{5,7},{6,4},{7,5},{8,10},{9,11},{10,... | collective-permute-start | bytes 147464 | tf_op jit(solution)/shard_map/ppermute | solution.py:264
  18.3 2.1 %collective-permute-start.5 = (bf16[16,384]{1,0:T(8,128)(2,1)S(1)}, bf16[16,384]{1,0:T(8,128)(2,1)S(1)}, u32[]{:S(2)}, u32[]{:S(2)}) collective-permute-start(bf16[16,384]{1,0:T(8,128)(2,1)S(1)} %slice_select_fusion.4), channel_id=1, source_target_pairs={{2,32},{3,34},{6,36},{7,38},{10,40},{11,42},{14,44},{15,46},{18,48... | collective-permute-start | bytes 36872 | tf_op jit(solution)/shard_map/ppermute | solution.py:264
  20.5 3.8 %collective-permute-done.5.edge_any = bf16[16,384]{1,0:T(8,128)(2,1)S(1)} collective-permute-done((bf16[16,384]{1,0:T(8,128)(2,1)S(1)}, bf16[16,384]{1,0:T(8,128)(2,1)S(1)}, u32[]{:S(2)}, u32[]{:S(2)}) %collective-permute-start.5) | collective-permute-done | bytes 12320 | tf_op jit(solution)/shard_map/ppermute | solution.py:264
  24.3 3.1 %collective-permute-start.6 = (bf16[16,384]{1,0:T(8,128)(2,1)S(1)}, bf16[16,384]{1,0:T(8,128)(2,1)S(1)}, u32[]{:S(2)}, u32[]{:S(2)}) collective-permute-start(bf16[16,384]{1,0:T(8,128)(2,1)S(1)} %collective-permute-done.5.edge_any), channel_id=1, source_target_pairs={{0,1},{1,0},{2,3},{3,2},{4,5},{5,4},{6,7},{7,6},{8,9},{9,8},{10,11... | collective-permute-start | bytes 36872 | tf_op jit(solution)/shard_map/ppermute | solution.py:264
  27.6 0.8 %collective-permute-done.6.edge_core_any = bf16[16,384]{1,0:T(8,128)(2,1)S(1)} collective-permute-done((bf16[16,384]{1,0:T(8,128)(2,1)S(1)}, bf16[16,384]{1,0:T(8,128)(2,1)S(1)}, u32[]{:S(2)}, u32[]{:S(2)}) %collective-permute-start.6) | collective-permute-done | bytes 12320 | tf_op jit(solution)/shard_map/ppermute | solution.py:264
  28.3 0.4 collective-permute-done.4.far_core_any
  28.7 1.0 %copy-done.1 = bf16[1,4,256,256]{3,2,1,0:T(8,128)(2,1)S(1)} copy-done((bf16[1,4,256,256]{3,2,1,0:T(8,128)(2,1)S(1)}, bf16[1,4,256,256]{3,2,1,0:T(8,128)(2,1)}, u32[]{:S(2)}) %copy-start.1) | copy-done | bytes 524312
  29.8 14.0 %fit.1 = (bf16[2,144,256]{2,1,0:T(8,128)(2,1)S(1)}, bf16[2,144,256]{2,1,0:T(8,128)(2,1)S(1)}) custom-call(s32[1]{0:T(128)} %bitcast.place_ref, bf16[128,384]{1,0:T(8,128)(2,1)S(1)} %fusion.6.own_any, bf16[64,384]{1,0:T(8,128)(2,1)S(1)} %collective-permute-done.3.far_any, bf16[64,384]{1,0:T(8,128)(2,1)S(1)} %collective-permute-done.4.far_core_any, ...), custom_call_target="tpu_custom_call" | custom-call | tf_op jit(solution)/shard_map/fit/pallas_call | solution.py:178
  44.0 0.7 copy-done.3
  44.8 0.5 collective-permute-done.7
  45.4 2.3 %collective-permute-start.8 = (f32[2,138,10]{2,1,0:T(8,128)S(1)}, f32[2,138,10]{2,1,0:T(8,128)S(1)}, u32[]{:S(2)}, u32[]{:S(2)}) collective-permute-start(f32[2,138,10]{2,1,0:T(8,128)S(1)} %slice_select_fusion), channel_id=1, source_target_pairs={{1,4},{3,6},{4,1},{5,8},{6,3},{7,10},{8,5},{9,12},{10,7},{11,14},{... | collective-permute-start | bytes 33128 | tf_op jit(solution)/shard_map/ppermute | solution.py:264
  47.7 8.1 %collective-permute-done.8.beside_ref = f32[2,138,10]{2,1,0:T(8,128)S(1)} collective-permute-done((f32[2,138,10]{2,1,0:T(8,128)S(1)}, f32[2,138,10]{2,1,0:T(8,128)S(1)}, u32[]{:S(2)}, u32[]{:S(2)}) %collective-permute-start.8) | collective-permute-done | bytes 11072 | tf_op jit(solution)/shard_map/ppermute | solution.py:264
  56.0 4.0 %collective-permute-start.10 = (f32[10,138]{1,0:T(8,128)S(1)}, f32[10,138]{1,0:T(8,128)S(1)}, u32[]{:S(2)}, u32[]{:S(2)}) collective-permute-start(f32[10,138]{1,0:T(8,128)S(1)} %get-tuple-element.20), channel_id=1, source_target_pairs={{2,32},{3,33},{6,36},{7,37},{10,40},{11,41},{14,44},{15,45},{18,48... | collective-permute-start | bytes 16568 | tf_op jit(solution)/shard_map/ppermute | solution.py:264
  60.0 5.4 %collective-permute-start.11 = (f32[10,138]{1,0:T(8,128)S(1)}, f32[10,138]{1,0:T(8,128)S(1)}, u32[]{:S(2)}, u32[]{:S(2)}) collective-permute-start(f32[10,138]{1,0:T(8,128)S(1)} %get-tuple-element.19), channel_id=1, source_target_pairs={{0,32},{1,33},{4,36},{5,37},{8,40},{9,41},{12,44},{13,45},{16,48},... | collective-permute-start | bytes 16568 | tf_op jit(solution)/shard_map/ppermute | solution.py:264
  65.5 1.3 %collective-permute-done.11.edge_too_ref = f32[10,138]{1,0:T(8,128)S(1)} collective-permute-done((f32[10,138]{1,0:T(8,128)S(1)}, f32[10,138]{1,0:T(8,128)S(1)}, u32[]{:S(2)}, u32[]{:S(2)}) %collective-permute-start.11) | collective-permute-done | bytes 5552 | tf_op jit(solution)/shard_map/ppermute | solution.py:264
  66.8 0.9 %filter.1 = (f32[64,256]{1,0:T(8,128)S(1)}, f32[64,256]{1,0:T(8,128)S(1)}, f32[64,256]{1,0:T(8,128)S(1)}) custom-call(s32[1]{0:T(128)} %bitcast.place_ref, f32[144,256]{1,0:T(8,128)S(1)} %slice_bitcast_fusion.near_ref, bf16[144,384]{1,0:T(8,128)(2,1)S(1)} %collective-permute-done.9.far_ref, f32[2,138,10]{2,1,0:T(8,128)S(1)} %collective-permute-done.8.beside_ref, ...), custom_call_target="tpu_custom_call" | custom-call | tf_op jit(solution)/shard_map/filter/pallas_call | solution.py:233
  67.8 1.2 %collective-permute-done.12 = f32[64,256]{1,0:T(8,128)S(1)} collective-permute-done((f32[64,256]{1,0:T(8,128)S(1)}, f32[64,256]{1,0:T(8,128)S(1)}, u32[]{:S(2)}, u32[]{:S(2)}) %collective-permute-start.12) | collective-permute-done | bytes 65568 | tf_op jit(solution)/shard_map/ppermute | solution.py:264
  69.1 0.6 divide_bitcast_fusion
  (44 shorter events, 1.6 us)
Async XLA Ops:
  0.0 2.5 %copy-start.2 = (bf16[1,64,256]{2,1,0:T(8,128)(2,1)S(1)}, bf16[1,64,256]{2,1,0:T(8,128)(2,1)}, u32[]{:S(2)}) copy-start(bf16[1,64,256]{2,1,0:T(8,128)(2,1)} %param.7) | copy-start | bytes 98308
  0.0 28.7 %copy-start = (s32[1,4,256,256]{3,2,1,0:T(8,128)S(1)}, s32[1,4,256,256]{3,2,1,0:T(8,128)}, u32[]{:S(2)}) copy-start(s32[1,4,256,256]{3,2,1,0:T(8,128)} %param.9) | copy-start | bytes 3145732
  0.0 2.5 %collective-permute-start = (bf16[64,256]{1,0:T(8,128)(2,1)}, bf16[64,256]{1,0:T(8,128)(2,1)S(1)}, u32[]{:S(2)}, u32[]{:S(2)}) collective-permute-start(bf16[64,256]{1,0:T(8,128)(2,1)} %bitcast.20), channel_id=1, source_target_pairs={{0,1},{1,0},{2,3},{3,2},{4,5},{5,4},{6,7},{7,6},{8,9},{9,8},{10,11... | collective-permute-start | bytes 98312 | tf_op jit(solution)/shard_map/ppermute | solution.py:264
  2.6 7.3 %collective-permute-start.1 = (bf16[128,10]{1,0:T(8,128)(2,1)S(1)}, bf16[128,10]{1,0:T(8,128)(2,1)S(1)}, u32[]{:S(2)}, u32[]{:S(2)}) collective-permute-start(bf16[128,10]{1,0:T(8,128)(2,1)S(1)} %pad_maximum_fusion.1), channel_id=1, source_target_pairs={{1,4},{3,6},{4,1},{5,8},{6,3},{7,10},{8,5},{9,12},{10,7},{11,14},{... | collective-permute-start | bytes 7688 | tf_op jit(solution)/shard_map/ppermute | solution.py:264
  9.9 1.2 %collective-permute-start.2 = (bf16[128,10]{1,0:T(8,128)(2,1)S(1)}, bf16[128,10]{1,0:T(8,128)(2,1)S(1)}, u32[]{:S(2)}, u32[]{:S(2)}) collective-permute-start(bf16[128,10]{1,0:T(8,128)(2,1)S(1)} %collective-permute-done.1), channel_id=1, source_target_pairs={{0,1},{1,0},{2,3},{3,2},{4,5},{5,4},{6,7},{7,6},{8,9},{9,8},{10,11... | collective-permute-start | bytes 7688 | tf_op jit(solution)/shard_map/ppermute | solution.py:264
  11.3 16.2 %collective-permute-start.3 = (bf16[64,384]{1,0:T(8,128)(2,1)S(1)}, bf16[64,384]{1,0:T(8,128)(2,1)S(1)}, u32[]{:S(2)}, u32[]{:S(2)}) collective-permute-start(bf16[64,384]{1,0:T(8,128)(2,1)S(1)} %slice_select_fusion.1), channel_id=1, source_target_pairs={{0,2},{1,3},{2,0},{3,1},{4,6},{5,7},{6,4},{7,5},{8,10},{9,11},{10,... | collective-permute-start | bytes 147464 | tf_op jit(solution)/shard_map/ppermute | solution.py:264
  18.3 2.1 %copy-start.4 = (f32[21]{0:T(128)S(1)}, f32[21]{0:T(128)}, u32[]{:S(2)}) copy-start(f32[21]{0:T(128)} %param.13) | copy-start | bytes 256
  18.3 6.0 %collective-permute-start.5 = (bf16[16,384]{1,0:T(8,128)(2,1)S(1)}, bf16[16,384]{1,0:T(8,128)(2,1)S(1)}, u32[]{:S(2)}, u32[]{:S(2)}) collective-permute-start(bf16[16,384]{1,0:T(8,128)(2,1)S(1)} %slice_select_fusion.4), channel_id=1, source_target_pairs={{2,32},{3,34},{6,36},{7,38},{10,40},{11,42},{14,44},{15,46},{18,48... | collective-permute-start | bytes 36872 | tf_op jit(solution)/shard_map/ppermute | solution.py:264
  24.3 4.0 %collective-permute-start.6 = (bf16[16,384]{1,0:T(8,128)(2,1)S(1)}, bf16[16,384]{1,0:T(8,128)(2,1)S(1)}, u32[]{:S(2)}, u32[]{:S(2)}) collective-permute-start(bf16[16,384]{1,0:T(8,128)(2,1)S(1)} %collective-permute-done.5.edge_any), channel_id=1, source_target_pairs={{0,1},{1,0},{2,3},{3,2},{4,5},{5,4},{6,7},{7,6},{8,9},{9,8},{10,11... | collective-permute-start | bytes 36872 | tf_op jit(solution)/shard_map/ppermute | solution.py:264
  27.5 1.2 %collective-permute-start.4 = (bf16[64,384]{1,0:T(8,128)(2,1)S(1)}, bf16[64,384]{1,0:T(8,128)(2,1)S(1)}, u32[]{:S(2)}, u32[]{:S(2)}) collective-permute-start(bf16[64,384]{1,0:T(8,128)(2,1)S(1)} %collective-permute-done.3.far_any), channel_id=1, source_target_pairs={{0,1},{1,0},{2,3},{3,2},{4,5},{5,4},{6,7},{7,6},{8,9},{9,8},{10,11... | collective-permute-start | bytes 147464 | tf_op jit(solution)/shard_map/ppermute | solution.py:264
  28.7 1.0 %copy-start.1 = (bf16[1,4,256,256]{3,2,1,0:T(8,128)(2,1)S(1)}, bf16[1,4,256,256]{3,2,1,0:T(8,128)(2,1)}, u32[]{:S(2)}) copy-start(bf16[1,4,256,256]{3,2,1,0:T(8,128)(2,1)} %param.8) | copy-start | bytes 1572868
  43.8 1.5 %collective-permute-start.7 = (bf16[2,144,256]{2,1,0:T(8,128)(2,1)S(1)}, bf16[2,144,256]{2,1,0:T(8,128)(2,1)S(1)}, u32[]{:S(2)}, u32[]{:S(2)}) collective-permute-start(bf16[2,144,256]{2,1,0:T(8,128)(2,1)S(1)} %get-tuple-element.13), channel_id=1, source_target_pairs={{0,1},{1,0},{2,3},{3,2},{4,5},{5,4},{6,7},{7,6},{8,9},{9,8},{10,11... | collective-permute-start | bytes 442376 | tf_op jit(solution)/shard_map/ppermute | solution.py:264
  44.0 0.7 copy-start.3
  45.4 10.4 %collective-permute-start.8 = (f32[2,138,10]{2,1,0:T(8,128)S(1)}, f32[2,138,10]{2,1,0:T(8,128)S(1)}, u32[]{:S(2)}, u32[]{:S(2)}) collective-permute-start(f32[2,138,10]{2,1,0:T(8,128)S(1)} %slice_select_fusion), channel_id=1, source_target_pairs={{1,4},{3,6},{4,1},{5,8},{6,3},{7,10},{8,5},{9,12},{10,7},{11,14},{... | collective-permute-start | bytes 33128 | tf_op jit(solution)/shard_map/ppermute | solution.py:264
  55.9 11.0 %collective-permute-start.9 = (bf16[144,384]{1,0:T(8,128)(2,1)S(1)}, bf16[144,384]{1,0:T(8,128)(2,1)S(1)}, u32[]{:S(2)}, u32[]{:S(2)}) collective-permute-start(bf16[144,384]{1,0:T(8,128)(2,1)S(1)} %fusion.4), channel_id=1, source_target_pairs={{0,2},{1,3},{2,0},{3,1},{4,6},{5,7},{6,4},{7,5},{8,10},{9,11},{10,... | collective-permute-start | bytes 331784 | tf_op jit(solution)/shard_map/ppermute | solution.py:264
  56.0 9.5 %collective-permute-start.10 = (f32[10,138]{1,0:T(8,128)S(1)}, f32[10,138]{1,0:T(8,128)S(1)}, u32[]{:S(2)}, u32[]{:S(2)}) collective-permute-start(f32[10,138]{1,0:T(8,128)S(1)} %get-tuple-element.20), channel_id=1, source_target_pairs={{2,32},{3,33},{6,36},{7,37},{10,40},{11,41},{14,44},{15,45},{18,48... | collective-permute-start | bytes 16568 | tf_op jit(solution)/shard_map/ppermute | solution.py:264
  60.0 6.8 %collective-permute-start.11 = (f32[10,138]{1,0:T(8,128)S(1)}, f32[10,138]{1,0:T(8,128)S(1)}, u32[]{:S(2)}, u32[]{:S(2)}) collective-permute-start(f32[10,138]{1,0:T(8,128)S(1)} %get-tuple-element.19), channel_id=1, source_target_pairs={{0,32},{1,33},{4,36},{5,37},{8,40},{9,41},{12,44},{13,45},{16,48},... | collective-permute-start | bytes 16568 | tf_op jit(solution)/shard_map/ppermute | solution.py:264
  67.7 1.3 %collective-permute-start.12 = (f32[64,256]{1,0:T(8,128)S(1)}, f32[64,256]{1,0:T(8,128)S(1)}, u32[]{:S(2)}, u32[]{:S(2)}) collective-permute-start(f32[64,256]{1,0:T(8,128)S(1)} %get-tuple-element.17), channel_id=1, source_target_pairs={{0,1},{1,0},{2,3},{3,2},{4,5},{5,4},{6,7},{7,6},{8,9},{9,8},{10,11... | collective-permute-start | bytes 196616 | tf_op jit(solution)/shard_map/ppermute | solution.py:264

commit v5 on v4

--- a/solution.py
+++ b/solution.py
@@ -23,7 +23,7 @@
 
 
 def fit_kernel(
-    place_ref, own_any, far_any, far_core_any, edge_any, edge_core_any, images_ref, masks_ref, row_taps_ref, col_taps_ref, mine_ref, theirs_ref,
+    place_ref, own_any, far_any, far_core_any, edge_any, edge_core_any, planes_ref, row_taps_ref, col_taps_ref, mine_ref, theirs_ref,
     own_ref, far_ref, edge_ref, window, col_band, row_band, first, slab_wide, slab, plane, counts, sky_sem,
 ):
     arriving = [
@@ -70,7 +70,7 @@
 
     for k in range(4):
         for half in range(2):
-            slab_wide[half, pl.ds((NB + k) * PITCH, PIX), :] = images_ref[
+            slab_wide[half, pl.ds((NB + k) * PITCH, PIX), :] = planes_ref[
                 k, :, half * 128:half * 128 + 128
             ].astype(F32)
     for half in range(2):
@@ -90,10 +90,11 @@
 
     lax.fori_loop(0, NB, rows_pass, 0, unroll=27)
 
-    def gram(group, total):
+    def gram(group, totals):
+        totals = list(totals)
         base = pl.multiple_of(group * 8 * SLAB, 8 * SLAB)
         at = pl.multiple_of(group * 8, 8)
-        valid = [masks_ref[k, pl.ds(at, 8), :].astype(F32) for k in range(4)]
+        valid = [planes_ref[4 + k, pl.ds(at, 8), :].astype(F32) for k in range(4)]
         for i in range(8):
             here = pl.ds(base + i * SLAB, SLAB)
             there = pl.ds(group * 8 + i, SLAB, stride=PITCH)
@@ -103,26 +104,49 @@
             masked = jnp.concatenate(
                 [low * jnp.broadcast_to(v[i:i + 1].astype(BF16), low.shape) for v in valid], 0
             )
-            total = total + lax.dot_general(
-                low, masked, (((1,), (1,)), ((), ())), preferred_element_type=F32
+            totals[i % 2] = totals[i % 2] + lax.dot_general(
+                masked, low, (((1,), (1,)), ((), ())), preferred_element_type=F32
             )
-        return total
-
-    matrix = lax.fori_loop(0, PIX // 8, gram, jnp.zeros((SLAB, 4 * SLAB), F32), unroll=2)
+        return tuple(totals)
+
+    matrix = sum(lax.fori_loop(0, PIX // 8, gram, (jnp.zeros((4 * SLAB, SLAB), F32),) * 2, unroll=8)).T
 
     lane = lax.broadcasted_iota(jnp.int32, (SLAB, 4 * SLAB), 1)
     row = lax.broadcasted_iota(jnp.int32, (SLAB, 4 * SLAB), 0)
     of_exposure = lane // SLAB
     of_basis = lane % SLAB
-    for k in range(NB):
-        column = jnp.take_along_axis(matrix, of_exposure * SLAB + k, axis=1)
-        pivot_row = matrix[k:k + 1, :]
-        pivot = column[k:k + 1, :]
-        scaled = jnp.where(of_basis[:1] == k, 0.0, pivot_row / pivot)
-        matrix = matrix - column * scaled
-    top = jnp.sum(jnp.where(row == NB + of_exposure, matrix, 0.0), axis=0, keepdims=True)
-    bottom = jnp.sum(jnp.where(row == of_basis, matrix, 0.0), axis=0, keepdims=True)
-    solved = jnp.broadcast_to(top / bottom, (8, 4 * SLAB))
+    def column_of(k):
+        return jnp.take_along_axis(matrix, of_exposure * SLAB + k, axis=1)
+
+    for k in range(0, NB - 1, 2):
+        here, there = column_of(k), column_of(k + 1)
+        inverse = 1.0 / here[k:k + 1]
+        ratio = here[k + 1:k + 2] * inverse
+        rest = there[k + 1:k + 2] - ratio * there[k:k + 1]
+        scaled_there = (matrix[k + 1:k + 2] - ratio * matrix[k:k + 1]) / rest
+        scaled_here = (matrix[k:k + 1] - there[k:k + 1] * scaled_there) * inverse
+        outside = of_basis[:1] // 2 != k // 2
+        matrix = matrix - (
+            here * jnp.where(outside, scaled_here, 0.0) + there * jnp.where(outside, scaled_there, 0.0)
+        )
+    here = column_of(NB - 1)
+    matrix = matrix - here * jnp.where(of_basis[:1] == NB - 1, 0.0, matrix[NB - 1:NB] / here[NB - 1:NB])
+
+    def picked(rows):
+        return jnp.sum(jnp.where(row == rows, matrix, 0.0), axis=0, keepdims=True)
+
+    right, own, mate = picked(NB + of_exposure), picked(of_basis), picked(of_basis ^ 1)
+    beside = lane[:8] ^ 1
+    right_b, own_b, mate_b = [
+        jnp.take_along_axis(jnp.broadcast_to(v, (8, 4 * SLAB)), beside, axis=1)[:1] for v in (right, own, mate)
+    ]
+    alone = of_basis[:1] == NB - 1
+    mate, mate_b = jnp.where(alone, 0.0, mate), jnp.where(alone, 0.0, mate_b)
+    right_b, own_b = jnp.where(alone, 0.0, right_b), jnp.where(alone, 1.0, own_b)
+    ratio = mate_b / own
+    other = (right_b - ratio * right) / (own_b - ratio * mate)
+    solved = (right - mate * other) / own
+    solved = jnp.broadcast_to(solved, (8, 4 * SLAB))
     lane8 = lax.broadcasted_iota(jnp.int32, (8, 4 * SLAB), 1)
     row8 = lax.broadcasted_iota(jnp.int32, (8, 4 * SLAB), 0)
     weights = []
@@ -143,7 +167,7 @@
         total = jnp.zeros((8, PIX), F32)
         seen = jnp.zeros((8, PIX), F32)
         for k in range(4):
-            valid = masks_ref[k, pl.ds(at, 8), :].astype(F32)
+            valid = planes_ref[4 + k, pl.ds(at, 8), :].astype(F32)
             seen = seen + valid
             total = total + (valid * left[8 * k:8 * k + 8]).astype(BF16).astype(F32)
         plane[pl.ds(pl.multiple_of(group * 8 + 16, 8), 8), :] = total
@@ -173,12 +197,12 @@
             theirs_ref[0], theirs_ref[1] = block(k ^ 1), block(k ^ 3)
 
 
-def fit(place, skies, images, masks, row_taps, col_taps):
+def fit(place, skies, planes, row_taps, col_taps):
     vmem = pl.BlockSpec(memory_space=pltpu.VMEM)
     return pl.pallas_call(
         fit_kernel,
         out_shape=[jax.ShapeDtypeStruct((2, HALF + 16, PIX), BF16)] * 2,
-        in_specs=[pl.BlockSpec(memory_space=pltpu.SMEM), *[pl.BlockSpec(memory_space=pl.ANY)] * 5] + [vmem] * 4,
+        in_specs=[pl.BlockSpec(memory_space=pltpu.SMEM), *[pl.BlockSpec(memory_space=pl.ANY)] * 5] + [vmem] * 3,
         out_specs=[vmem] * 2,
         scratch_shapes=[
             pltpu.VMEM((HALF, 384), BF16),
@@ -196,7 +220,7 @@
         ],
         compiler_params=pltpu.CompilerParams(vmem_limit_bytes=48 * 1024 * 1024),
         name="fit",
-    )(place, *skies, images, masks, row_taps, col_taps)
+    )(place, *skies, planes, row_taps, col_taps)
 
 
 def filter_kernel(
@@ -283,22 +307,25 @@
         [jnp.where(on_left, own[:, :HW], other[:, -HW:]), jnp.where(on_left, other[:, :HW], own[:, -HW:])], 0
     )
     strip = send(strip, beside)
+    strip, basis_rows, basis_cols = lax.optimization_barrier((strip, basis_rows, basis_cols))
     half = jnp.where(on_left, jnp.concatenate([own, other], 0), jnp.concatenate([other, own], 0))
     strip_core = send(strip, core)
     west, east = jnp.where(on_left, strip, strip_core), jnp.where(on_left, strip_core, strip)
     wide = lax.optimization_barrier(jnp.pad(jnp.concatenate([west, half, east], 1), ((0, 0), (0, 108))))
+    wide, exposures, masks = lax.optimization_barrier((wide, exposures, masks))
+    planes = jnp.concatenate([exposures[0], masks[0].astype(BF16)], 0)
     far = send(jnp.where(on_left, wide[:ROWS], wide[ROWS:]), chip)
     rows = send(jnp.where(on_top, wide[:16], wide[-16:]), edge)
     far_core, rows_core = send(far, core), send(rows, core)
 
     rounded = lambda taps: taps.astype(BF16).astype(F32)
     mine, theirs = fit(
-        place[None], (wide, far, far_core, rows, rows_core), exposures[0], masks[0],
+        place[None], (wide, far, far_core, rows, rows_core), planes,
         rising(rounded(basis_rows)), falling(rounded(basis_cols)),
     )
     pair = mine.astype(F32) + send(theirs, core).astype(F32)
     main = pair[:, :HALF + HW, :HALF]
-    strip = send(jnp.where(on_left, main[:, :, :HW], main[:, :, -HW:]), beside)
+    strip = send(jnp.where(on_left, main[:, :, :HW], main[:, :, -HW:]).astype(BF16), beside).astype(F32)
     far = jnp.concatenate([pair[1], jnp.pad(strip[1], ((0, 6), (0, HALF - HW)))], 1).astype(BF16)
     ends = jnp.concatenate([main, strip], 2)
     far, ends = lax.optimization_barrier((far, ends))

time: 70.1 us -> 66.3 us (0.946)
  Pallas kernels: 14.9 us -> 12.5 us
  waiting for transfers between devices: 21.5 us -> 19.1 us
    pallas_call x1, Pallas kernels: 14 us -> 11.6 us  [fit(): pl.pallas_call(fit_kernel, out_shape=[jax.ShapeDtypeStruct((2, HALF + 16,...]
    ppermute x13, waiting for transfers between devices: 21.5 us -> 19.1 us  [send(): return lax.ppermute(values, ('tile', 'exp'), route)]
    unnamed x10 -> x8, local copies, waits for them, and re-layouts: 1.71 us -> 0.67 us
  transfers between devices with their start and end apart: 13 -> 13, of which waited for: 9 -> 10; matrix products, arithmetic and copies ran while one was open for 3% -> 3% of each run, Pallas kernels for 0% -> 0%
where the time goes in v5:
time: 66.3 us; the launch traced here: 65.3 us
  starting transfers between devices  28.7 us (43%)
  waiting for transfers between devices  19.1 us (29%)
  Pallas kernels  12.5 us (19%)
  other arithmetic  2.83 us (4%)
  local copies, waits for them, and re-layouts  1.91 us (3%)
    ppermute x13, starting transfers between devices, send(): return lax.ppermute(values, ('tile', 'exp'), route)  28.7 us
    ppermute x13, waiting for transfers between devices, send(): return lax.ppermute(values, ('tile', 'exp'), route)  19.1 us
    pallas_call x1, Pallas kernels, fit(): pl.pallas_call(fit_kernel, out_shape=[jax.ShapeDtypeStruct((2, HALF + 16,...  11.6 us
    convert_element_type x2, other arithmetic, shards(): rounded = lambda taps: taps.astype(BF16).astype(F32)  1.42 us
  transfers between devices with their start and end apart: 13, of which 10 were waited for; matrix products, arithmetic and copies ran while one was open for 3% of the time, Pallas kernels for 0%

profile of v5, /device:TPU:31, one launch (start us, length us, event | category | flops | bytes accessed | tf_op | source)
XLA Modules:
  0.0 65.3 jit_solution(12696995518905520688)
XLA Ops:
  0.0 0.7 %collective-permute-start = (bf16[64,256]{1,0:T(8,128)(2,1)}, bf16[64,256]{1,0:T(8,128)(2,1)S(1)}, u32[]{:S(2)}, u32[]{:S(2)}) collective-permute-start(bf16[64,256]{1,0:T(8,128)(2,1)} %bitcast.20), channel_id=1, source_target_pairs={{0,1},{1,0},{2,3},{3,2},{4,5},{5,4},{6,7},{7,6},{8,9},{9,8},{10,11... | collective-permute-start | bytes 98312 | tf_op jit(solution)/shard_map/ppermute | solution.py:288
  0.7 0.7 %reverse.3 = f32[21]{0:T(128)S(1)} reverse(f32[21]{0:T(128)} %param.13), dimensions={0} | reverse | bytes 168 | tf_op jit(solution)/shard_map/reverse
  1.9 3.4 %collective-permute-start.1 = (bf16[128,10]{1,0:T(8,128)(2,1)S(1)}, bf16[128,10]{1,0:T(8,128)(2,1)S(1)}, u32[]{:S(2)}, u32[]{:S(2)}) collective-permute-start(bf16[128,10]{1,0:T(8,128)(2,1)S(1)} %pad_maximum_fusion.2), channel_id=1, source_target_pairs={{1,4},{3,6},{4,1},{5,8},{6,3},{7,10},{8,5},{9,12},{10,7},{11,14},{... | collective-permute-start | bytes 7688 | tf_op jit(solution)/shard_map/ppermute | solution.py:288
  5.3 3.9 %collective-permute-done.1 = bf16[128,10]{1,0:T(8,128)(2,1)S(1)} collective-permute-done((bf16[128,10]{1,0:T(8,128)(2,1)S(1)}, bf16[128,10]{1,0:T(8,128)(2,1)S(1)}, u32[]{:S(2)}, u32[]{:S(2)}) %collective-permute-start.1) | collective-permute-done | bytes 2592 | tf_op jit(solution)/shard_map/ppermute | solution.py:288
  9.2 0.7 %convert_element_type.42 = bf16[27,21]{0,1:T(8,128)(2,1)S(1)} convert(f32[27,21]{0,1:T(8,128)} %param.11) | non-fusion elementwise | flops 567 | bytes 3402 | tf_op jit(solution)/shard_map/convert_element_type | solution.py:321
  10.2 0.7 %convert_element_type.41 = bf16[27,21]{0,1:T(8,128)(2,1)S(1)} convert(f32[27,21]{0,1:T(8,128)} %param.10) | non-fusion elementwise | flops 567 | bytes 3402 | tf_op jit(solution)/shard_map/convert_element_type | solution.py:321
  11.1 0.3 collective-permute-done.2
  11.6 7.0 %collective-permute-start.3 = (bf16[64,384]{1,0:T(8,128)(2,1)S(1)}, bf16[64,384]{1,0:T(8,128)(2,1)S(1)}, u32[]{:S(2)}, u32[]{:S(2)}) collective-permute-start(bf16[64,384]{1,0:T(8,128)(2,1)S(1)} %slice_select_fusion.1), channel_id=1, source_target_pairs={{0,2},{1,3},{2,0},{3,1},{4,6},{5,7},{6,4},{7,5},{8,10},{9,11},{10,... | collective-permute-start | bytes 147464 | tf_op jit(solution)/shard_map/ppermute | solution.py:288
  18.6 2.1 %collective-permute-start.5 = (bf16[16,384]{1,0:T(8,128)(2,1)S(1)}, bf16[16,384]{1,0:T(8,128)(2,1)S(1)}, u32[]{:S(2)}, u32[]{:S(2)}) collective-permute-start(bf16[16,384]{1,0:T(8,128)(2,1)S(1)} %slice_select_fusion.4), channel_id=1, source_target_pairs={{2,32},{3,34},{6,36},{7,38},{10,40},{11,42},{14,44},{15,46},{18,48... | collective-permute-start | bytes 36872 | tf_op jit(solution)/shard_map/ppermute | solution.py:288
  20.7 3.9 %collective-permute-done.5.edge_any = bf16[16,384]{1,0:T(8,128)(2,1)S(1)} collective-permute-done((bf16[16,384]{1,0:T(8,128)(2,1)S(1)}, bf16[16,384]{1,0:T(8,128)(2,1)S(1)}, u32[]{:S(2)}, u32[]{:S(2)}) %collective-permute-start.5) | collective-permute-done | bytes 12320 | tf_op jit(solution)/shard_map/ppermute | solution.py:288
  24.6 3.2 %collective-permute-start.6 = (bf16[16,384]{1,0:T(8,128)(2,1)S(1)}, bf16[16,384]{1,0:T(8,128)(2,1)S(1)}, u32[]{:S(2)}, u32[]{:S(2)}) collective-permute-start(bf16[16,384]{1,0:T(8,128)(2,1)S(1)} %collective-permute-done.5.edge_any), channel_id=1, source_target_pairs={{0,1},{1,0},{2,3},{3,2},{4,5},{5,4},{6,7},{7,6},{8,9},{9,8},{10,11... | collective-permute-start | bytes 36872 | tf_op jit(solution)/shard_map/ppermute | solution.py:288
  27.9 0.7 %collective-permute-done.6.edge_core_any = bf16[16,384]{1,0:T(8,128)(2,1)S(1)} collective-permute-done((bf16[16,384]{1,0:T(8,128)(2,1)S(1)}, bf16[16,384]{1,0:T(8,128)(2,1)S(1)}, u32[]{:S(2)}, u32[]{:S(2)}) %collective-permute-start.6) | collective-permute-done | bytes 12320 | tf_op jit(solution)/shard_map/ppermute | solution.py:288
  28.6 0.4 collective-permute-done.4.far_core_any
  29.0 11.6 %fit.1 = (bf16[2,144,256]{2,1,0:T(8,128)(2,1)S(1)}, bf16[2,144,256]{2,1,0:T(8,128)(2,1)S(1)}) custom-call(s32[1]{0:T(128)} %bitcast.place_ref, bf16[128,384]{1,0:T(8,128)(2,1)S(1)} %fusion.7.own_any, bf16[64,384]{1,0:T(8,128)(2,1)S(1)} %collective-permute-done.3.far_any, bf16[64,384]{1,0:T(8,128)(2,1)S(1)} %collective-permute-done.4.far_core_any, ...), custom_call_target="tpu_custom_call" | custom-call | tf_op jit(solution)/shard_map/fit/pallas_call | solution.py:202
  40.9 0.7 copy-done.3
  41.7 0.5 collective-permute-done.7
  42.3 2.5 %collective-permute-start.8 = (bf16[2,138,10]{2,1,0:T(8,128)(2,1)S(1)}, bf16[2,138,10]{2,1,0:T(8,128)(2,1)S(1)}, u32[]{:S(2)}, u32[]{:S(2)}) collective-permute-start(bf16[2,138,10]{2,1,0:T(8,128)(2,1)S(1)} %fusion.4), channel_id=1, source_target_pairs={{1,4},{3,6},{4,1},{5,8},{6,3},{7,10},{8,5},{9,12},{10,7},{11,14},{... | collective-permute-start | bytes 16568 | tf_op jit(solution)/shard_map/ppermute | solution.py:288
  44.8 6.9 %collective-permute-done.8 = bf16[2,138,10]{2,1,0:T(8,128)(2,1)S(1)} collective-permute-done((bf16[2,138,10]{2,1,0:T(8,128)(2,1)S(1)}, bf16[2,138,10]{2,1,0:T(8,128)(2,1)S(1)}, u32[]{:S(2)}, u32[]{:S(2)}) %collective-permute-start.8) | collective-permute-done | bytes 5552 | tf_op jit(solution)/shard_map/ppermute | solution.py:288
  51.9 4.3 %collective-permute-start.10 = (f32[10,138]{1,0:T(8,128)S(1)}, f32[10,138]{1,0:T(8,128)S(1)}, u32[]{:S(2)}, u32[]{:S(2)}) collective-permute-start(f32[10,138]{1,0:T(8,128)S(1)} %get-tuple-element.32), channel_id=1, source_target_pairs={{2,32},{3,33},{6,36},{7,37},{10,40},{11,41},{14,44},{15,45},{18,48... | collective-permute-start | bytes 16568 | tf_op jit(solution)/shard_map/ppermute | solution.py:288
  56.2 5.2 %collective-permute-start.11 = (f32[10,138]{1,0:T(8,128)S(1)}, f32[10,138]{1,0:T(8,128)S(1)}, u32[]{:S(2)}, u32[]{:S(2)}) collective-permute-start(f32[10,138]{1,0:T(8,128)S(1)} %get-tuple-element.31), channel_id=1, source_target_pairs={{0,32},{1,33},{4,36},{5,37},{8,40},{9,41},{12,44},{13,45},{16,48},... | collective-permute-start | bytes 16568 | tf_op jit(solution)/shard_map/ppermute | solution.py:288
  61.4 1.1 %collective-permute-done.11.edge_too_ref = f32[10,138]{1,0:T(8,128)S(1)} collective-permute-done((f32[10,138]{1,0:T(8,128)S(1)}, f32[10,138]{1,0:T(8,128)S(1)}, u32[]{:S(2)}, u32[]{:S(2)}) %collective-permute-start.11) | collective-permute-done | bytes 5552 | tf_op jit(solution)/shard_map/ppermute | solution.py:288
  62.4 0.9 %filter.1 = (f32[64,256]{1,0:T(8,128)S(1)}, f32[64,256]{1,0:T(8,128)S(1)}, f32[64,256]{1,0:T(8,128)S(1)}) custom-call(s32[1]{0:T(128)} %bitcast.place_ref, f32[144,256]{1,0:T(8,128)S(1)} %slice_bitcast_fusion.near_ref, bf16[144,384]{1,0:T(8,128)(2,1)S(1)} %collective-permute-done.9.far_ref, f32[2,138,10]{2,1,0:T(8,128)S(1)} %convert_element_type.47.beside_ref, ...), custom_call_target="tpu_custom_call" | custom-call | tf_op jit(solution)/shard_map/filter/pallas_call | solution.py:257
  63.4 1.2 %collective-permute-done.12 = f32[64,256]{1,0:T(8,128)S(1)} collective-permute-done((f32[64,256]{1,0:T(8,128)S(1)}, f32[64,256]{1,0:T(8,128)S(1)}, u32[]{:S(2)}, u32[]{:S(2)}) %collective-permute-start.12) | collective-permute-done | bytes 65568 | tf_op jit(solution)/shard_map/ppermute | solution.py:288
  64.7 0.6 divide_bitcast_fusion
  (45 shorter events, 2.0 us)
Async XLA Ops:
  0.0 1.8 %copy-start.2 = (bf16[1,64,256]{2,1,0:T(8,128)(2,1)S(1)}, bf16[1,64,256]{2,1,0:T(8,128)(2,1)}, u32[]{:S(2)}) copy-start(bf16[1,64,256]{2,1,0:T(8,128)(2,1)} %param.7) | copy-start | bytes 98308
  0.0 20.6 %copy-start = (s32[1,4,256,256]{3,2,1,0:T(8,128)S(1)}, s32[1,4,256,256]{3,2,1,0:T(8,128)}, u32[]{:S(2)}) copy-start(s32[1,4,256,256]{3,2,1,0:T(8,128)} %param.9) | copy-start | bytes 3145732
  0.0 1.7 %collective-permute-start = (bf16[64,256]{1,0:T(8,128)(2,1)}, bf16[64,256]{1,0:T(8,128)(2,1)S(1)}, u32[]{:S(2)}, u32[]{:S(2)}) collective-permute-start(bf16[64,256]{1,0:T(8,128)(2,1)} %bitcast.20), channel_id=1, source_target_pairs={{0,1},{1,0},{2,3},{3,2},{4,5},{5,4},{6,7},{7,6},{8,9},{9,8},{10,11... | collective-permute-start | bytes 98312 | tf_op jit(solution)/shard_map/ppermute | solution.py:288
  1.9 7.3 %collective-permute-start.1 = (bf16[128,10]{1,0:T(8,128)(2,1)S(1)}, bf16[128,10]{1,0:T(8,128)(2,1)S(1)}, u32[]{:S(2)}, u32[]{:S(2)}) collective-permute-start(bf16[128,10]{1,0:T(8,128)(2,1)S(1)} %pad_maximum_fusion.2), channel_id=1, source_target_pairs={{1,4},{3,6},{4,1},{5,8},{6,3},{7,10},{8,5},{9,12},{10,7},{11,14},{... | collective-permute-start | bytes 7688 | tf_op jit(solution)/shard_map/ppermute | solution.py:288
  10.2 1.3 %collective-permute-start.2 = (bf16[128,10]{1,0:T(8,128)(2,1)S(1)}, bf16[128,10]{1,0:T(8,128)(2,1)S(1)}, u32[]{:S(2)}, u32[]{:S(2)}) collective-permute-start(bf16[128,10]{1,0:T(8,128)(2,1)S(1)} %collective-permute-done.1), channel_id=1, source_target_pairs={{0,1},{1,0},{2,3},{3,2},{4,5},{5,4},{6,7},{7,6},{8,9},{9,8},{10,11... | collective-permute-start | bytes 7688 | tf_op jit(solution)/shard_map/ppermute | solution.py:288
  11.6 16.2 %collective-permute-start.3 = (bf16[64,384]{1,0:T(8,128)(2,1)S(1)}, bf16[64,384]{1,0:T(8,128)(2,1)S(1)}, u32[]{:S(2)}, u32[]{:S(2)}) collective-permute-start(bf16[64,384]{1,0:T(8,128)(2,1)S(1)} %slice_select_fusion.1), channel_id=1, source_target_pairs={{0,2},{1,3},{2,0},{3,1},{4,6},{5,7},{6,4},{7,5},{8,10},{9,11},{10,... | collective-permute-start | bytes 147464 | tf_op jit(solution)/shard_map/ppermute | solution.py:288
  18.6 9.2 %copy-start.1 = (bf16[1,4,256,256]{3,2,1,0:T(8,128)(2,1)S(1)}, bf16[1,4,256,256]{3,2,1,0:T(8,128)(2,1)}, u32[]{:S(2)}) copy-start(bf16[1,4,256,256]{3,2,1,0:T(8,128)(2,1)} %param.8) | copy-start | bytes 1572868
  18.6 6.0 %collective-permute-start.5 = (bf16[16,384]{1,0:T(8,128)(2,1)S(1)}, bf16[16,384]{1,0:T(8,128)(2,1)S(1)}, u32[]{:S(2)}, u32[]{:S(2)}) collective-permute-start(bf16[16,384]{1,0:T(8,128)(2,1)S(1)} %slice_select_fusion.4), channel_id=1, source_target_pairs={{2,32},{3,34},{6,36},{7,38},{10,40},{11,42},{14,44},{15,46},{18,48... | collective-permute-start | bytes 36872 | tf_op jit(solution)/shard_map/ppermute | solution.py:288
  24.6 4.0 %collective-permute-start.6 = (bf16[16,384]{1,0:T(8,128)(2,1)S(1)}, bf16[16,384]{1,0:T(8,128)(2,1)S(1)}, u32[]{:S(2)}, u32[]{:S(2)}) collective-permute-start(bf16[16,384]{1,0:T(8,128)(2,1)S(1)} %collective-permute-done.5.edge_any), channel_id=1, source_target_pairs={{0,1},{1,0},{2,3},{3,2},{4,5},{5,4},{6,7},{7,6},{8,9},{9,8},{10,11... | collective-permute-start | bytes 36872 | tf_op jit(solution)/shard_map/ppermute | solution.py:288
  27.8 1.2 %collective-permute-start.4 = (bf16[64,384]{1,0:T(8,128)(2,1)S(1)}, bf16[64,384]{1,0:T(8,128)(2,1)S(1)}, u32[]{:S(2)}, u32[]{:S(2)}) collective-permute-start(bf16[64,384]{1,0:T(8,128)(2,1)S(1)} %collective-permute-done.3.far_any), channel_id=1, source_target_pairs={{0,1},{1,0},{2,3},{3,2},{4,5},{5,4},{6,7},{7,6},{8,9},{9,8},{10,11... | collective-permute-start | bytes 147464 | tf_op jit(solution)/shard_map/ppermute | solution.py:288
  40.7 1.5 %collective-permute-start.7 = (bf16[2,144,256]{2,1,0:T(8,128)(2,1)S(1)}, bf16[2,144,256]{2,1,0:T(8,128)(2,1)S(1)}, u32[]{:S(2)}, u32[]{:S(2)}) collective-permute-start(bf16[2,144,256]{2,1,0:T(8,128)(2,1)S(1)} %get-tuple-element.25), channel_id=1, source_target_pairs={{0,1},{1,0},{2,3},{3,2},{4,5},{5,4},{6,7},{7,6},{8,9},{9,8},{10,11... | collective-permute-start | bytes 442376 | tf_op jit(solution)/shard_map/ppermute | solution.py:288
  40.9 0.7 %copy-start.3 = (f32[21]{0:T(128)S(1)}, f32[21]{0:T(128)}, u32[]{:S(2)}) copy-start(f32[21]{0:T(128)} %param.12) | copy-start | bytes 256
  42.3 9.4 %collective-permute-start.8 = (bf16[2,138,10]{2,1,0:T(8,128)(2,1)S(1)}, bf16[2,138,10]{2,1,0:T(8,128)(2,1)S(1)}, u32[]{:S(2)}, u32[]{:S(2)}) collective-permute-start(bf16[2,138,10]{2,1,0:T(8,128)(2,1)S(1)} %fusion.4), channel_id=1, source_target_pairs={{1,4},{3,6},{4,1},{5,8},{6,3},{7,10},{8,5},{9,12},{10,7},{11,14},{... | collective-permute-start | bytes 16568 | tf_op jit(solution)/shard_map/ppermute | solution.py:288
  51.8 10.7 %collective-permute-start.9 = (bf16[144,384]{1,0:T(8,128)(2,1)S(1)}, bf16[144,384]{1,0:T(8,128)(2,1)S(1)}, u32[]{:S(2)}, u32[]{:S(2)}) collective-permute-start(bf16[144,384]{1,0:T(8,128)(2,1)S(1)} %fusion.5), channel_id=1, source_target_pairs={{0,2},{1,3},{2,0},{3,1},{4,6},{5,7},{6,4},{7,5},{8,10},{9,11},{10,... | collective-permute-start | bytes 331784 | tf_op jit(solution)/shard_map/ppermute | solution.py:288
  51.9 9.5 %collective-permute-start.10 = (f32[10,138]{1,0:T(8,128)S(1)}, f32[10,138]{1,0:T(8,128)S(1)}, u32[]{:S(2)}, u32[]{:S(2)}) collective-permute-start(f32[10,138]{1,0:T(8,128)S(1)} %get-tuple-element.32), channel_id=1, source_target_pairs={{2,32},{3,33},{6,36},{7,37},{10,40},{11,41},{14,44},{15,45},{18,48... | collective-permute-start | bytes 16568 | tf_op jit(solution)/shard_map/ppermute | solution.py:288
  56.2 6.3 %collective-permute-start.11 = (f32[10,138]{1,0:T(8,128)S(1)}, f32[10,138]{1,0:T(8,128)S(1)}, u32[]{:S(2)}, u32[]{:S(2)}) collective-permute-start(f32[10,138]{1,0:T(8,128)S(1)} %get-tuple-element.31), channel_id=1, source_target_pairs={{0,32},{1,33},{4,36},{5,37},{8,40},{9,41},{12,44},{13,45},{16,48},... | collective-permute-start | bytes 16568 | tf_op jit(solution)/shard_map/ppermute | solution.py:288
  63.3 1.3 %collective-permute-start.12 = (f32[64,256]{1,0:T(8,128)S(1)}, f32[64,256]{1,0:T(8,128)S(1)}, u32[]{:S(2)}, u32[]{:S(2)}) collective-permute-start(f32[64,256]{1,0:T(8,128)S(1)} %get-tuple-element.29), channel_id=1, source_target_pairs={{0,1},{1,0},{2,3},{3,2},{4,5},{5,4},{6,7},{7,6},{8,9},{9,8},{10,11... | collective-permute-start | bytes 196616 | tf_op jit(solution)/shard_map/ppermute | solution.py:288

commit v6 on v5

--- a/solution.py
+++ b/solution.py
@@ -23,8 +23,8 @@
 
 
 def fit_kernel(
-    place_ref, own_any, far_any, far_core_any, edge_any, edge_core_any, planes_ref, row_taps_ref, col_taps_ref, mine_ref, theirs_ref,
-    own_ref, far_ref, edge_ref, window, col_band, row_band, first, slab_wide, slab, plane, counts, sky_sem,
+    place_ref, own_any, far_any, far_core_any, edge_any, edge_core_any, planes_ref, row_basis_ref, col_basis_ref, mine_ref, theirs_ref,
+    row_taps_ref, col_taps_ref, own_ref, far_ref, edge_ref, window, col_band, row_band, first, slab_wide, slab, plane, counts, sky_sem,
 ):
     arriving = [
         pltpu.make_async_copy(source, target, sky_sem.at[k])
@@ -35,6 +35,19 @@
     ]
     for copy in arriving:
         copy.start()
+
+    def along_lanes(ref):
+        taps = jnp.concatenate([ref[...], jnp.zeros((128 - KW, NB), F32)], 0)
+        return jnp.transpose(jnp.concatenate([taps, jnp.zeros((128, 128 - NB), F32)], 1))[:SLAB]
+
+    row_taps = along_lanes(row_basis_ref)
+    row_taps_ref[...] = jnp.concatenate([row_taps, jnp.zeros_like(row_taps)], 1)
+    col_taps = along_lanes(col_basis_ref)
+    tap = lax.broadcasted_iota(jnp.int32, (SLAB, 128), 1)
+    back = jnp.take_along_axis(col_taps, jnp.minimum(128 - tap, 127), axis=1)
+    col_taps_ref[...] = jnp.concatenate(
+        [jnp.where(tap == 0, col_taps, 0.0), jnp.where(tap > 128 - KW, back, 0.0)], 1
+    )
 
     def build(b, carry):
         col = toeplitz_rows(col_taps_ref[pl.ds(b, 1), :], 256)
@@ -109,7 +122,7 @@
             )
         return tuple(totals)
 
-    matrix = sum(lax.fori_loop(0, PIX // 8, gram, (jnp.zeros((4 * SLAB, SLAB), F32),) * 2, unroll=8)).T
+    matrix = sum(lax.fori_loop(0, PIX // 8, gram, (jnp.zeros((4 * SLAB, SLAB), F32),) * 2, unroll=16)).T
 
     lane = lax.broadcasted_iota(jnp.int32, (SLAB, 4 * SLAB), 1)
     row = lax.broadcasted_iota(jnp.int32, (SLAB, 4 * SLAB), 0)
@@ -174,7 +187,7 @@
         counts[pl.ds(at, 8), :] = seen
         return carry
 
-    lax.fori_loop(0, PIX // 8, residual, 0, unroll=8)
+    lax.fori_loop(0, PIX // 8, residual, 0, unroll=16)
 
     def block(k):
         side = pl.ds(HALF * (k % 2), HALF)
@@ -205,6 +218,8 @@
         in_specs=[pl.BlockSpec(memory_space=pltpu.SMEM), *[pl.BlockSpec(memory_space=pl.ANY)] * 5] + [vmem] * 3,
         out_specs=[vmem] * 2,
         scratch_shapes=[
+            pltpu.VMEM((SLAB, 256), F32),
+            pltpu.VMEM((SLAB, 256), F32),
             pltpu.VMEM((HALF, 384), BF16),
             pltpu.VMEM((2, ROWS, 384), BF16),
             pltpu.VMEM((2, 16, 384), BF16),
@@ -307,7 +322,6 @@
         [jnp.where(on_left, own[:, :HW], other[:, -HW:]), jnp.where(on_left, other[:, :HW], own[:, -HW:])], 0
     )
     strip = send(strip, beside)
-    strip, basis_rows, basis_cols = lax.optimization_barrier((strip, basis_rows, basis_cols))
     half = jnp.where(on_left, jnp.concatenate([own, other], 0), jnp.concatenate([other, own], 0))
     strip_core = send(strip, core)
     west, east = jnp.where(on_left, strip, strip_core), jnp.where(on_left, strip_core, strip)
@@ -318,10 +332,9 @@
     rows = send(jnp.where(on_top, wide[:16], wide[-16:]), edge)
     far_core, rows_core = send(far, core), send(rows, core)
 
-    rounded = lambda taps: taps.astype(BF16).astype(F32)
     mine, theirs = fit(
         place[None], (wide, far, far_core, rows, rows_core), planes,
-        rising(rounded(basis_rows)), falling(rounded(basis_cols)),
+        basis_rows.T, basis_cols.T,
     )
     pair = mine.astype(F32) + send(theirs, core).astype(F32)
     main = pair[:, :HALF + HW, :HALF]

time: 66.3 us -> 64.8 us (0.977)
    convert_element_type x2 -> x0, other arithmetic: 1.42 us -> none  [shards(): rounded = lambda taps: taps.astype(BF16).astype(F32)]
    convert_element_type x1, other arithmetic: 0.08 us -> 1.31 us  [shards(): planes = jnp.concatenate([exposures[0], masks[0].astype(BF16)], 0)]
  transfers between devices with their start and end apart: 13 -> 13, of which waited for: 10 -> 10; matrix products, arithmetic and copies ran while one was open for 3% -> 4% of each run, Pallas kernels for 0% -> 0%
where the time goes in v6:
time: 64.8 us; the launch traced here: 63.9 us
  starting transfers between devices  28.7 us (44%)
  waiting for transfers between devices  18.7 us (29%)
  Pallas kernels  12.2 us (19%)
  other arithmetic  2.54 us (4%)
  local copies, waits for them, and re-layouts  1.54 us (2%)
    ppermute x13, starting transfers between devices, send(): return lax.ppermute(values, ('tile', 'exp'), route)  28.7 us
    ppermute x13, waiting for transfers between devices, send(): return lax.ppermute(values, ('tile', 'exp'), route)  18.7 us
    pallas_call x1, Pallas kernels, fit(): pl.pallas_call(fit_kernel, out_shape=[jax.ShapeDtypeStruct((2, HALF + 16,...  11.3 us
    convert_element_type x1, other arithmetic, shards(): planes = jnp.concatenate([exposures[0], masks[0].astype(BF16)], 0)  1.31 us
  transfers between devices with their start and end apart: 13, of which 10 were waited for; matrix products, arithmetic and copies ran while one was open for 4% of the time, Pallas kernels for 0%

profile of v6, /device:TPU:31, one launch (start us, length us, event | category | flops | bytes accessed | tf_op | source)
XLA Modules:
  0.0 63.9 jit_solution(16661753125973829449)
XLA Ops:
  0.0 0.7 %collective-permute-start = (bf16[64,256]{1,0:T(8,128)(2,1)}, bf16[64,256]{1,0:T(8,128)(2,1)S(1)}, u32[]{:S(2)}, u32[]{:S(2)}) collective-permute-start(bf16[64,256]{1,0:T(8,128)(2,1)} %bitcast.24), channel_id=1, source_target_pairs={{0,1},{1,0},{2,3},{3,2},{4,5},{5,4},{6,7},{7,6},{8,9},{9,8},{10,11... | collective-permute-start | bytes 98312 | tf_op jit(solution)/shard_map/ppermute | solution.py:303
  0.7 0.7 %reverse.3 = f32[21]{0:T(128)S(1)} reverse(f32[21]{0:T(128)} %param.13), dimensions={0} | reverse | bytes 168 | tf_op jit(solution)/shard_map/reverse
  1.4 0.3 collective-permute-done
  1.8 3.4 %collective-permute-start.1 = (bf16[128,10]{1,0:T(8,128)(2,1)S(1)}, bf16[128,10]{1,0:T(8,128)(2,1)S(1)}, u32[]{:S(2)}, u32[]{:S(2)}) collective-permute-start(bf16[128,10]{1,0:T(8,128)(2,1)S(1)} %pad_maximum_fusion.2), channel_id=1, source_target_pairs={{1,4},{3,6},{4,1},{5,8},{6,3},{7,10},{8,5},{9,12},{10,7},{11,14},{... | collective-permute-start | bytes 7688 | tf_op jit(solution)/shard_map/ppermute | solution.py:303
  5.4 3.8 %collective-permute-done.1 = bf16[128,10]{1,0:T(8,128)(2,1)S(1)} collective-permute-done((bf16[128,10]{1,0:T(8,128)(2,1)S(1)}, bf16[128,10]{1,0:T(8,128)(2,1)S(1)}, u32[]{:S(2)}, u32[]{:S(2)}) %collective-permute-start.1) | collective-permute-done | bytes 2592 | tf_op jit(solution)/shard_map/ppermute | solution.py:303
  9.2 1.2 %collective-permute-done.2 = bf16[128,10]{1,0:T(8,128)(2,1)S(1)} collective-permute-done((bf16[128,10]{1,0:T(8,128)(2,1)S(1)}, bf16[128,10]{1,0:T(8,128)(2,1)S(1)}, u32[]{:S(2)}, u32[]{:S(2)}) %collective-permute-start.2) | collective-permute-done | bytes 2592 | tf_op jit(solution)/shard_map/ppermute | solution.py:303
  10.5 7.0 %collective-permute-start.3 = (bf16[64,384]{1,0:T(8,128)(2,1)S(1)}, bf16[64,384]{1,0:T(8,128)(2,1)S(1)}, u32[]{:S(2)}, u32[]{:S(2)}) collective-permute-start(bf16[64,384]{1,0:T(8,128)(2,1)S(1)} %slice_select_fusion.1), channel_id=1, source_target_pairs={{0,2},{1,3},{2,0},{3,1},{4,6},{5,7},{6,4},{7,5},{8,10},{9,11},{10,... | collective-permute-start | bytes 147464 | tf_op jit(solution)/shard_map/ppermute | solution.py:303
  17.6 2.1 %collective-permute-start.5 = (bf16[16,384]{1,0:T(8,128)(2,1)S(1)}, bf16[16,384]{1,0:T(8,128)(2,1)S(1)}, u32[]{:S(2)}, u32[]{:S(2)}) collective-permute-start(bf16[16,384]{1,0:T(8,128)(2,1)S(1)} %slice_select_fusion.4), channel_id=1, source_target_pairs={{2,32},{3,34},{6,36},{7,38},{10,40},{11,42},{14,44},{15,46},{18,48... | collective-permute-start | bytes 36872 | tf_op jit(solution)/shard_map/ppermute | solution.py:303
  19.6 1.3 %convert_bitcast_fusion = bf16[4,256,256]{2,1,0:T(8,128)(2,1)S(1)} fusion(s32[1,4,256,256]{3,2,1,0:T(8,128)} %param.9), kind=kLoop, calls=%fused_computation.1 | loop fusion | flops 262144 | bytes 1572864 | tf_op jit(solution)/shard_map/convert_element_type | solution.py:330
  20.9 2.7 %collective-permute-done.5.edge_any = bf16[16,384]{1,0:T(8,128)(2,1)S(1)} collective-permute-done((bf16[16,384]{1,0:T(8,128)(2,1)S(1)}, bf16[16,384]{1,0:T(8,128)(2,1)S(1)}, u32[]{:S(2)}, u32[]{:S(2)}) %collective-permute-start.5) | collective-permute-done | bytes 12320 | tf_op jit(solution)/shard_map/ppermute | solution.py:303
  23.6 3.1 %collective-permute-start.6 = (bf16[16,384]{1,0:T(8,128)(2,1)S(1)}, bf16[16,384]{1,0:T(8,128)(2,1)S(1)}, u32[]{:S(2)}, u32[]{:S(2)}) collective-permute-start(bf16[16,384]{1,0:T(8,128)(2,1)S(1)} %collective-permute-done.5.edge_any), channel_id=1, source_target_pairs={{0,1},{1,0},{2,3},{3,2},{4,5},{5,4},{6,7},{7,6},{8,9},{9,8},{10,11... | collective-permute-start | bytes 36872 | tf_op jit(solution)/shard_map/ppermute | solution.py:303
  26.9 0.7 %collective-permute-done.6.edge_core_any = bf16[16,384]{1,0:T(8,128)(2,1)S(1)} collective-permute-done((bf16[16,384]{1,0:T(8,128)(2,1)S(1)}, bf16[16,384]{1,0:T(8,128)(2,1)S(1)}, u32[]{:S(2)}, u32[]{:S(2)}) %collective-permute-start.6) | collective-permute-done | bytes 12320 | tf_op jit(solution)/shard_map/ppermute | solution.py:303
  27.6 0.4 collective-permute-done.4.far_core_any
  28.0 11.3 %fit.1 = (bf16[2,144,256]{2,1,0:T(8,128)(2,1)S(1)}, bf16[2,144,256]{2,1,0:T(8,128)(2,1)S(1)}) custom-call(s32[1]{0:T(128)} %bitcast.place_ref, bf16[128,384]{1,0:T(8,128)(2,1)S(1)} %fusion.7.own_any, bf16[64,384]{1,0:T(8,128)(2,1)S(1)} %collective-permute-done.3.far_any, bf16[64,384]{1,0:T(8,128)(2,1)S(1)} %collective-permute-done.4.far_core_any, ...), custom_call_target="tpu_custom_call" | custom-call | tf_op jit(solution)/shard_map/fit/pallas_call | solution.py:215
  39.5 0.7 %copy-done.4 = f32[21]{0:T(128)S(1)} copy-done((f32[21]{0:T(128)S(1)}, f32[21]{0:T(128)}, u32[]{:S(2)}) %copy-start.4) | copy-done | bytes 108
  40.2 0.5 collective-permute-done.7
  40.8 2.5 %collective-permute-start.8 = (bf16[2,138,10]{2,1,0:T(8,128)(2,1)S(1)}, bf16[2,138,10]{2,1,0:T(8,128)(2,1)S(1)}, u32[]{:S(2)}, u32[]{:S(2)}) collective-permute-start(bf16[2,138,10]{2,1,0:T(8,128)(2,1)S(1)} %fusion.4), channel_id=1, source_target_pairs={{1,4},{3,6},{4,1},{5,8},{6,3},{7,10},{8,5},{9,12},{10,7},{11,14},{... | collective-permute-start | bytes 16568 | tf_op jit(solution)/shard_map/ppermute | solution.py:303
  43.4 6.9 %collective-permute-done.8 = bf16[2,138,10]{2,1,0:T(8,128)(2,1)S(1)} collective-permute-done((bf16[2,138,10]{2,1,0:T(8,128)(2,1)S(1)}, bf16[2,138,10]{2,1,0:T(8,128)(2,1)S(1)}, u32[]{:S(2)}, u32[]{:S(2)}) %collective-permute-start.8) | collective-permute-done | bytes 5552 | tf_op jit(solution)/shard_map/ppermute | solution.py:303
  50.5 4.2 %collective-permute-start.10 = (f32[10,138]{1,0:T(8,128)S(1)}, f32[10,138]{1,0:T(8,128)S(1)}, u32[]{:S(2)}, u32[]{:S(2)}) collective-permute-start(f32[10,138]{1,0:T(8,128)S(1)} %get-tuple-element.26), channel_id=1, source_target_pairs={{2,32},{3,33},{6,36},{7,37},{10,40},{11,41},{14,44},{15,45},{18,48... | collective-permute-start | bytes 16568 | tf_op jit(solution)/shard_map/ppermute | solution.py:303
  54.7 5.2 %collective-permute-start.11 = (f32[10,138]{1,0:T(8,128)S(1)}, f32[10,138]{1,0:T(8,128)S(1)}, u32[]{:S(2)}, u32[]{:S(2)}) collective-permute-start(f32[10,138]{1,0:T(8,128)S(1)} %get-tuple-element.25), channel_id=1, source_target_pairs={{0,32},{1,33},{4,36},{5,37},{8,40},{9,41},{12,44},{13,45},{16,48},... | collective-permute-start | bytes 16568 | tf_op jit(solution)/shard_map/ppermute | solution.py:303
  60.0 1.0 %collective-permute-done.11.edge_too_ref = f32[10,138]{1,0:T(8,128)S(1)} collective-permute-done((f32[10,138]{1,0:T(8,128)S(1)}, f32[10,138]{1,0:T(8,128)S(1)}, u32[]{:S(2)}, u32[]{:S(2)}) %collective-permute-start.11) | collective-permute-done | bytes 5552 | tf_op jit(solution)/shard_map/ppermute | solution.py:303
  61.0 0.9 %filter.1 = (f32[64,256]{1,0:T(8,128)S(1)}, f32[64,256]{1,0:T(8,128)S(1)}, f32[64,256]{1,0:T(8,128)S(1)}) custom-call(s32[1]{0:T(128)} %bitcast.place_ref, f32[144,256]{1,0:T(8,128)S(1)} %slice_bitcast_fusion.near_ref, bf16[144,384]{1,0:T(8,128)(2,1)S(1)} %collective-permute-done.9.far_ref, f32[2,138,10]{2,1,0:T(8,128)S(1)} %convert_element_type.31.beside_ref, ...), custom_call_target="tpu_custom_call" | custom-call | tf_op jit(solution)/shard_map/filter/pallas_call | solution.py:272
  62.0 1.2 %collective-permute-done.12 = f32[64,256]{1,0:T(8,128)S(1)} collective-permute-done((f32[64,256]{1,0:T(8,128)S(1)}, f32[64,256]{1,0:T(8,128)S(1)}, u32[]{:S(2)}, u32[]{:S(2)}) %collective-permute-start.12) | collective-permute-done | bytes 65568 | tf_op jit(solution)/shard_map/ppermute | solution.py:303
  63.2 0.6 %divide_bitcast_fusion = f32[1,64,256]{2,1,0:T(8,128)} fusion(f32[64,256]{1,0:T(8,128)S(1)} %get-tuple-element.24, f32[64,256]{1,0:T(8,128)S(1)} %get-tuple-element.22, f32[64,256]{1,0:T(8,128)S(1)} %collective-permute-done.12), kind=kLoop, calls=%fused_computation.19 | loop fusion | flops 32768 | bytes 262144 | tf_op jit(solution)/shard_map/broadcast_in_dim | solution.py:351
  (38 shorter events, 1.2 us)
Async XLA Ops:
  0.0 1.8 %copy-start.3 = (bf16[1,64,256]{2,1,0:T(8,128)(2,1)S(1)}, bf16[1,64,256]{2,1,0:T(8,128)(2,1)}, u32[]{:S(2)}) copy-start(bf16[1,64,256]{2,1,0:T(8,128)(2,1)} %param.7) | copy-start | bytes 98308
  0.0 1.7 %collective-permute-start = (bf16[64,256]{1,0:T(8,128)(2,1)}, bf16[64,256]{1,0:T(8,128)(2,1)S(1)}, u32[]{:S(2)}, u32[]{:S(2)}) collective-permute-start(bf16[64,256]{1,0:T(8,128)(2,1)} %bitcast.24), channel_id=1, source_target_pairs={{0,1},{1,0},{2,3},{3,2},{4,5},{5,4},{6,7},{7,6},{8,9},{9,8},{10,11... | collective-permute-start | bytes 98312 | tf_op jit(solution)/shard_map/ppermute | solution.py:303
  1.8 7.3 %collective-permute-start.1 = (bf16[128,10]{1,0:T(8,128)(2,1)S(1)}, bf16[128,10]{1,0:T(8,128)(2,1)S(1)}, u32[]{:S(2)}, u32[]{:S(2)}) collective-permute-start(bf16[128,10]{1,0:T(8,128)(2,1)S(1)} %pad_maximum_fusion.2), channel_id=1, source_target_pairs={{1,4},{3,6},{4,1},{5,8},{6,3},{7,10},{8,5},{9,12},{10,7},{11,14},{... | collective-permute-start | bytes 7688 | tf_op jit(solution)/shard_map/ppermute | solution.py:303
  9.2 1.2 %collective-permute-start.2 = (bf16[128,10]{1,0:T(8,128)(2,1)S(1)}, bf16[128,10]{1,0:T(8,128)(2,1)S(1)}, u32[]{:S(2)}, u32[]{:S(2)}) collective-permute-start(bf16[128,10]{1,0:T(8,128)(2,1)S(1)} %collective-permute-done.1), channel_id=1, source_target_pairs={{0,1},{1,0},{2,3},{3,2},{4,5},{5,4},{6,7},{7,6},{8,9},{9,8},{10,11... | collective-permute-start | bytes 7688 | tf_op jit(solution)/shard_map/ppermute | solution.py:303
  10.5 16.2 %collective-permute-start.3 = (bf16[64,384]{1,0:T(8,128)(2,1)S(1)}, bf16[64,384]{1,0:T(8,128)(2,1)S(1)}, u32[]{:S(2)}, u32[]{:S(2)}) collective-permute-start(bf16[64,384]{1,0:T(8,128)(2,1)S(1)} %slice_select_fusion.1), channel_id=1, source_target_pairs={{0,2},{1,3},{2,0},{3,1},{4,6},{5,7},{6,4},{7,5},{8,10},{9,11},{10,... | collective-permute-start | bytes 147464 | tf_op jit(solution)/shard_map/ppermute | solution.py:303
  17.6 9.2 %copy-start.2 = (bf16[1,4,256,256]{3,2,1,0:T(8,128)(2,1)S(1)}, bf16[1,4,256,256]{3,2,1,0:T(8,128)(2,1)}, u32[]{:S(2)}) copy-start(bf16[1,4,256,256]{3,2,1,0:T(8,128)(2,1)} %param.8) | copy-start | bytes 1572868
  17.6 6.0 %collective-permute-start.5 = (bf16[16,384]{1,0:T(8,128)(2,1)S(1)}, bf16[16,384]{1,0:T(8,128)(2,1)S(1)}, u32[]{:S(2)}, u32[]{:S(2)}) collective-permute-start(bf16[16,384]{1,0:T(8,128)(2,1)S(1)} %slice_select_fusion.4), channel_id=1, source_target_pairs={{2,32},{3,34},{6,36},{7,38},{10,40},{11,42},{14,44},{15,46},{18,48... | collective-permute-start | bytes 36872 | tf_op jit(solution)/shard_map/ppermute | solution.py:303
  23.6 4.0 %collective-permute-start.6 = (bf16[16,384]{1,0:T(8,128)(2,1)S(1)}, bf16[16,384]{1,0:T(8,128)(2,1)S(1)}, u32[]{:S(2)}, u32[]{:S(2)}) collective-permute-start(bf16[16,384]{1,0:T(8,128)(2,1)S(1)} %collective-permute-done.5.edge_any), channel_id=1, source_target_pairs={{0,1},{1,0},{2,3},{3,2},{4,5},{5,4},{6,7},{7,6},{8,9},{9,8},{10,11... | collective-permute-start | bytes 36872 | tf_op jit(solution)/shard_map/ppermute | solution.py:303
  26.7 1.2 %collective-permute-start.4 = (bf16[64,384]{1,0:T(8,128)(2,1)S(1)}, bf16[64,384]{1,0:T(8,128)(2,1)S(1)}, u32[]{:S(2)}, u32[]{:S(2)}) collective-permute-start(bf16[64,384]{1,0:T(8,128)(2,1)S(1)} %collective-permute-done.3.far_any), channel_id=1, source_target_pairs={{0,1},{1,0},{2,3},{3,2},{4,5},{5,4},{6,7},{7,6},{8,9},{9,8},{10,11... | collective-permute-start | bytes 147464 | tf_op jit(solution)/shard_map/ppermute | solution.py:303
  26.7 1.2 %copy-start = (f32[27,21]{0,1:T(8,128)S(1)}, f32[27,21]{0,1:T(8,128)}, u32[]{:S(2)}) copy-start(f32[27,21]{0,1:T(8,128)} %param.10) | copy-start | bytes 6808
  26.7 1.2 %copy-start.1 = (f32[27,21]{0,1:T(8,128)S(1)}, f32[27,21]{0,1:T(8,128)}, u32[]{:S(2)}) copy-start(f32[27,21]{0,1:T(8,128)} %param.11) | copy-start | bytes 6808
  39.3 1.5 %collective-permute-start.7 = (bf16[2,144,256]{2,1,0:T(8,128)(2,1)S(1)}, bf16[2,144,256]{2,1,0:T(8,128)(2,1)S(1)}, u32[]{:S(2)}, u32[]{:S(2)}) collective-permute-start(bf16[2,144,256]{2,1,0:T(8,128)(2,1)S(1)} %get-tuple-element.19), channel_id=1, source_target_pairs={{0,1},{1,0},{2,3},{3,2},{4,5},{5,4},{6,7},{7,6},{8,9},{9,8},{10,11... | collective-permute-start | bytes 442376 | tf_op jit(solution)/shard_map/ppermute | solution.py:303
  39.5 0.7 %copy-start.4 = (f32[21]{0:T(128)S(1)}, f32[21]{0:T(128)}, u32[]{:S(2)}) copy-start(f32[21]{0:T(128)} %param.12) | copy-start | bytes 256
  40.8 9.5 %collective-permute-start.8 = (bf16[2,138,10]{2,1,0:T(8,128)(2,1)S(1)}, bf16[2,138,10]{2,1,0:T(8,128)(2,1)S(1)}, u32[]{:S(2)}, u32[]{:S(2)}) collective-permute-start(bf16[2,138,10]{2,1,0:T(8,128)(2,1)S(1)} %fusion.4), channel_id=1, source_target_pairs={{1,4},{3,6},{4,1},{5,8},{6,3},{7,10},{8,5},{9,12},{10,7},{11,14},{... | collective-permute-start | bytes 16568 | tf_op jit(solution)/shard_map/ppermute | solution.py:303
  50.4 10.6 %collective-permute-start.9 = (bf16[144,384]{1,0:T(8,128)(2,1)S(1)}, bf16[144,384]{1,0:T(8,128)(2,1)S(1)}, u32[]{:S(2)}, u32[]{:S(2)}) collective-permute-start(bf16[144,384]{1,0:T(8,128)(2,1)S(1)} %fusion.5), channel_id=1, source_target_pairs={{0,2},{1,3},{2,0},{3,1},{4,6},{5,7},{6,4},{7,5},{8,10},{9,11},{10,... | collective-permute-start | bytes 331784 | tf_op jit(solution)/shard_map/ppermute | solution.py:303
  50.5 9.5 %collective-permute-start.10 = (f32[10,138]{1,0:T(8,128)S(1)}, f32[10,138]{1,0:T(8,128)S(1)}, u32[]{:S(2)}, u32[]{:S(2)}) collective-permute-start(f32[10,138]{1,0:T(8,128)S(1)} %get-tuple-element.26), channel_id=1, source_target_pairs={{2,32},{3,33},{6,36},{7,37},{10,40},{11,41},{14,44},{15,45},{18,48... | collective-permute-start | bytes 16568 | tf_op jit(solution)/shard_map/ppermute | solution.py:303
  54.7 6.3 %collective-permute-start.11 = (f32[10,138]{1,0:T(8,128)S(1)}, f32[10,138]{1,0:T(8,128)S(1)}, u32[]{:S(2)}, u32[]{:S(2)}) collective-permute-start(f32[10,138]{1,0:T(8,128)S(1)} %get-tuple-element.25), channel_id=1, source_target_pairs={{0,32},{1,33},{4,36},{5,37},{8,40},{9,41},{12,44},{13,45},{16,48},... | collective-permute-start | bytes 16568 | tf_op jit(solution)/shard_map/ppermute | solution.py:303
  61.9 1.3 %collective-permute-start.12 = (f32[64,256]{1,0:T(8,128)S(1)}, f32[64,256]{1,0:T(8,128)S(1)}, u32[]{:S(2)}, u32[]{:S(2)}) collective-permute-start(f32[64,256]{1,0:T(8,128)S(1)} %get-tuple-element.23), channel_id=1, source_target_pairs={{0,1},{1,0},{2,3},{3,2},{4,5},{5,4},{6,7},{7,6},{8,9},{9,8},{10,11... | collective-permute-start | bytes 196616 | tf_op jit(solution)/shard_map/ppermute | solution.py:303

commit v7 on v6

--- a/solution.py
+++ b/solution.py
@@ -187,7 +187,7 @@
         counts[pl.ds(at, 8), :] = seen
         return carry
 
-    lax.fori_loop(0, PIX // 8, residual, 0, unroll=16)
+    lax.fori_loop(0, PIX // 8, residual, 0, unroll=32)
 
     def block(k):
         side = pl.ds(HALF * (k % 2), HALF)

time: 64.8 us -> 64.7 us (level)
  no operation moved by 1% of the time
where the time goes in v7:
time: 64.7 us; the launch traced here: 63.8 us
  starting transfers between devices  28.7 us (44%)
  waiting for transfers between devices  18.8 us (29%)
  Pallas kernels  12 us (19%)
  other arithmetic  2.54 us (4%)
  local copies, waits for them, and re-layouts  1.54 us (2%)
    ppermute x13, starting transfers between devices, send(): return lax.ppermute(values, ('tile', 'exp'), route)  28.7 us
    ppermute x13, waiting for transfers between devices, send(): return lax.ppermute(values, ('tile', 'exp'), route)  18.8 us
    pallas_call x1, Pallas kernels, fit(): pl.pallas_call(fit_kernel, out_shape=[jax.ShapeDtypeStruct((2, HALF + 16,...  11.2 us
    convert_element_type x1, other arithmetic, shards(): planes = jnp.concatenate([exposures[0], masks[0].astype(BF16)], 0)  1.31 us
  transfers between devices with their start and end apart: 13, of which 10 were waited for; matrix products, arithmetic and copies ran while one was open for 4% of the time, Pallas kernels for 0%

profile of v7, /device:TPU:31, one launch (start us, length us, event | category | flops | bytes accessed | tf_op | source)
XLA Modules:
  0.0 63.8 jit_solution(8656180039043079657)
XLA Ops:
  0.0 0.7 %collective-permute-start = (bf16[64,256]{1,0:T(8,128)(2,1)}, bf16[64,256]{1,0:T(8,128)(2,1)S(1)}, u32[]{:S(2)}, u32[]{:S(2)}) collective-permute-start(bf16[64,256]{1,0:T(8,128)(2,1)} %bitcast.24), channel_id=1, source_target_pairs={{0,1},{1,0},{2,3},{3,2},{4,5},{5,4},{6,7},{7,6},{8,9},{9,8},{10,11... | collective-permute-start | bytes 98312 | tf_op jit(solution)/shard_map/ppermute | solution.py:303
  0.7 0.7 %reverse.3 = f32[21]{0:T(128)S(1)} reverse(f32[21]{0:T(128)} %param.13), dimensions={0} | reverse | bytes 168 | tf_op jit(solution)/shard_map/reverse
  1.4 0.3 collective-permute-done
  1.8 3.4 %collective-permute-start.1 = (bf16[128,10]{1,0:T(8,128)(2,1)S(1)}, bf16[128,10]{1,0:T(8,128)(2,1)S(1)}, u32[]{:S(2)}, u32[]{:S(2)}) collective-permute-start(bf16[128,10]{1,0:T(8,128)(2,1)S(1)} %pad_maximum_fusion.2), channel_id=1, source_target_pairs={{1,4},{3,6},{4,1},{5,8},{6,3},{7,10},{8,5},{9,12},{10,7},{11,14},{... | collective-permute-start | bytes 7688 | tf_op jit(solution)/shard_map/ppermute | solution.py:303
  5.4 3.8 %collective-permute-done.1 = bf16[128,10]{1,0:T(8,128)(2,1)S(1)} collective-permute-done((bf16[128,10]{1,0:T(8,128)(2,1)S(1)}, bf16[128,10]{1,0:T(8,128)(2,1)S(1)}, u32[]{:S(2)}, u32[]{:S(2)}) %collective-permute-start.1) | collective-permute-done | bytes 2592 | tf_op jit(solution)/shard_map/ppermute | solution.py:303
  9.2 1.2 %collective-permute-done.2 = bf16[128,10]{1,0:T(8,128)(2,1)S(1)} collective-permute-done((bf16[128,10]{1,0:T(8,128)(2,1)S(1)}, bf16[128,10]{1,0:T(8,128)(2,1)S(1)}, u32[]{:S(2)}, u32[]{:S(2)}) %collective-permute-start.2) | collective-permute-done | bytes 2592 | tf_op jit(solution)/shard_map/ppermute | solution.py:303
  10.5 7.0 %collective-permute-start.3 = (bf16[64,384]{1,0:T(8,128)(2,1)S(1)}, bf16[64,384]{1,0:T(8,128)(2,1)S(1)}, u32[]{:S(2)}, u32[]{:S(2)}) collective-permute-start(bf16[64,384]{1,0:T(8,128)(2,1)S(1)} %slice_select_fusion.1), channel_id=1, source_target_pairs={{0,2},{1,3},{2,0},{3,1},{4,6},{5,7},{6,4},{7,5},{8,10},{9,11},{10,... | collective-permute-start | bytes 147464 | tf_op jit(solution)/shard_map/ppermute | solution.py:303
  17.6 2.1 %collective-permute-start.5 = (bf16[16,384]{1,0:T(8,128)(2,1)S(1)}, bf16[16,384]{1,0:T(8,128)(2,1)S(1)}, u32[]{:S(2)}, u32[]{:S(2)}) collective-permute-start(bf16[16,384]{1,0:T(8,128)(2,1)S(1)} %slice_select_fusion.4), channel_id=1, source_target_pairs={{2,32},{3,34},{6,36},{7,38},{10,40},{11,42},{14,44},{15,46},{18,48... | collective-permute-start | bytes 36872 | tf_op jit(solution)/shard_map/ppermute | solution.py:303
  19.6 1.3 %convert_bitcast_fusion = bf16[4,256,256]{2,1,0:T(8,128)(2,1)S(1)} fusion(s32[1,4,256,256]{3,2,1,0:T(8,128)} %param.9), kind=kLoop, calls=%fused_computation.1 | loop fusion | flops 262144 | bytes 1572864 | tf_op jit(solution)/shard_map/convert_element_type | solution.py:330
  20.9 2.7 %collective-permute-done.5.edge_any = bf16[16,384]{1,0:T(8,128)(2,1)S(1)} collective-permute-done((bf16[16,384]{1,0:T(8,128)(2,1)S(1)}, bf16[16,384]{1,0:T(8,128)(2,1)S(1)}, u32[]{:S(2)}, u32[]{:S(2)}) %collective-permute-start.5) | collective-permute-done | bytes 12320 | tf_op jit(solution)/shard_map/ppermute | solution.py:303
  23.6 3.1 %collective-permute-start.6 = (bf16[16,384]{1,0:T(8,128)(2,1)S(1)}, bf16[16,384]{1,0:T(8,128)(2,1)S(1)}, u32[]{:S(2)}, u32[]{:S(2)}) collective-permute-start(bf16[16,384]{1,0:T(8,128)(2,1)S(1)} %collective-permute-done.5.edge_any), channel_id=1, source_target_pairs={{0,1},{1,0},{2,3},{3,2},{4,5},{5,4},{6,7},{7,6},{8,9},{9,8},{10,11... | collective-permute-start | bytes 36872 | tf_op jit(solution)/shard_map/ppermute | solution.py:303
  26.9 0.7 %collective-permute-done.6.edge_core_any = bf16[16,384]{1,0:T(8,128)(2,1)S(1)} collective-permute-done((bf16[16,384]{1,0:T(8,128)(2,1)S(1)}, bf16[16,384]{1,0:T(8,128)(2,1)S(1)}, u32[]{:S(2)}, u32[]{:S(2)}) %collective-permute-start.6) | collective-permute-done | bytes 12320 | tf_op jit(solution)/shard_map/ppermute | solution.py:303
  27.6 0.4 collective-permute-done.4.far_core_any
  28.0 11.2 %fit.1 = (bf16[2,144,256]{2,1,0:T(8,128)(2,1)S(1)}, bf16[2,144,256]{2,1,0:T(8,128)(2,1)S(1)}) custom-call(s32[1]{0:T(128)} %bitcast.place_ref, bf16[128,384]{1,0:T(8,128)(2,1)S(1)} %fusion.7.own_any, bf16[64,384]{1,0:T(8,128)(2,1)S(1)} %collective-permute-done.3.far_any, bf16[64,384]{1,0:T(8,128)(2,1)S(1)} %collective-permute-done.4.far_core_any, ...), custom_call_target="tpu_custom_call" | custom-call | tf_op jit(solution)/shard_map/fit/pallas_call | solution.py:215
  39.4 0.7 %copy-done.4 = f32[21]{0:T(128)S(1)} copy-done((f32[21]{0:T(128)S(1)}, f32[21]{0:T(128)}, u32[]{:S(2)}) %copy-start.4) | copy-done | bytes 108
  40.1 0.5 collective-permute-done.7
  40.7 2.5 %collective-permute-start.8 = (bf16[2,138,10]{2,1,0:T(8,128)(2,1)S(1)}, bf16[2,138,10]{2,1,0:T(8,128)(2,1)S(1)}, u32[]{:S(2)}, u32[]{:S(2)}) collective-permute-start(bf16[2,138,10]{2,1,0:T(8,128)(2,1)S(1)} %fusion.4), channel_id=1, source_target_pairs={{1,4},{3,6},{4,1},{5,8},{6,3},{7,10},{8,5},{9,12},{10,7},{11,14},{... | collective-permute-start | bytes 16568 | tf_op jit(solution)/shard_map/ppermute | solution.py:303
  43.3 6.9 %collective-permute-done.8 = bf16[2,138,10]{2,1,0:T(8,128)(2,1)S(1)} collective-permute-done((bf16[2,138,10]{2,1,0:T(8,128)(2,1)S(1)}, bf16[2,138,10]{2,1,0:T(8,128)(2,1)S(1)}, u32[]{:S(2)}, u32[]{:S(2)}) %collective-permute-start.8) | collective-permute-done | bytes 5552 | tf_op jit(solution)/shard_map/ppermute | solution.py:303
  50.4 4.2 %collective-permute-start.10 = (f32[10,138]{1,0:T(8,128)S(1)}, f32[10,138]{1,0:T(8,128)S(1)}, u32[]{:S(2)}, u32[]{:S(2)}) collective-permute-start(f32[10,138]{1,0:T(8,128)S(1)} %get-tuple-element.26), channel_id=1, source_target_pairs={{2,32},{3,33},{6,36},{7,37},{10,40},{11,41},{14,44},{15,45},{18,48... | collective-permute-start | bytes 16568 | tf_op jit(solution)/shard_map/ppermute | solution.py:303
  54.6 5.2 %collective-permute-start.11 = (f32[10,138]{1,0:T(8,128)S(1)}, f32[10,138]{1,0:T(8,128)S(1)}, u32[]{:S(2)}, u32[]{:S(2)}) collective-permute-start(f32[10,138]{1,0:T(8,128)S(1)} %get-tuple-element.25), channel_id=1, source_target_pairs={{0,32},{1,33},{4,36},{5,37},{8,40},{9,41},{12,44},{13,45},{16,48},... | collective-permute-start | bytes 16568 | tf_op jit(solution)/shard_map/ppermute | solution.py:303
  59.9 1.0 %collective-permute-done.11.edge_too_ref = f32[10,138]{1,0:T(8,128)S(1)} collective-permute-done((f32[10,138]{1,0:T(8,128)S(1)}, f32[10,138]{1,0:T(8,128)S(1)}, u32[]{:S(2)}, u32[]{:S(2)}) %collective-permute-start.11) | collective-permute-done | bytes 5552 | tf_op jit(solution)/shard_map/ppermute | solution.py:303
  60.9 0.9 %filter.1 = (f32[64,256]{1,0:T(8,128)S(1)}, f32[64,256]{1,0:T(8,128)S(1)}, f32[64,256]{1,0:T(8,128)S(1)}) custom-call(s32[1]{0:T(128)} %bitcast.place_ref, f32[144,256]{1,0:T(8,128)S(1)} %slice_bitcast_fusion.near_ref, bf16[144,384]{1,0:T(8,128)(2,1)S(1)} %collective-permute-done.9.far_ref, f32[2,138,10]{2,1,0:T(8,128)S(1)} %convert_element_type.31.beside_ref, ...), custom_call_target="tpu_custom_call" | custom-call | tf_op jit(solution)/shard_map/filter/pallas_call | solution.py:272
  61.9 1.2 %collective-permute-done.12 = f32[64,256]{1,0:T(8,128)S(1)} collective-permute-done((f32[64,256]{1,0:T(8,128)S(1)}, f32[64,256]{1,0:T(8,128)S(1)}, u32[]{:S(2)}, u32[]{:S(2)}) %collective-permute-start.12) | collective-permute-done | bytes 65568 | tf_op jit(solution)/shard_map/ppermute | solution.py:303
  63.1 0.6 %divide_bitcast_fusion = f32[1,64,256]{2,1,0:T(8,128)} fusion(f32[64,256]{1,0:T(8,128)S(1)} %get-tuple-element.24, f32[64,256]{1,0:T(8,128)S(1)} %get-tuple-element.22, f32[64,256]{1,0:T(8,128)S(1)} %collective-permute-done.12), kind=kLoop, calls=%fused_computation.19 | loop fusion | flops 32768 | bytes 262144 | tf_op jit(solution)/shard_map/broadcast_in_dim | solution.py:351
  (38 shorter events, 1.2 us)
Async XLA Ops:
  0.0 1.8 %copy-start.3 = (bf16[1,64,256]{2,1,0:T(8,128)(2,1)S(1)}, bf16[1,64,256]{2,1,0:T(8,128)(2,1)}, u32[]{:S(2)}) copy-start(bf16[1,64,256]{2,1,0:T(8,128)(2,1)} %param.7) | copy-start | bytes 98308
  0.0 1.7 %collective-permute-start = (bf16[64,256]{1,0:T(8,128)(2,1)}, bf16[64,256]{1,0:T(8,128)(2,1)S(1)}, u32[]{:S(2)}, u32[]{:S(2)}) collective-permute-start(bf16[64,256]{1,0:T(8,128)(2,1)} %bitcast.24), channel_id=1, source_target_pairs={{0,1},{1,0},{2,3},{3,2},{4,5},{5,4},{6,7},{7,6},{8,9},{9,8},{10,11... | collective-permute-start | bytes 98312 | tf_op jit(solution)/shard_map/ppermute | solution.py:303
  1.8 7.3 %collective-permute-start.1 = (bf16[128,10]{1,0:T(8,128)(2,1)S(1)}, bf16[128,10]{1,0:T(8,128)(2,1)S(1)}, u32[]{:S(2)}, u32[]{:S(2)}) collective-permute-start(bf16[128,10]{1,0:T(8,128)(2,1)S(1)} %pad_maximum_fusion.2), channel_id=1, source_target_pairs={{1,4},{3,6},{4,1},{5,8},{6,3},{7,10},{8,5},{9,12},{10,7},{11,14},{... | collective-permute-start | bytes 7688 | tf_op jit(solution)/shard_map/ppermute | solution.py:303
  9.2 1.2 %collective-permute-start.2 = (bf16[128,10]{1,0:T(8,128)(2,1)S(1)}, bf16[128,10]{1,0:T(8,128)(2,1)S(1)}, u32[]{:S(2)}, u32[]{:S(2)}) collective-permute-start(bf16[128,10]{1,0:T(8,128)(2,1)S(1)} %collective-permute-done.1), channel_id=1, source_target_pairs={{0,1},{1,0},{2,3},{3,2},{4,5},{5,4},{6,7},{7,6},{8,9},{9,8},{10,11... | collective-permute-start | bytes 7688 | tf_op jit(solution)/shard_map/ppermute | solution.py:303
  10.5 16.2 %collective-permute-start.3 = (bf16[64,384]{1,0:T(8,128)(2,1)S(1)}, bf16[64,384]{1,0:T(8,128)(2,1)S(1)}, u32[]{:S(2)}, u32[]{:S(2)}) collective-permute-start(bf16[64,384]{1,0:T(8,128)(2,1)S(1)} %slice_select_fusion.1), channel_id=1, source_target_pairs={{0,2},{1,3},{2,0},{3,1},{4,6},{5,7},{6,4},{7,5},{8,10},{9,11},{10,... | collective-permute-start | bytes 147464 | tf_op jit(solution)/shard_map/ppermute | solution.py:303
  17.6 9.2 %copy-start.2 = (bf16[1,4,256,256]{3,2,1,0:T(8,128)(2,1)S(1)}, bf16[1,4,256,256]{3,2,1,0:T(8,128)(2,1)}, u32[]{:S(2)}) copy-start(bf16[1,4,256,256]{3,2,1,0:T(8,128)(2,1)} %param.8) | copy-start | bytes 1572868
  17.6 6.0 %collective-permute-start.5 = (bf16[16,384]{1,0:T(8,128)(2,1)S(1)}, bf16[16,384]{1,0:T(8,128)(2,1)S(1)}, u32[]{:S(2)}, u32[]{:S(2)}) collective-permute-start(bf16[16,384]{1,0:T(8,128)(2,1)S(1)} %slice_select_fusion.4), channel_id=1, source_target_pairs={{2,32},{3,34},{6,36},{7,38},{10,40},{11,42},{14,44},{15,46},{18,48... | collective-permute-start | bytes 36872 | tf_op jit(solution)/shard_map/ppermute | solution.py:303
  23.6 4.0 %collective-permute-start.6 = (bf16[16,384]{1,0:T(8,128)(2,1)S(1)}, bf16[16,384]{1,0:T(8,128)(2,1)S(1)}, u32[]{:S(2)}, u32[]{:S(2)}) collective-permute-start(bf16[16,384]{1,0:T(8,128)(2,1)S(1)} %collective-permute-done.5.edge_any), channel_id=1, source_target_pairs={{0,1},{1,0},{2,3},{3,2},{4,5},{5,4},{6,7},{7,6},{8,9},{9,8},{10,11... | collective-permute-start | bytes 36872 | tf_op jit(solution)/shard_map/ppermute | solution.py:303
  26.7 1.2 %collective-permute-start.4 = (bf16[64,384]{1,0:T(8,128)(2,1)S(1)}, bf16[64,384]{1,0:T(8,128)(2,1)S(1)}, u32[]{:S(2)}, u32[]{:S(2)}) collective-permute-start(bf16[64,384]{1,0:T(8,128)(2,1)S(1)} %collective-permute-done.3.far_any), channel_id=1, source_target_pairs={{0,1},{1,0},{2,3},{3,2},{4,5},{5,4},{6,7},{7,6},{8,9},{9,8},{10,11... | collective-permute-start | bytes 147464 | tf_op jit(solution)/shard_map/ppermute | solution.py:303
  26.7 1.2 %copy-start = (f32[27,21]{0,1:T(8,128)S(1)}, f32[27,21]{0,1:T(8,128)}, u32[]{:S(2)}) copy-start(f32[27,21]{0,1:T(8,128)} %param.10) | copy-start | bytes 6808
  26.7 1.2 %copy-start.1 = (f32[27,21]{0,1:T(8,128)S(1)}, f32[27,21]{0,1:T(8,128)}, u32[]{:S(2)}) copy-start(f32[27,21]{0,1:T(8,128)} %param.11) | copy-start | bytes 6808
  39.1 1.5 %collective-permute-start.7 = (bf16[2,144,256]{2,1,0:T(8,128)(2,1)S(1)}, bf16[2,144,256]{2,1,0:T(8,128)(2,1)S(1)}, u32[]{:S(2)}, u32[]{:S(2)}) collective-permute-start(bf16[2,144,256]{2,1,0:T(8,128)(2,1)S(1)} %get-tuple-element.19), channel_id=1, source_target_pairs={{0,1},{1,0},{2,3},{3,2},{4,5},{5,4},{6,7},{7,6},{8,9},{9,8},{10,11... | collective-permute-start | bytes 442376 | tf_op jit(solution)/shard_map/ppermute | solution.py:303
  39.4 0.7 %copy-start.4 = (f32[21]{0:T(128)S(1)}, f32[21]{0:T(128)}, u32[]{:S(2)}) copy-start(f32[21]{0:T(128)} %param.12) | copy-start | bytes 256
  40.7 9.5 %collective-permute-start.8 = (bf16[2,138,10]{2,1,0:T(8,128)(2,1)S(1)}, bf16[2,138,10]{2,1,0:T(8,128)(2,1)S(1)}, u32[]{:S(2)}, u32[]{:S(2)}) collective-permute-start(bf16[2,138,10]{2,1,0:T(8,128)(2,1)S(1)} %fusion.4), channel_id=1, source_target_pairs={{1,4},{3,6},{4,1},{5,8},{6,3},{7,10},{8,5},{9,12},{10,7},{11,14},{... | collective-permute-start | bytes 16568 | tf_op jit(solution)/shard_map/ppermute | solution.py:303
  50.3 10.6 %collective-permute-start.9 = (bf16[144,384]{1,0:T(8,128)(2,1)S(1)}, bf16[144,384]{1,0:T(8,128)(2,1)S(1)}, u32[]{:S(2)}, u32[]{:S(2)}) collective-permute-start(bf16[144,384]{1,0:T(8,128)(2,1)S(1)} %fusion.5), channel_id=1, source_target_pairs={{0,2},{1,3},{2,0},{3,1},{4,6},{5,7},{6,4},{7,5},{8,10},{9,11},{10,... | collective-permute-start | bytes 331784 | tf_op jit(solution)/shard_map/ppermute | solution.py:303
  50.4 9.5 %collective-permute-start.10 = (f32[10,138]{1,0:T(8,128)S(1)}, f32[10,138]{1,0:T(8,128)S(1)}, u32[]{:S(2)}, u32[]{:S(2)}) collective-permute-start(f32[10,138]{1,0:T(8,128)S(1)} %get-tuple-element.26), channel_id=1, source_target_pairs={{2,32},{3,33},{6,36},{7,37},{10,40},{11,41},{14,44},{15,45},{18,48... | collective-permute-start | bytes 16568 | tf_op jit(solution)/shard_map/ppermute | solution.py:303
  54.6 6.3 %collective-permute-start.11 = (f32[10,138]{1,0:T(8,128)S(1)}, f32[10,138]{1,0:T(8,128)S(1)}, u32[]{:S(2)}, u32[]{:S(2)}) collective-permute-start(f32[10,138]{1,0:T(8,128)S(1)} %get-tuple-element.25), channel_id=1, source_target_pairs={{0,32},{1,33},{4,36},{5,37},{8,40},{9,41},{12,44},{13,45},{16,48},... | collective-permute-start | bytes 16568 | tf_op jit(solution)/shard_map/ppermute | solution.py:303
  61.8 1.3 %collective-permute-start.12 = (f32[64,256]{1,0:T(8,128)S(1)}, f32[64,256]{1,0:T(8,128)S(1)}, u32[]{:S(2)}, u32[]{:S(2)}) collective-permute-start(f32[64,256]{1,0:T(8,128)S(1)} %get-tuple-element.23), channel_id=1, source_target_pairs={{0,1},{1,0},{2,3},{3,2},{4,5},{5,4},{6,7},{7,6},{8,9},{9,8},{10,11... | collective-permute-start | bytes 196616 | tf_op jit(solution)/shard_map/ppermute | solution.py:303
